TPU v7x, 128 devices: a whole 4x4x4 slice. The times are simulated.
128 devices in a mesh: row: 8 (over x, y_lo), col: 16 (over y_hi, z, core).
Axes of the slice: x: 4, y: 4 (y_hi: 2, y_lo: 2; y = y_hi * 2 + y_lo), z: 4, core: 2. Of those that a mesh axis runs over, the one named last changes fastest.
Arguments:
- latent: bfloat16 [256, 512, 512], P('row', 'col'), may hold values from -12 to 12
- conv_scale: float32 [512], replicated, may hold values from 0.5 to 1.5
- conv_shift: float32 [512], replicated, may hold values from -3 to 3
- expand_weight: bfloat16 [512, 2048], replicated, may hold values from -0.25 to 0.25
- depth_kernel: float32 [9, 2048], replicated, may hold values from -2 to 2
- squeeze_down: bfloat16 [2048, 128], replicated, may hold values from -0.5 to 0.5
- squeeze_up: bfloat16 [128, 2048], replicated, may hold values from -0.5 to 0.5
- project_weight: bfloat16 [2048, 512], replicated, may hold values from -0.125 to 0.125
- block_gain: float32 [512], replicated, may hold values from 0.5 to 1.5
- block_projection: bfloat16 [512, 1536], replicated, may hold values from -0.25 to 0.25
- block_output: bfloat16 [512, 512], replicated, may hold values from -0.25 to 0.25
- block_table: float32 [16, 225], replicated, may hold values from -4 to 300
- first_gain: float32 [512], replicated, may hold values from 0.5 to 1.5
- first_expand: bfloat16 [512, 2048], replicated, may hold values from -0.25 to 0.25
- first_reduce: bfloat16 [2048, 512], replicated, may hold values from -0.125 to 0.125
- grid_gain: float32 [512], replicated, may hold values from 0.5 to 1.5
- grid_projection: bfloat16 [512, 1536], replicated, may hold values from -0.25 to 0.25
- grid_output: bfloat16 [512, 512], replicated, may hold values from -0.25 to 0.25
- grid_table: float32 [16, 225], replicated, may hold values from -4 to 300
- second_gain: float32 [512], replicated, may hold values from 0.5 to 1.5
- second_expand: bfloat16 [512, 2048], replicated, may hold values from -0.25 to 0.25
- second_reduce: bfloat16 [2048, 512], replicated, may hold values from -0.125 to 0.125
Outputs:
- nowcast_latent: bfloat16 [256, 512, 512], P('row', 'col')
All inputs are finite; a program needn't handle non-finite values.
Results may differ from a plain program's by a relative error of at most 0.012.
Values may be sent and summed in bfloat16 or wider, within the bound.
No kernel may reach another device: no remote copies, remote signals or barrier semaphores. Data moves between devices by JAX's collectives and lax.ppermute only.
A program may use at most 128 MiB of HBM per device.

v0:
```python
import jax
import jax.numpy as jnp
from jax import lax
from jax.sharding import PartitionSpec as P

WIN = 8


def extended(cells, sides, width):
    for axis, dim in sides:
        count = lax.axis_size(axis)
        ends = count - 1
        head = lax.slice_in_dim(cells, 0, width, axis=dim)
        tail = lax.slice_in_dim(cells, cells.shape[dim] - width, cells.shape[dim], axis=dim)
        cells = jnp.concatenate(
            [
                lax.ppermute(tail, axis, [(i, (i + 1) % count) for i in range(ends)]),
                cells,
                lax.ppermute(head, axis, [((i + 1) % count, i) for i in range(ends)]),
            ],
            axis=dim,
        )
    return cells


def layer_norm_apply(values, norm_gain):
    widened = values.astype(jnp.float32)
    center = widened - jnp.mean(widened, axis=-1, keepdims=True)
    spread = jnp.mean(center * center, axis=-1, keepdims=True)
    return (center * lax.rsqrt(spread + 1e-05) * norm_gain).astype(jnp.bfloat16)


def position_bias(offset_bias_lookup):
    spots = offset_bias_lookup.shape[1]
    position = jnp.arange(WIN * WIN)
    down_pos = position // WIN
    across = position % WIN
    relative = (down_pos[:, None] - down_pos[None, :] + WIN - 1) * (2 * WIN - 1) + (
        across[:, None] - across[None, :] + WIN - 1
    )
    indicator_matrix = (relative[:, :, None] == jnp.arange(spots)[None, None, :]).astype(
        jnp.float32
    )
    return jnp.einsum(
        "bp,rjp->brj", offset_bias_lookup, indicator_matrix, precision=lax.Precision.HIGHEST
    )


def attend(triple, pos_bias):
    window_count, tokens, three_width = triple.shape
    feature_width = three_width // 3
    head_count = pos_bias.shape[0]
    head_size = feature_width // head_count
    queries = triple[..., :feature_width].reshape(window_count, tokens, head_count, head_size)
    key_row_list = triple[..., feature_width : 2 * feature_width].reshape(
        window_count, tokens, head_count, head_size
    )
    values = triple[..., 2 * feature_width :].reshape(window_count, tokens, head_count, head_size)
    scores = (
        jnp.einsum("nqhd,nkhd->nhqk", queries, key_row_list, preferred_element_type=jnp.float32)
        * head_size ** (-0.5)
        + pos_bias[None]
    )
    row_max = jnp.max(scores, axis=-1, keepdims=True)
    weight_tensors = jnp.exp(scores - row_max)
    attention_weight_map = (
        weight_tensors / jnp.sum(weight_tensors, axis=-1, keepdims=True)
    ).astype(jnp.bfloat16)
    mixed = jnp.einsum(
        "nhqk,nkhd->nqhd", attention_weight_map, values, preferred_element_type=jnp.float32
    )
    return mixed.astype(jnp.bfloat16).reshape(window_count, tokens, feature_width)


def attention_sublayer(windows, norm_gain, in_weight, out_weight, pos_bias):
    normed = layer_norm_apply(windows, norm_gain)
    triple = jnp.dot(normed, in_weight, preferred_element_type=jnp.float32).astype(jnp.bfloat16)
    mixed = attend(triple, pos_bias)
    return (
        windows.astype(jnp.float32) + jnp.dot(mixed, out_weight, preferred_element_type=jnp.float32)
    ).astype(jnp.bfloat16)


def feed_forward(values, norm_gain, in_weight, out_weight):
    normed = layer_norm_apply(values, norm_gain)
    hidden = jax.nn.gelu(
        jnp.dot(normed, in_weight, preferred_element_type=jnp.float32), approximate=True
    ).astype(jnp.bfloat16)
    return (
        values.astype(jnp.float32) + jnp.dot(hidden, out_weight, preferred_element_type=jnp.float32)
    ).astype(jnp.bfloat16)


def to_blocks(field):
    row_count, col_count, feats = field.shape
    return (
        field.reshape(row_count // WIN, WIN, col_count // WIN, WIN, feats)
        .transpose(0, 2, 1, 3, 4)
        .reshape(-1, WIN * WIN, feats)
    )


def from_blocks(windows, row_count, col_count):
    feats = windows.shape[-1]
    return (
        windows.reshape(row_count // WIN, col_count // WIN, WIN, WIN, feats)
        .transpose(0, 2, 1, 3, 4)
        .reshape(row_count, col_count, feats)
    )


def axis_shape(length, devices):
    fold = max(1, WIN // devices)
    rest = length // max(devices, WIN)
    span = min(devices, WIN)
    return (fold, rest, span, devices // span)


def grid_layout(field):
    row_devices = lax.axis_size("row")
    col_devices = lax.axis_size("col")
    row_count, col_count, feats = field.shape
    row_fold, row_rest, row_span, row_hop = axis_shape(row_count, row_devices)
    col_fold, col_rest, col_span, col_hop = axis_shape(col_count, col_devices)
    ordered_layout = field.reshape(
        row_fold, row_devices, row_rest, col_fold, col_devices, col_rest, feats
    )
    flat = ordered_layout.transpose(1, 4, 0, 2, 3, 5, 6).reshape(
        row_devices * col_devices, row_fold, row_rest, col_fold, col_rest, feats
    )
    flat = lax.all_to_all(flat, ("row", "col"), split_axis=0, concat_axis=0, tiled=True)
    moved = flat.reshape(
        row_devices, col_devices, row_fold, row_rest, col_fold, col_rest, feats
    ).transpose(2, 0, 3, 4, 1, 5, 6)
    moved = moved.reshape(
        row_fold, row_span, row_hop, row_rest, col_fold, col_span, col_hop, col_rest, feats
    )
    return moved.transpose(2, 3, 6, 7, 1, 0, 5, 4, 8).reshape(-1, WIN * WIN, feats)


def spatial_layout(windows, row_count, col_count):
    row_devices = lax.axis_size("row")
    col_devices = lax.axis_size("col")
    feats = windows.shape[-1]
    row_fold, row_rest, row_span, row_hop = axis_shape(row_count, row_devices)
    col_fold, col_rest, col_span, col_hop = axis_shape(col_count, col_devices)
    gridded = windows.reshape(
        row_hop, row_rest, col_hop, col_rest, row_span, row_fold, col_span, col_fold, feats
    )
    ordered_layout = gridded.transpose(5, 4, 0, 1, 7, 6, 2, 3, 8).reshape(
        row_fold, row_devices, row_rest, col_fold, col_devices, col_rest, feats
    )
    flat = ordered_layout.transpose(1, 4, 0, 2, 3, 5, 6).reshape(
        row_devices * col_devices, row_fold, row_rest, col_fold, col_rest, feats
    )
    flat = lax.all_to_all(flat, ("row", "col"), split_axis=0, concat_axis=0, tiled=True)
    moved = flat.reshape(
        row_devices, col_devices, row_fold, row_rest, col_fold, col_rest, feats
    ).transpose(2, 0, 3, 4, 1, 5, 6)
    return moved.reshape(row_count, col_count, feats)


def squeeze_gate(pooled, squeeze_down, squeeze_up):
    reduced = jax.nn.silu(
        jnp.dot(pooled[None, :], squeeze_down.astype(jnp.float32), precision=lax.Precision.HIGHEST)
    )
    return jax.nn.sigmoid(
        jnp.dot(reduced, squeeze_up.astype(jnp.float32), precision=lax.Precision.HIGHEST)
    )[0]


def per_device(
    latent,
    conv_scale,
    conv_shift,
    expand_weight,
    depth_kernel,
    squeeze_down,
    squeeze_up,
    project_weight,
    block_gain,
    block_projection,
    block_output,
    block_table,
    first_gain,
    first_expand,
    first_reduce,
    grid_gain,
    grid_projection,
    grid_output,
    grid_table,
    second_gain,
    second_expand,
    second_reduce,
):
    row_devices = lax.axis_size("row")
    col_devices = lax.axis_size("col")
    row_count, col_count, channels = latent.shape
    conv_in = (latent.astype(jnp.float32) * conv_scale + conv_shift).astype(jnp.bfloat16)
    expanded = jax.nn.gelu(
        jnp.dot(conv_in, expand_weight, preferred_element_type=jnp.float32), approximate=True
    ).astype(jnp.bfloat16)
    padded = extended(expanded, (("row", 0), ("col", 1)), 1)
    summed = jnp.zeros((row_count, col_count, padded.shape[-1]), jnp.float32)
    for offset in range(9):
        down_step = offset // 3
        side_step = offset % 3
        summed = (
            summed
            + padded[down_step : down_step + row_count, side_step : side_step + col_count].astype(
                jnp.float32
            )
            * depth_kernel[offset]
        )
    depthwise = jax.nn.gelu(summed, approximate=True)
    channel_sums = lax.psum(jnp.sum(depthwise, axis=(0, 1)), ("row", "col"))
    pooled = channel_sums / (row_count * row_devices * col_count * col_devices)
    excite = squeeze_gate(pooled, squeeze_down, squeeze_up)
    gated = (depthwise * excite).astype(jnp.bfloat16)
    conv_out = (
        latent.astype(jnp.float32)
        + jnp.dot(gated, project_weight, preferred_element_type=jnp.float32)
    ).astype(jnp.bfloat16)
    windows = attention_sublayer(
        to_blocks(conv_out), block_gain, block_projection, block_output, position_bias(block_table)
    )
    windows = feed_forward(windows, first_gain, first_expand, first_reduce)
    section = from_blocks(windows, row_count, col_count)
    grid_bias = position_bias(grid_table)
    normed = layer_norm_apply(section, grid_gain)
    triple = jnp.dot(normed, grid_projection, preferred_element_type=jnp.float32).astype(
        jnp.bfloat16
    )
    mixed = attend(grid_layout(triple), grid_bias)
    mixed = spatial_layout(mixed, row_count, col_count)
    section = (
        section.astype(jnp.float32)
        + jnp.dot(mixed, grid_output, preferred_element_type=jnp.float32)
    ).astype(jnp.bfloat16)
    return feed_forward(section, second_gain, second_expand, second_reduce)


def solution(mesh):
    placed = (
        P("row", "col", None),
        P(),
        P(),
        P(),
        P(),
        P(),
        P(),
        P(),
        P(),
        P(),
        P(),
        P(),
        P(),
        P(),
        P(),
        P(),
        P(),
        P(),
        P(),
        P(),
        P(),
        P(),
    )
    return jax.shard_map(
        per_device, mesh=mesh, in_specs=placed, out_specs=P("row", "col", None), check_vma=False
    )
```

profile of v0, /device:TPU:1, one launch (start us, length us, event | category | flops | bytes accessed | tf_op | source)
XLA Modules:
  0.0 321.3 jit_solution(7310170428775599099)
XLA Ops:
  1.6 5.2 %fusion.9 = bf16[32,32,2048]{2,1,0:T(8,128)(2,1)S(1)} fusion(bf16[512,2048]{1,0:T(8,128)(2,1)S(1)} %copy-done, bf16[32,32,512]{2,1,0:T(8,128)(2,1)} %param.22, f32[512]{0:T(512)} %param.24, f32[512]{0:T(512)} %param.23), kind=kOutput, calls=%fused_computation.13 | convolution fusion | flops 2168455168 | bytes 7344128 | tf_op jit(solution)/shard_map/dot_general | solution.py:201
  6.8 4.0 %collective-permute-start = (bf16[1,32,2048]{2,1,0:T(8,128)(2,1)S(1)}, bf16[1,32,2048]{2,1,0:T(8,128)(2,1)S(1)}, u32[]{:S(2)}, u32[]{:S(2)}) collective-permute-start(bf16[1,32,2048]{2,1,0:T(8,128)(2,1)S(1)} %get-tuple-element.11), channel_id=1, source_target_pairs={{0,16},{16,32},{32,48},{48,64},{64,80},{80,96},{96,112},{1,17},{17... | collective-permute-start | bytes 393224 | tf_op jit(solution)/shard_map/ppermute | solution.py:17
  13.0 3.6 %collective-permute-done.1 = bf16[1,32,2048]{2,1,0:T(8,128)(2,1)S(1)} collective-permute-done((bf16[1,32,2048]{2,1,0:T(8,128)(2,1)S(1)}, bf16[1,32,2048]{2,1,0:T(8,128)(2,1)S(1)}, u32[]{:S(2)}, u32[]{:S(2)}) %collective-permute-start.1) | collective-permute-done | bytes 131104 | tf_op jit(solution)/shard_map/ppermute | solution.py:19
  17.1 5.5 %collective-permute-start.2 = (bf16[34,1,2048]{2,1,0:T(2,128)(2,1)S(1)}, bf16[34,1,2048]{2,1,0:T(2,128)(2,1)S(1)}, u32[]{:S(2)}, u32[]{:S(2)}) collective-permute-start(bf16[34,1,2048]{2,1,0:T(2,128)(2,1)S(1)} %get-tuple-element.9), channel_id=1, source_target_pairs={{0,1},{1,2},{2,3},{3,4},{4,5},{5,6},{6,7},{7,8},{8,9},{9,10},{10,1... | collective-permute-start | bytes 417800 | tf_op jit(solution)/shard_map/ppermute | solution.py:17
  24.6 3.2 %fusion.95 = f32[16,64,64]{2,0,1:T(8,128)S(1)} fusion(s32[64,64]{1,0:T(8,128)S(1)} %add_add_fusion, f32[16,225]{1,0:T(8,128)S(1)} %copy-done.9), kind=kOutput, calls=%fused_computation.110 | convolution fusion | flops 177868800 | bytes 292928 | tf_op jit(solution)/shard_map/bp,rjp->brj/dot_general | solution.py:44
  30.5 6.1 %maximum_maximum_fusion = (bf16[34,33,2048]{2,1,0:T(8,128)(2,1)S(1)}, bf16[34,33,2048]{2,1,0:T(8,128)(2,1)S(1)}) fusion(bf16[1,32,2048]{2,1,0:T(8,128)(2,1)S(1)} %collective-permute-done.1, bf16[32,32,2048]{2,1,0:T(8,128)(2,1)} %copy-done.2, bf16[1,32,2048]{2,1,0:T(8,128)(2,1)S(1)} %collective-permute-done, ...), kind=kLoop, calls=%fused_computation.46 | loop fusion | flops 36765696 | bytes 13926400 | tf_op jit(solution)/shard_map/concatenate | solution.py:15
  36.7 14.6 %fusion.150 = (f32[2048]{0:T(1024)S(1)}, f32[32,32,2048]{2,1,0:T(8,128)}) fusion(f32[2048]{0:T(1024)S(1)} %bitcast.174, bf16[34,33,2048]{2,1,0:T(8,128)(2,1)S(1)} %get-tuple-element.8, f32[2048]{0:T(1024)S(1)} %bitcast.175, bf16[1,32,2048]{2,1,0:T(8,128)(2,1)S(1)} %collective-permute-done.1, bf16[32,32,2048]{2,1,0:T(8,128)(2,1)S(1)} %copy-done.3, ...), kind=kLoop, calls=%fused_computation.173 | loop fusion | flops 77592576 | bytes 38092800 | tf_op jit(solution)/shard_map/reduce_sum | solution.py:216
  51.3 70.0 %psum.7 = f32[2048]{0:T(1024)S(1)} all-reduce(f32[2048]{0:T(1024)S(1)} %get-tuple-element.5), channel_id=1, replica_groups=mesh['row'=8,'col'=16] {'row','col'}, use_global_device_ids=true, to_apply=%region_1.0 | all-reduce | flops 2048 | bytes 16384 | tf_op jit(solution)/shard_map/psum | solution.py:216
  121.9 6.3 %fusion.61 = bf16[32,32,512]{2,1,0:T(8,128)(2,1)S(1)} fusion(bf16[32,32,512]{2,1,0:T(8,128)(2,1)S(1)} %copy-done.8, bf16[2048,512]{1,0:T(8,128)(2,1)} %param.29, f32[32,32,2048]{2,1,0:T(8,128)} %get-tuple-element.6, f32[2048]{0:T(1024)S(1)} %add_divide_fusion), kind=kOutput, calls=%fused_computation.85 | convolution fusion | flops 2153250816 | bytes 12591104 | tf_op jit(solution)/shard_map/dot_general | solution.py:222
  132.7 3.3 %convolution_convert_fusion.1 = bf16[16,64,1536]{2,1,0:T(8,128)(2,1)S(1)} fusion(bf16[512,1536]{1,0:T(8,128)(2,1)} %param.31, f32[16,64,512]{2,1,0:T(8,128)S(1)} %bitcast.154, f32[512]{0:T(512)S(1)} %copy-done.11, f32[16,64]{1,0:T(8,128)S(1)} %rsqrt.39, f32[16,64]{1,0:T(8,128)S(1)} %div.76), kind=kOutput, calls=%fused_computation.64 | convolution fusion | flops 1614282752 | bytes 6825984 | tf_op jit(solution)/shard_map/dot_general | solution.py:77
  137.7 2.8 copy.147
  140.4 2.7 copy.148
  145.1 8.9 %fusion.156 = (f32[16,16,64]{2,1,0:T(8,128)S(1)}, f32[16,16,64,64]{2,3,1,0:T(8,128)}) fusion(f32[16,64,64]{1,2,0:T(8,128)} %copy.149, bf16[16,64,16,32]{1,3,2,0:T(8,128)(2,1)} %bitcast.160, bf16[16,64,16,32]{1,3,2,0:T(8,128)(2,1)} %bitcast.162), kind=kOutput, calls=%fused_computation.178 | convolution fusion | flops 71303232 | bytes 6619136 | tf_op jit(solution)/shard_map/sub | solution.py:65
  154.1 5.3 %fusion.78 = bf16[16,16,32,64]{3,2,1,0:T(8,128)(2,1)S(1)} fusion(bf16[16,64,16,32]{1,3,2,0:T(8,128)(2,1)} %bitcast.163, f32[16,16,64,64]{2,3,1,0:T(8,128)} %get-tuple-element.29, f32[16,16,64]{2,1,0:T(8,128)S(1)} %get-tuple-element.28), kind=kOutput, calls=%fused_computation.107 | convolution fusion | flops 69730304 | bytes 6356992 | tf_op jit(solution)/shard_map/nhqk,nkhd->nqhd/dot_general | solution.py:69
  160.7 7.1 %fusion.62 = bf16[16,64,512]{2,1,0:T(8,128)(2,1)S(1)} fusion(bf16[16,64,512]{2,1,0:T(8,128)(2,1)S(1)} %get-tuple-element.31, bf16[2048,512]{1,0:T(8,128)(2,1)} %param.36, bf16[512,2048]{1,0:T(8,128)(2,1)} %param.35, f32[512]{0:T(512)S(1)} %copy-done.12, f32[16,64]{1,0:T(8,128)S(1)} %add_rsqrt_fusion.2, f32[16,64]{1,0:T(8,128)S(1)} %broadcast_multiply_fusion.2), kind=kOutput, calls=%fused_computation.86 | convolution fusion | flops 4318035968 | bytes 6301696 | tf_op jit(solution)/shard_map/dot_general | solution.py:90
  172.2 5.4 %convolution_convert_fusion = bf16[32,32,1536]{2,1,0:T(8,128)(2,1)} fusion(bf16[512,1536]{1,0:T(8,128)(2,1)} %param.38, f32[32,32,512]{2,1,0:T(8,128)S(1)} %bitcast.152, f32[512]{0:T(512)S(1)} %copy-done.13, f32[32,32]{1,0:T(8,128)S(1)} %rsqrt.42, f32[32,32]{1,0:T(8,128)S(1)} %div.85), kind=kOutput, calls=%fused_computation.63 | convolution fusion | flops 1614282752 | bytes 6825984 | tf_op jit(solution)/shard_map/dot_general | solution.py:231
  177.6 7.2 %reshape.290 = bf16[1,8,4,1,16,2,1536]{6,5,4,2,1,3,0:T(2,128)(2,1)} reshape(bf16[32,32,1536]{2,1,0:T(8,128)(2,1)} %convolution_convert_fusion) | data formatting | bytes 6291456 | tf_op jit(solution)/shard_map/reshape | solution.py:125
  184.8 2.6 copy.155
  187.4 4.9 %copy.156 = bf16[128,1,4,1,2,1536]{5,4,2,3,1,0:T(2,128)(2,1)} copy(bf16[128,1,4,1,2,1536]{5,0,4,2,3,1:T(8,128)(2,1)S(1)} %bitcast.143) | data formatting | bytes 6291456 | tf_op jit(solution)/shard_map/reshape | solution.py:128
  192.3 6.2 %all-to-all-start = ((bf16[128,1,4,1,2,1536]{5,4,2,3,1,0:T(2,128)(2,1)}), bf16[128,1,4,1,2,1536]{5,4,2,3,1,0:T(2,128)(2,1)}, u32[]{:S(2)}, u32[]{:S(2)}) async-start(bf16[128,1,4,1,2,1536]{5,4,2,3,1,0:T(2,128)(2,1)} %copy.156), calls=%async_computation | async-start | bytes 6291456 | tf_op jit(solution)/shard_map/all_to_all | solution.py:131
  198.6 3.2 %fusion.96 = f32[16,64,64]{2,0,1:T(8,128)S(1)} fusion(s32[64,64]{1,0:T(8,128)S(1)} %add_add_fusion, f32[16,225]{1,0:T(8,128)S(1)} %copy-done.10), kind=kOutput, calls=%fused_computation.111 | convolution fusion | flops 177868800 | bytes 292928 | tf_op jit(solution)/shard_map/bp,rjp->brj/dot_general | solution.py:44
  202.9 36.4 %all-to-all-done = bf16[128,1,4,1,2,1536]{5,4,2,3,1,0:T(2,128)(2,1)} async-done(((bf16[128,1,4,1,2,1536]{5,4,2,3,1,0:T(2,128)(2,1)}), bf16[128,1,4,1,2,1536]{5,4,2,3,1,0:T(2,128)(2,1)}, u32[]{:S(2)}, u32[]{:S(2)}) %all-to-all-start) | async-done | bytes 3145760 | tf_op jit(solution)/shard_map/all_to_all | solution.py:131
  239.3 2.8 copy.157
  247.3 2.7 copy.161
  250.1 2.7 copy.162
  254.6 8.9 %fusion.157 = (f32[16,16,64]{2,1,0:T(8,128)S(1)}, f32[16,16,64,64]{2,3,1,0:T(8,128)}) fusion(f32[16,64,64]{1,2,0:T(8,128)} %copy.163, bf16[16,64,16,32]{1,3,2,0:T(8,128)(2,1)} %bitcast.161, bf16[16,64,16,32]{1,3,2,0:T(8,128)(2,1)} %bitcast.164), kind=kOutput, calls=%fused_computation.179 | convolution fusion | flops 71303232 | bytes 6619136 | tf_op jit(solution)/shard_map/sub | solution.py:65
  263.6 6.5 %convert_bitcast_fusion.2 = bf16[16,64,16,32]{1,3,2,0:T(8,128)(2,1)} fusion(bf16[16,64,16,32]{1,3,2,0:T(8,128)(2,1)} %bitcast.165, f32[16,16,64,64]{2,3,1,0:T(8,128)} %get-tuple-element.33, f32[16,16,64]{2,1,0:T(8,128)S(1)} %get-tuple-element.32), kind=kOutput, calls=%fused_computation.99 | convolution fusion | flops 69730304 | bytes 6356992 | tf_op jit(solution)/shard_map/nhqk,nkhd->nqhd/dot_general | solution.py:69
  270.1 5.9 %copy.165 = bf16[16,64,16,32]{3,2,1,0:T(8,128)(2,1)} copy(bf16[16,64,16,32]{1,3,2,0:T(8,128)(2,1)} %convert_bitcast_fusion.2) | data formatting | bytes 2097152 | tf_op jit(solution)/shard_map/convert_element_type | solution.py:72
  275.9 5.9 %reshape_reshape.3 = bf16[1,4,2,2,8,1,8,1,512]{8,6,4,3,2,1,7,5,0:T(8,128)(2,1)S(1)} reshape(bf16[16,64,16,32]{3,2,1,0:T(8,128)(2,1)} %copy.165) | data formatting | bytes 2097152 | tf_op jit(solution)/shard_map/reshape;reshape | solution.py:147
  283.9 23.6 %all_to_all.10 = bf16[128,1,4,1,2,512]{5,4,2,3,1,0:T(2,128)(2,1)S(1)} all-to-all(bf16[128,1,4,1,2,512]{5,4,2,3,1,0:T(2,128)(2,1)S(1)} %copy.168), channel_id=1, replica_groups=mesh['row'=8,'col'=16] {'row','col'}, dimensions={0} | all-to-all | bytes 2097152 | tf_op jit(solution)/shard_map/all_to_all | solution.py:156
  310.2 2.1 convert_reduce_fusion
  312.9 8.2 %fusion.63 = bf16[32,32,512]{2,1,0:T(8,128)(2,1)} fusion(bf16[32,32,512]{2,1,0:T(8,128)(2,1)S(1)} %get-tuple-element.35, bf16[2048,512]{1,0:T(8,128)(2,1)} %param.43, bf16[512,2048]{1,0:T(8,128)(2,1)} %param.42, f32[512]{0:T(512)S(1)} %copy-done.14, f32[32,32]{1,0:T(8,128)S(1)} %add_rsqrt_fusion.1, f32[32,32]{1,0:T(8,128)S(1)} %broadcast_multiply_fusion.1), kind=kOutput, calls=%fused_computation.87 | convolution fusion | flops 4318035968 | bytes 6301696 | tf_op jit(solution)/shard_map/dot_general | solution.py:90
  (84 shorter events, 36.6 us)
Async XLA Ops:
  0.0 1.6 copy-start
  0.0 12.2 %copy-start.7 = (f32[9,2048]{1,0:T(8,128)S(1)}, f32[9,2048]{1,0:T(8,128)}, u32[]{:S(2)}) copy-start(f32[9,2048]{1,0:T(8,128)} %param.26) | copy-start | bytes 221188
  6.8 9.8 %copy-start.2 = (bf16[32,32,2048]{2,1,0:T(8,128)(2,1)}, bf16[32,32,2048]{2,1,0:T(8,128)(2,1)S(1)}, u32[]{:S(2)}) copy-start(bf16[32,32,2048]{2,1,0:T(8,128)(2,1)S(1)} %fusion.9) | copy-start | bytes 12582916
  6.8 17.7 %copy-start.9 = (f32[16,225]{1,0:T(8,128)S(1)}, f32[16,225]{1,0:T(8,128)}, u32[]{:S(2)}) copy-start(f32[16,225]{1,0:T(8,128)} %param.33) | copy-start | bytes 43204
  6.8 6.2 %collective-permute-start = (bf16[1,32,2048]{2,1,0:T(8,128)(2,1)S(1)}, bf16[1,32,2048]{2,1,0:T(8,128)(2,1)S(1)}, u32[]{:S(2)}, u32[]{:S(2)}) collective-permute-start(bf16[1,32,2048]{2,1,0:T(8,128)(2,1)S(1)} %get-tuple-element.11), channel_id=1, source_target_pairs={{0,16},{16,32},{32,48},{48,64},{64,80},{80,96},{96,112},{1,17},{17... | collective-permute-start | bytes 393224 | tf_op jit(solution)/shard_map/ppermute | solution.py:17
  10.9 5.7 %collective-permute-start.1 = (bf16[1,32,2048]{2,1,0:T(8,128)(2,1)S(1)}, bf16[1,32,2048]{2,1,0:T(8,128)(2,1)S(1)}, u32[]{:S(2)}, u32[]{:S(2)}) collective-permute-start(bf16[1,32,2048]{2,1,0:T(8,128)(2,1)S(1)} %get-tuple-element.12), channel_id=1, source_target_pairs={{16,0},{32,16},{48,32},{64,48},{80,64},{96,80},{112,96},{17,1},{33... | collective-permute-start | bytes 393224 | tf_op jit(solution)/shard_map/ppermute | solution.py:19
  17.1 11.8 %collective-permute-start.2 = (bf16[34,1,2048]{2,1,0:T(2,128)(2,1)S(1)}, bf16[34,1,2048]{2,1,0:T(2,128)(2,1)S(1)}, u32[]{:S(2)}, u32[]{:S(2)}) collective-permute-start(bf16[34,1,2048]{2,1,0:T(2,128)(2,1)S(1)} %get-tuple-element.9), channel_id=1, source_target_pairs={{0,1},{1,2},{2,3},{3,4},{4,5},{5,6},{6,7},{7,8},{8,9},{9,10},{10,1... | collective-permute-start | bytes 417800 | tf_op jit(solution)/shard_map/ppermute | solution.py:17
  22.6 7.9 %collective-permute-start.3 = (bf16[34,1,2048]{2,1,0:T(2,128)(2,1)S(1)}, bf16[34,1,2048]{2,1,0:T(2,128)(2,1)S(1)}, u32[]{:S(2)}, u32[]{:S(2)}) collective-permute-start(bf16[34,1,2048]{2,1,0:T(2,128)(2,1)S(1)} %get-tuple-element.10), channel_id=1, source_target_pairs={{1,0},{2,1},{3,2},{4,3},{5,4},{6,5},{7,6},{8,7},{9,8},{10,9},{11,1... | collective-permute-start | bytes 417800 | tf_op jit(solution)/shard_map/ppermute | solution.py:19
  28.9 7.8 %copy-start.3 = (bf16[32,32,2048]{2,1,0:T(8,128)(2,1)S(1)}, bf16[32,32,2048]{2,1,0:T(8,128)(2,1)}, u32[]{:S(2)}) copy-start(bf16[32,32,2048]{2,1,0:T(8,128)(2,1)} %copy-done.2) | copy-start | bytes 12582916
  36.6 84.6 %copy-start.4 = (bf16[2048,128]{1,0:T(8,128)(2,1)S(1)}, bf16[2048,128]{1,0:T(8,128)(2,1)}, u32[]{:S(2)}) copy-start(bf16[2048,128]{1,0:T(8,128)(2,1)} %param.27) | copy-start | bytes 1572868
  36.6 84.9 %copy-start.5 = (bf16[128,2048]{1,0:T(8,128)(2,1)S(1)}, bf16[128,2048]{1,0:T(8,128)(2,1)}, u32[]{:S(2)}) copy-start(bf16[128,2048]{1,0:T(8,128)(2,1)} %param.28) | copy-start | bytes 1572868
  36.7 85.2 %copy-start.8 = (bf16[32,32,512]{2,1,0:T(8,128)(2,1)S(1)}, bf16[32,32,512]{2,1,0:T(8,128)(2,1)}, u32[]{:S(2)}) copy-start(bf16[32,32,512]{2,1,0:T(8,128)(2,1)} %param.22) | copy-start | bytes 3145732
  128.5 4.3 %copy-start.11 = (f32[512]{0:T(512)S(1)}, f32[512]{0:T(512)}, u32[]{:S(2)}) copy-start(f32[512]{0:T(512)} %param.30) | copy-start | bytes 6148
  154.1 5.3 %copy-start.6 = (bf16[512,512]{1,0:T(8,128)(2,1)S(1)}, bf16[512,512]{1,0:T(8,128)(2,1)}, u32[]{:S(2)}) copy-start(bf16[512,512]{1,0:T(8,128)(2,1)} %param.32) | copy-start | bytes 1572868
  159.3 1.3 copy-start.12
  168.0 4.2 %copy-start.13 = (f32[512]{0:T(512)S(1)}, f32[512]{0:T(512)}, u32[]{:S(2)}) copy-start(f32[512]{0:T(512)} %param.37) | copy-start | bytes 6148
  192.3 6.2 %copy-start.10 = (f32[16,225]{1,0:T(8,128)S(1)}, f32[16,225]{1,0:T(8,128)}, u32[]{:S(2)}) copy-start(f32[16,225]{1,0:T(8,128)} %param.40) | copy-start | bytes 43204
  192.3 46.9 %all-to-all-start = ((bf16[128,1,4,1,2,1536]{5,4,2,3,1,0:T(2,128)(2,1)}), bf16[128,1,4,1,2,1536]{5,4,2,3,1,0:T(2,128)(2,1)}, u32[]{:S(2)}, u32[]{:S(2)}) async-start(bf16[128,1,4,1,2,1536]{5,4,2,3,1,0:T(2,128)(2,1)} %copy.156), calls=%async_computation | async-start | bytes 6291456 | tf_op jit(solution)/shard_map/all_to_all | solution.py:131
  308.9 3.9 %copy-start.14 = (f32[512]{0:T(512)S(1)}, f32[512]{0:T(512)}, u32[]{:S(2)}) copy-start(f32[512]{0:T(512)} %param.41) | copy-start | bytes 6148
  312.9 8.2 %copy-start.1 = (bf16[512,2048]{1,0:T(8,128)(2,1)S(1)}, bf16[512,2048]{1,0:T(8,128)(2,1)}, u32[]{:S(2)}) copy-start(bf16[512,2048]{1,0:T(8,128)(2,1)} %param.25) | copy-start | bytes 6291460
where the time goes:
time: 327 us; the launch traced here: 321 us
  blocking collectives  93.6 us (29%)
  matrix products  75 us (23%)
  local copies, waits for them, and re-layouts  63.6 us (19%)
  waiting for transfers between devices  42.3 us (13%)
  other arithmetic  27.1 us (8%)
  starting transfers between devices  19 us (6%)
    psum x1, blocking collectives, per_device(): channel_sums = lax.psum(jnp.sum(depthwise, axis=(0, 1)), ('row', 'col'))  70 us
    all_to_all x1, waiting for transfers between devices, grid_layout(): lax.all_to_all(flat, ('row', 'col'), split_axis=0, concat_axis=0, tiled=T...  36.4 us
    all_to_all x1, blocking collectives, spatial_layout(): lax.all_to_all(flat, ('row', 'col'), split_axis=0, concat_axis=0, tiled=T...  23.6 us
    sub x2, matrix products, attend(): weight_tensors = jnp.exp(scores - row_max)  17.8 us
    dot_general x2, matrix products, feed_forward(): jnp.dot(hidden, out_weight, preferred_element_type=jnp.float32)  15.2 us
    reduce_sum x1, other arithmetic, per_device(): channel_sums = lax.psum(jnp.sum(depthwise, axis=(0, 1)), ('row', 'col'))  14.6 us
    dot_general x2, matrix products, attend(): jnp.einsum('nhqk,nkhd->nqhd', attention_weight_map, values, preferred_ele...  11.8 us
    reshape x2, local copies, waits for them, and re-layouts, grid_layout(): field.reshape(row_fold, row_devices, row_rest, col_fold, col_devices, col...  9.8 us
  transfers between devices with their start and end apart: 5, of which 4 were waited for; matrix products, arithmetic and copies ran while one was open for 3% of the time, Pallas kernels for 0%

commit v1 on v0

v1 whole, which is shorter than its diff:
```python
import jax
import jax.numpy as jnp
from jax import lax
from jax.experimental import pallas as pl
from jax.experimental.pallas import tpu as pltpu
from jax.sharding import Mesh, PartitionSpec as P

BF = jnp.bfloat16
F32 = jnp.float32


def norm(xf, g):
    center = xf - jnp.mean(xf, axis=-1, keepdims=True)
    spread = jnp.mean(center * center, axis=-1, keepdims=True)
    return (center * lax.rsqrt(spread + 1e-05) * g).astype(BF)


def gelu(v):
    half = 0.5 * v
    return half + half * jnp.tanh(v * (0.7978845608028654 + 0.035677408136300125 * (v * v)))


def dot(a, b):
    return jnp.dot(a, b, preferred_element_type=F32)


def dot_nt(a, b):
    return lax.dot_general(a, b, (((1,), (1,)), ((), ())), preferred_element_type=F32)


def dot_tn(a, b):
    return lax.dot_general(a, b, (((0,), (0,)), ((), ())), preferred_element_type=F32)


def attn_ff(x, g1, pk, pqvt, o, bias, g2, u, w, mixt, kbuf, qvt, ff_block=512):
    m = x.shape[0]
    xf = x.astype(F32)
    n = norm(xf, g1[...])
    kbuf[...] = dot(n, pk[...]).astype(BF)
    qvt[...] = dot_nt(pqvt[...], n).astype(BF)
    low = lax.broadcasted_iota(jnp.int32, (64, 128), 1) < 64
    zero = jnp.zeros((32, 128), BF)

    def pair(p, carry):
        lanes = pl.ds(pl.multiple_of(p * 128, 128), 128)
        for g in range(4):
            keys = kbuf[lanes, 128 * g:128 * g + 128]
            q = [qvt[128 * g + 32 * h:128 * g + 32 * h + 32, lanes] for h in range(4)]
            qbd = jnp.concatenate(
                [jnp.concatenate([q[h] if j == h else zero for j in range(4)], axis=0) for h in range(4)],
                axis=1)
            s4 = dot(keys, qbd)
            for h in range(4):
                head = 4 * g + h
                s = s4[:, 128 * h:128 * h + 128]
                s = jnp.where(low, s[:64], s[64:]) * (32 ** -0.5) + bias[head]
                e = jnp.exp(s - jnp.max(s, axis=0, keepdims=True))
                r = 1.0 / jnp.sum(e, axis=0, keepdims=True)
                pbd = jnp.concatenate(
                    [jnp.where(low, e, 0.0).astype(BF), jnp.where(low, 0.0, e).astype(BF)], axis=0)
                vt = qvt[512 + 32 * head:544 + 32 * head, lanes]
                mixt[32 * head:32 * head + 32, lanes] = (dot(vt, pbd) * r).astype(BF)
        return carry

    lax.fori_loop(0, m // 128, pair, 0)
    y = (xf + dot_tn(mixt[...], o[...])).astype(BF)
    yf = y.astype(F32)
    n2 = norm(yf, g2[...])
    acc = yf
    for j in range(u.shape[1] // ff_block):
        cols = slice(j * ff_block, (j + 1) * ff_block)
        hidden = gelu(dot(n2, u[:, cols])).astype(BF)
        acc = acc + dot(hidden, w[cols, :])
    return acc.astype(BF)


def section_body(x, g1, pk, pqvt, o, bias, g2, u, w, out, mixt, kbuf, qvt):
    out[...] = attn_ff(x[...], g1, pk, pqvt, o, bias, g2, u, w, mixt, kbuf, qvt)


def whole(shape):
    return pl.BlockSpec(shape, lambda i: (0,) * len(shape))


def section_call(x, g1, pk, pqvt, o, bias, g2, u, w, m=256):
    cells, feats = x.shape
    args = (g1.reshape(1, -1), pk, pqvt, o, bias, g2.reshape(1, -1), u, w)
    return pl.pallas_call(
        section_body,
        grid=(cells // m,),
        in_specs=[pl.BlockSpec((m, feats), lambda i: (i, 0))] + [whole(a.shape) for a in args],
        out_specs=pl.BlockSpec((m, feats), lambda i: (i, 0)),
        out_shape=jax.ShapeDtypeStruct((cells, feats), BF),
        scratch_shapes=[pltpu.VMEM((feats, m), BF), pltpu.VMEM((m, feats), BF), pltpu.VMEM((2 * feats, m), BF)],
        compiler_params=pltpu.CompilerParams(vmem_limit_bytes=48 * 2**20),
    )(x, *args)


def bias_table(table):
    t = table.reshape(-1, 15, 15)
    rows = jnp.stack([t[:, 7 - q:15 - q] for q in range(8)], axis=1)
    both = jnp.stack([rows[..., 7 - q:15 - q] for q in range(8)], axis=2)
    out = both.reshape(-1, 64, 64)
    return jnp.concatenate([out, out], axis=-1)


def extended(cells, sides, width):
    for axis, dim, count in sides:
        ends = count - 1
        head = lax.slice_in_dim(cells, 0, width, axis=dim)
        tail = lax.slice_in_dim(cells, cells.shape[dim] - width, cells.shape[dim], axis=dim)
        cells = jnp.concatenate(
            [
                lax.ppermute(tail, axis, [(i, i + 1) for i in range(ends)]),
                cells,
                lax.ppermute(head, axis, [(i + 1, i) for i in range(ends)]),
            ],
            axis=dim,
        )
    return cells


def squeeze_gate(pooled, squeeze_down, squeeze_up):
    reduced = jax.nn.silu(
        jnp.dot(pooled[None, :], squeeze_down.astype(F32), precision=lax.Precision.HIGHEST)
    )
    return jax.nn.sigmoid(
        jnp.dot(reduced, squeeze_up.astype(F32), precision=lax.Precision.HIGHEST)
    )[0]


def channel_total(sums):
    sums = sums + lax.ppermute(sums, "core", [(0, 1), (1, 0)])
    width = sums.shape[0]
    copies = jnp.broadcast_to(sums.reshape(1, width // 128, 128), (64, width // 128, 128))
    copies = lax.all_to_all(copies, ("row", "ch"), 0, 0, tiled=True)
    return copies.sum(0).reshape(width)


def swap(windows):
    return lax.all_to_all(
        windows.reshape(16, 64, -1), ("row", "ch"), split_axis=1, concat_axis=1, tiled=True
    ).reshape(1024, -1)


def per_device(
    latent, conv_scale, conv_shift, expand_weight, depth_kernel, squeeze_down, squeeze_up, project_weight,
    block_gain, block_projection, block_output, block_table, first_gain, first_expand, first_reduce,
    grid_gain, grid_projection, grid_output, grid_table, second_gain, second_expand, second_reduce,
):
    row_count, col_count, channels = latent.shape
    conv_in = (latent.astype(F32) * conv_scale + conv_shift).astype(BF)
    expanded = jax.nn.gelu(dot(conv_in, expand_weight), approximate=True).astype(BF)
    padded = extended(expanded, (("row", 0, 8), (("ch", "core"), 1, 16)), 1)
    summed = jnp.zeros((row_count, col_count, padded.shape[-1]), F32)
    for offset in range(9):
        down_step = offset // 3
        side_step = offset % 3
        summed = (
            summed
            + padded[down_step : down_step + row_count, side_step : side_step + col_count].astype(F32)
            * depth_kernel[offset]
        )
    depthwise = jax.nn.gelu(summed, approximate=True)
    channel_sums = channel_total(jnp.sum(depthwise, axis=(0, 1)))
    excite = squeeze_gate(channel_sums / (256 * 512), squeeze_down, squeeze_up)
    gated = (depthwise * excite).astype(BF)
    conv_out = (latent.astype(F32) + dot(gated, project_weight)).astype(BF)
    windows = conv_out.reshape(4, 8, 4, 8, channels).transpose(0, 2, 1, 3, 4).reshape(1024, channels)

    def split(projection):
        keys = projection[:, channels : 2 * channels]
        others = jnp.concatenate([projection[:, :channels], projection[:, 2 * channels :]], axis=1).T
        return keys, others

    windows = section_call(
        windows, block_gain, *split(block_projection), block_output, bias_table(block_table),
        first_gain, first_expand, first_reduce,
    )
    windows = swap(windows)
    windows = section_call(
        windows, grid_gain, *split(grid_projection), grid_output, bias_table(grid_table),
        second_gain, second_expand, second_reduce,
    )
    windows = swap(windows)
    return windows.reshape(4, 4, 8, 8, channels).transpose(0, 2, 1, 3, 4).reshape(row_count, col_count, channels)


def solution(mesh):
    wide = Mesh(mesh.devices.reshape(8, 8, 2), ("row", "ch", "core"))
    field = P("row", ("ch", "core"), None)
    return jax.shard_map(
        per_device, mesh=wide, in_specs=(field,) + (P(),) * 21, out_specs=field, check_vma=False
    )
```

time: 327 us -> 201 us (0.61)
  blocking collectives: 93.6 us -> 22.5 us
  matrix products: 75 us -> 14.5 us
  Pallas kernels: 0 us -> 44.8 us
  waiting for transfers between devices: 42.3 us -> 10.8 us
  local copies, waits for them, and re-layouts: 63.6 us -> 45.9 us
  starting transfers between devices: 19 us -> 30.7 us
    psum x1 -> x0, blocking collectives: 70 us -> none  [per_device(): channel_sums = lax.psum(jnp.sum(depthwise, axis=(0, 1)), ('row', 'col'))]
    pallas_call x0 -> x2, Pallas kernels: none -> 44.8 us  [section_call(): pl.pallas_call(section_body, grid=(cells // m,), in_specs=[pl.BlockSpec((...]
    dot_general x14 -> x4, matrix products: 57.2 us -> 14.5 us  [the longest x2 11.8 us: dot(): return jnp.dot(a, b, preferred_element_type=F32)]
    all_to_all x1 -> x2, waiting for transfers between devices: 36.4 us -> 9.83 us  [the longest x1 8.13 us: channel_total(): copies = lax.all_to_all(copies, ('row', 'ch'), 0, 0, tiled=True)]
    sub x2 -> x0, matrix products: 17.8 us -> none  [attend(): weight_tensors = jnp.exp(scores - row_max)]
    unnamed x30 -> x66, local copies, waits for them, and re-layouts: 1.66 us -> 19.1 us
    slice x8 -> x2, local copies, waits for them, and re-layouts: 18.1 us -> 3.42 us  [split(): projection[:, :channels]]
    all_to_all x1 -> x2, starting transfers between devices: 6.21 us -> 18 us  [the longest x1 12.3 us: channel_total(): copies = lax.all_to_all(copies, ('row', 'ch'), 0, 0, tiled=True)]
  transfers between devices with their start and end apart: 5 -> 7, of which waited for: 4 -> 3; matrix products, arithmetic and copies ran while one was open for 3% -> 19% of each run, Pallas kernels for 0% -> 0%
where the time goes in v1:
time: 201 us; the launch traced here: 197 us
  local copies, waits for them, and re-layouts  45.9 us (23%)
  Pallas kernels  44.8 us (22%)
  starting transfers between devices  30.7 us (15%)
  other arithmetic  27.5 us (14%)
  blocking collectives  22.5 us (11%)
  matrix products  14.5 us (7%)
  waiting for transfers between devices  10.8 us (5%)
    pallas_call x2, Pallas kernels, section_call(): pl.pallas_call(section_body, grid=(cells // m,), in_specs=[pl.BlockSpec((...  44.8 us
    all_to_all x1, blocking collectives, swap(): lax.all_to_all(windows.reshape(16, 64, -1), ('row', 'ch'), split_axis=1,...  22.5 us
    unnamed x66, local copies, waits for them, and re-layouts  19.1 us
    reduce_sum x1, other arithmetic, per_device(): channel_sums = channel_total(jnp.sum(depthwise, axis=(0, 1)))  14.6 us
    all_to_all x1, starting transfers between devices, channel_total(): copies = lax.all_to_all(copies, ('row', 'ch'), 0, 0, tiled=True)  12.3 us
    dot_general x2, matrix products, dot(): return jnp.dot(a, b, preferred_element_type=F32)  11.8 us
    ppermute x2, starting transfers between devices, extended(): lax.ppermute(tail, axis, [(i, i + 1) for i in range(ends)])  9.49 us
    another operation x4, local copies, waits for them, and re-layouts, bias_table(): both = jnp.stack([rows[..., 7 - q:15 - q] for q in range(8)], axis=2)  9.32 us
  transfers between devices with their start and end apart: 7, of which 3 were waited for; matrix products, arithmetic and copies ran while one was open for 19% of the time, Pallas kernels for 0%

profile of v1, /device:TPU:1, one launch (start us, length us, event | category | flops | bytes accessed | tf_op | source)
XLA Modules:
  0.0 197.3 jit_solution(11893594566220661071)
XLA Ops:
  0.0 1.6 copy-done
  1.6 5.2 %fusion.7 = bf16[32,32,2048]{2,1,0:T(8,128)(2,1)S(1)} fusion(bf16[512,2048]{1,0:T(8,128)(2,1)S(1)} %copy-done, bf16[32,32,512]{2,1,0:T(8,128)(2,1)} %param.22, f32[512]{0:T(512)} %param.24, f32[512]{0:T(512)} %param.23), kind=kOutput, calls=%fused_computation.9 | convolution fusion | flops 2168455168 | bytes 7344128 | tf_op jit(solution)/shard_map/dot_general | solution.py:24
  6.8 1.3 collective-permute-start.1
  8.1 4.7 %collective-permute-start = (bf16[1,32,2048]{2,1,0:T(8,128)(2,1)S(1)}, bf16[1,32,2048]{2,1,0:T(8,128)(2,1)S(1)}, u32[]{:S(2)}, u32[]{:S(2)}) collective-permute-start(bf16[1,32,2048]{2,1,0:T(8,128)(2,1)S(1)} %get-tuple-element.11), channel_id=1, source_target_pairs={{0,16},{16,32},{32,48},{48,64},{64,80},{80,96},{96,112},{1,17},{17... | collective-permute-start | bytes 393224 | tf_op jit(solution)/shard_map/ppermute | solution.py:114
  22.3 1.1 fusion.34
  24.3 2.8 %pad_maximum_fusion.7 = (bf16[34,1,2048]{2,1,0:T(2,128)(2,1)}, bf16[34,1,2048]{2,1,0:T(2,128)(2,1)}) fusion(bf16[1,32,2048]{2,1,0:T(8,128)(2,1)S(1)} %collective-permute-done.1, bf16[32,32,2048]{2,1,0:T(8,128)(2,1)} %copy-done.8, bf16[1,32,2048]{2,1,0:T(8,128)(2,1)S(1)} %collective-permute-done), kind=kLoop, calls=%fused_computation.72 | loop fusion | flops 835584 | bytes 4734976 | tf_op jit(solution)/shard_map/slice | solution.py:111
  27.1 4.8 %collective-permute-start.2 = (bf16[34,1,2048]{2,1,0:T(2,128)(2,1)}, bf16[34,1,2048]{2,1,0:T(2,128)(2,1)}, u32[]{:S(2)}, u32[]{:S(2)}) collective-permute-start(bf16[34,1,2048]{2,1,0:T(2,128)(2,1)} %get-tuple-element.9), channel_id=1, source_target_pairs={{0,1},{1,2},{2,3},{3,4},{4,5},{5,6},{6,7},{7,8},{8,9},{9,10},{10,1... | collective-permute-start | bytes 417800 | tf_op jit(solution)/shard_map/ppermute | solution.py:114
  32.0 1.9 collective-permute-start.3
  36.1 3.8 %copy.87 = f32[16,8,8,8,8]{0,4,3,2,1:T(8,128)} copy(f32[16,8,8,8,8]{4,3,0,1,2:T(8,128)} %fusion.35) | data formatting | bytes 524288 | tf_op jit(solution)/shard_map/stack | solution.py:102
  39.9 2.3 %copy.88 = f32[16,64,64]{2,1,0:T(8,128)S(1)} copy(f32[16,64,64]{0,2,1:T(8,128)} %bitcast.188) | data formatting | bytes 524288 | tf_op jit(solution)/shard_map/reshape | solution.py:103
  42.2 1.1 maximum_bitcast_fusion.pqvt
  43.4 6.1 %maximum_maximum_fusion = (bf16[34,33,2048]{2,1,0:T(8,128)(2,1)S(1)}, bf16[34,33,2048]{2,1,0:T(8,128)(2,1)S(1)}) fusion(bf16[1,32,2048]{2,1,0:T(8,128)(2,1)S(1)} %collective-permute-done.1, bf16[32,32,2048]{2,1,0:T(8,128)(2,1)} %copy-done.8, bf16[1,32,2048]{2,1,0:T(8,128)(2,1)S(1)} %collective-permute-done, bf16[34,1,2048]{2,1,0:T(2,128)(2,1)} %collective-permute-done.2, ...), kind=kLoop, calls=%fused_computation.18 | loop fusion | flops 36765696 | bytes 13926400 | tf_op jit(solution)/shard_map/concatenate | solution.py:112
  49.5 14.6 %fusion.49 = (f32[2048]{0:T(1024)S(1)}, f32[32,32,2048]{2,1,0:T(8,128)}) fusion(f32[2048]{0:T(1024)S(1)} %bitcast.199, bf16[34,33,2048]{2,1,0:T(8,128)(2,1)S(1)} %get-tuple-element.8, f32[2048]{0:T(1024)S(1)} %bitcast.200, bf16[1,32,2048]{2,1,0:T(8,128)(2,1)S(1)} %collective-permute-done.1, bf16[32,32,2048]{2,1,0:T(8,128)(2,1)S(1)} %copy-done.9, ...), kind=kLoop, calls=%fused_computation.115 | loop fusion | flops 77592576 | bytes 38092800 | tf_op jit(solution)/shard_map/reduce_sum | solution.py:165
  66.1 12.3 %all-to-all-start = ((f32[64,16,128]{2,1,0:T(8,128)}), f32[64,16,128]{2,1,0:T(8,128)}, u32[]{:S(2)}, u32[]{:S(2)}) async-start(f32[64,16,128]{2,1,0:T(8,128)} %broadcast_in_dim.5), calls=%async_computation | async-start | bytes 1048576 | tf_op jit(solution)/shard_map/all_to_all | solution.py:136
  79.5 2.5 %fusion.52 = (bf16[512,512]{1,0:T(8,128)(2,1)}, bf16[512,512]{1,0:T(8,128)(2,1)S(1)}, bf16[512,512]{1,0:T(8,128)(2,1)}) fusion(bf16[512,1536]{1,0:T(8,128)(2,1)} %param.38), kind=kLoop, calls=%fused_computation.117 | loop fusion | bytes 3145728 | tf_op jit(solution)/shard_map/slice | solution.py:173
  82.0 8.1 %all-to-all-done = f32[64,16,128]{2,1,0:T(8,128)} async-done(((f32[64,16,128]{2,1,0:T(8,128)}), f32[64,16,128]{2,1,0:T(8,128)}, u32[]{:S(2)}, u32[]{:S(2)}) %all-to-all-start) | async-done | bytes 524320 | tf_op jit(solution)/shard_map/all_to_all | solution.py:136
  90.1 1.1 reduce_sum.19
  91.2 1.4 convolution_bitcast_fusion
  92.6 1.4 fusion.43
  94.0 6.6 %fusion.19 = bf16[32,32,512]{2,1,0:T(8,128)(2,1)S(1)} fusion(bf16[32,32,512]{2,1,0:T(8,128)(2,1)} %param.22, bf16[2048,512]{1,0:T(8,128)(2,1)} %param.29, f32[32,32,2048]{2,1,0:T(8,128)} %get-tuple-element.6, f32[2048]{0:T(1024)S(1)} %add_divide_fusion), kind=kOutput, calls=%fused_computation.28 | convolution fusion | flops 2153250816 | bytes 12591104 | tf_op jit(solution)/shard_map/dot_general | solution.py:24
  100.8 22.4 %shard_map.208 = bf16[1024,512]{1,0:T(8,128)(2,1)S(1)} custom-call(bf16[1024,512]{1,0:T(8,128)(2,1)S(1)} %bitcast.180, f32[1,512]{1,0:T(1,128)S(1)} %bitcast.184, bf16[512,512]{1,0:T(8,128)(2,1)S(1)} %get-tuple-element.17.pk, bf16[1024,512]{1,0:T(8,128)(2,1)S(1)} %maximum_bitcast_fusion.pqvt, bf16[512,512]{1,0:T(8,128)(2,1)S(1)} %copy-done.2, ...), custom_call_target="tpu_custom_call" | custom-call | tf_op jit(solution)/shard_map/pallas_call | solution.py:88
  123.2 1.5 copy.90
  124.8 5.7 %all-to-all-start.1 = ((bf16[16,64,512]{2,0,1:T(8,128)(2,1)}), bf16[16,64,512]{2,0,1:T(8,128)(2,1)}, u32[]{:S(2)}, u32[]{:S(2)}) async-start(bf16[16,64,512]{2,0,1:T(8,128)(2,1)} %copy.90), calls=%async_computation.1 | async-start | bytes 2097152 | tf_op jit(solution)/shard_map/all_to_all | solution.py:141
  136.4 3.8 %copy.94 = f32[16,8,8,8,8]{0,4,3,2,1:T(8,128)} copy(f32[16,8,8,8,8]{4,3,0,1,2:T(8,128)} %fusion.27) | data formatting | bytes 524288 | tf_op jit(solution)/shard_map/stack | solution.py:102
  140.2 2.4 %copy.95 = f32[16,64,64]{2,1,0:T(8,128)S(1)} copy(f32[16,64,64]{0,2,1:T(8,128)} %bitcast.189) | data formatting | bytes 524288 | tf_op jit(solution)/shard_map/reshape | solution.py:103
  142.8 1.3 maximum_bitcast_fusion.1.pqvt
  144.0 1.7 all-to-all-done.1
  145.7 1.8 copy.91
  147.6 22.4 %shard_map.209 = bf16[1024,512]{1,0:T(8,128)(2,1)S(1)} custom-call(bf16[1024,512]{1,0:T(8,128)(2,1)S(1)} %bitcast.181, f32[1,512]{1,0:T(1,128)S(1)} %bitcast.186, bf16[512,512]{1,0:T(8,128)(2,1)S(1)} %get-tuple-element.14.pk, bf16[1024,512]{1,0:T(8,128)(2,1)S(1)} %maximum_bitcast_fusion.1.pqvt, bf16[512,512]{1,0:T(8,128)(2,1)S(1)} %copy-done.3, ...), custom_call_target="tpu_custom_call" | custom-call | tf_op jit(solution)/shard_map/pallas_call | solution.py:88
  170.6 22.5 %all_to_all.15 = bf16[16,64,512]{2,0,1:T(8,128)(2,1)S(1)} all-to-all(bf16[16,64,512]{2,0,1:T(8,128)(2,1)S(1)} %copy.97), channel_id=1, replica_groups=mesh['row'=8,'ch'=8,'core'=2] {'row','ch'}, dimensions={1} | all-to-all | bytes 2097152 | tf_op jit(solution)/shard_map/all_to_all | solution.py:141
  193.1 1.1 reshape_reshape.3
  194.3 3.1 %copy.98 = bf16[4,8,4,8,512]{4,3,2,1,0:T(8,128)(2,1)} copy(bf16[4,8,4,8,512]{4,2,0,3,1:T(4,128)(2,1)} %bitcast.190) | data formatting | bytes 2097152 | tf_op jit(solution)/shard_map/transpose | solution.py:186
  (87 shorter events, 22.4 us)
Async XLA Ops:
  0.0 1.6 copy-start
  0.0 12.8 %copy-start.14 = (f32[9,2048]{1,0:T(8,128)S(1)}, f32[9,2048]{1,0:T(8,128)}, u32[]{:S(2)}) copy-start(f32[9,2048]{1,0:T(8,128)} %param.26) | copy-start | bytes 221188
  0.0 12.9 %copy-start.13 = (bf16[512,1536]{1,0:T(8,128)(2,1)S(1)}, bf16[512,1536]{1,0:T(8,128)(2,1)}, u32[]{:S(2)}) copy-start(bf16[512,1536]{1,0:T(8,128)(2,1)} %param.31) | copy-start | bytes 4718596
  0.0 13.8 %copy-start.15 = (f32[16,225]{1,0:T(8,128)S(1)}, f32[16,225]{1,0:T(8,128)}, u32[]{:S(2)}) copy-start(f32[16,225]{1,0:T(8,128)} %param.33) | copy-start | bytes 43204
  6.8 6.0 %copy-start.8 = (bf16[32,32,2048]{2,1,0:T(8,128)(2,1)}, bf16[32,32,2048]{2,1,0:T(8,128)(2,1)S(1)}, u32[]{:S(2)}) copy-start(bf16[32,32,2048]{2,1,0:T(8,128)(2,1)S(1)} %fusion.7) | copy-start | bytes 12582916
  6.8 17.5 %collective-permute-start.1 = (bf16[1,32,2048]{2,1,0:T(8,128)(2,1)S(1)}, bf16[1,32,2048]{2,1,0:T(8,128)(2,1)S(1)}, u32[]{:S(2)}, u32[]{:S(2)}) collective-permute-start(bf16[1,32,2048]{2,1,0:T(8,128)(2,1)S(1)} %get-tuple-element.12), channel_id=1, source_target_pairs={{16,0},{32,16},{48,32},{64,48},{80,64},{96,80},{112,96},{17,1},{33... | collective-permute-start | bytes 393224 | tf_op jit(solution)/shard_map/ppermute | solution.py:116
  8.1 16.2 %collective-permute-start = (bf16[1,32,2048]{2,1,0:T(8,128)(2,1)S(1)}, bf16[1,32,2048]{2,1,0:T(8,128)(2,1)S(1)}, u32[]{:S(2)}, u32[]{:S(2)}) collective-permute-start(bf16[1,32,2048]{2,1,0:T(8,128)(2,1)S(1)} %get-tuple-element.11), channel_id=1, source_target_pairs={{0,16},{16,32},{32,48},{48,64},{64,80},{80,96},{96,112},{1,17},{17... | collective-permute-start | bytes 393224 | tf_op jit(solution)/shard_map/ppermute | solution.py:114
  14.1 7.9 %copy-start.16 = (f32[16,225]{1,0:T(8,128)S(1)}, f32[16,225]{1,0:T(8,128)}, u32[]{:S(2)}) copy-start(f32[16,225]{1,0:T(8,128)} %param.40) | copy-start | bytes 43204
  22.2 12.7 %copy-start.10 = (bf16[512,512]{1,0:T(8,128)(2,1)S(1)}, bf16[512,512]{1,0:T(8,128)(2,1)}, u32[]{:S(2)}) copy-start(bf16[512,512]{1,0:T(8,128)(2,1)} %get-tuple-element.18) | copy-start | bytes 1572868
  27.1 16.2 %collective-permute-start.2 = (bf16[34,1,2048]{2,1,0:T(2,128)(2,1)}, bf16[34,1,2048]{2,1,0:T(2,128)(2,1)}, u32[]{:S(2)}, u32[]{:S(2)}) collective-permute-start(bf16[34,1,2048]{2,1,0:T(2,128)(2,1)} %get-tuple-element.9), channel_id=1, source_target_pairs={{0,1},{1,2},{2,3},{3,4},{4,5},{5,6},{6,7},{7,8},{8,9},{9,10},{10,1... | collective-permute-start | bytes 417800 | tf_op jit(solution)/shard_map/ppermute | solution.py:114
  32.0 11.4 %collective-permute-start.3 = (bf16[34,1,2048]{2,1,0:T(2,128)(2,1)}, bf16[34,1,2048]{2,1,0:T(2,128)(2,1)}, u32[]{:S(2)}, u32[]{:S(2)}) collective-permute-start(bf16[34,1,2048]{2,1,0:T(2,128)(2,1)} %get-tuple-element.10), channel_id=1, source_target_pairs={{1,0},{2,1},{3,2},{4,3},{5,4},{6,5},{7,6},{8,7},{9,8},{10,9},{11,1... | collective-permute-start | bytes 417800 | tf_op jit(solution)/shard_map/ppermute | solution.py:116
  43.4 6.1 %copy-start.9 = (bf16[32,32,2048]{2,1,0:T(8,128)(2,1)S(1)}, bf16[32,32,2048]{2,1,0:T(8,128)(2,1)}, u32[]{:S(2)}) copy-start(bf16[32,32,2048]{2,1,0:T(8,128)(2,1)} %copy-done.8) | copy-start | bytes 12582916
  64.1 1.2 collective-permute-start.4
  66.1 24.0 %all-to-all-start = ((f32[64,16,128]{2,1,0:T(8,128)}), f32[64,16,128]{2,1,0:T(8,128)}, u32[]{:S(2)}, u32[]{:S(2)}) async-start(f32[64,16,128]{2,1,0:T(8,128)} %broadcast_in_dim.5), calls=%async_computation | async-start | bytes 1048576 | tf_op jit(solution)/shard_map/all_to_all | solution.py:136
  94.0 6.8 %copy-start.2 = (bf16[512,512]{1,0:T(8,128)(2,1)S(1)}, bf16[512,512]{1,0:T(8,128)(2,1)}, u32[]{:S(2)}) copy-start(bf16[512,512]{1,0:T(8,128)(2,1)} %o.2) | copy-start | bytes 1572868
  94.0 6.8 %copy-start.4 = (f32[512]{0:T(512)S(1)}, f32[512]{0:T(512)}, u32[]{:S(2)}) copy-start(f32[512]{0:T(512)} %param.30) | copy-start | bytes 6148
  94.0 6.8 %copy-start.5 = (f32[512]{0:T(512)S(1)}, f32[512]{0:T(512)}, u32[]{:S(2)}) copy-start(f32[512]{0:T(512)} %param.34) | copy-start | bytes 6148
  123.2 8.3 %copy-start.12 = (bf16[512,512]{1,0:T(8,128)(2,1)S(1)}, bf16[512,512]{1,0:T(8,128)(2,1)}, u32[]{:S(2)}) copy-start(bf16[512,512]{1,0:T(8,128)(2,1)} %get-tuple-element.15) | copy-start | bytes 1572868
  123.2 9.3 %copy-start.11 = (bf16[512,512]{1,0:T(8,128)(2,1)S(1)}, bf16[512,512]{1,0:T(8,128)(2,1)}, u32[]{:S(2)}) copy-start(bf16[512,512]{1,0:T(8,128)(2,1)} %get-tuple-element.13) | copy-start | bytes 1572868
  124.8 21.0 %all-to-all-start.1 = ((bf16[16,64,512]{2,0,1:T(8,128)(2,1)}), bf16[16,64,512]{2,0,1:T(8,128)(2,1)}, u32[]{:S(2)}, u32[]{:S(2)}) async-start(bf16[16,64,512]{2,0,1:T(8,128)(2,1)} %copy.90), calls=%async_computation.1 | async-start | bytes 2097152 | tf_op jit(solution)/shard_map/all_to_all | solution.py:141
  140.2 7.4 %copy-start.3 = (bf16[512,512]{1,0:T(8,128)(2,1)S(1)}, bf16[512,512]{1,0:T(8,128)(2,1)}, u32[]{:S(2)}) copy-start(bf16[512,512]{1,0:T(8,128)(2,1)} %o.3) | copy-start | bytes 1572868
  140.2 7.4 %copy-start.6 = (f32[512]{0:T(512)S(1)}, f32[512]{0:T(512)}, u32[]{:S(2)}) copy-start(f32[512]{0:T(512)} %param.37) | copy-start | bytes 6148
  140.2 7.4 %copy-start.7 = (f32[512]{0:T(512)S(1)}, f32[512]{0:T(512)}, u32[]{:S(2)}) copy-start(f32[512]{0:T(512)} %param.41) | copy-start | bytes 6148
  170.0 27.3 %copy-start.1 = (bf16[512,2048]{1,0:T(8,128)(2,1)S(1)}, bf16[512,2048]{1,0:T(8,128)(2,1)}, u32[]{:S(2)}) copy-start(bf16[512,2048]{1,0:T(8,128)(2,1)} %param.25) | copy-start | bytes 6291460

commit v2 on v1

v2 whole, which is shorter than its diff:
```python
import jax
import jax.numpy as jnp
from jax import lax
from jax.experimental import pallas as pl
from jax.experimental.pallas import tpu as pltpu
from jax.sharding import Mesh, PartitionSpec as P

BF = jnp.bfloat16
F32 = jnp.float32
CELLS = 1024
HALO = 160


def norm(xf, g):
    center = xf - jnp.mean(xf, axis=-1, keepdims=True)
    spread = jnp.mean(center * center, axis=-1, keepdims=True)
    return (center * lax.rsqrt(spread + 1e-05) * g).astype(BF)


def gelu(v):
    half = 0.5 * v
    return half + half * jnp.tanh(v * (0.7978845608028654 + 0.035677408136300125 * (v * v)))


def dot(a, b):
    return jnp.dot(a, b, preferred_element_type=F32)


def dot_nt(a, b):
    return lax.dot_general(a, b, (((1,), (1,)), ((), ())), preferred_element_type=F32)


def dot_tn(a, b):
    return lax.dot_general(a, b, (((0,), (0,)), ((), ())), preferred_element_type=F32)


def swapped(rows, cols):
    size = rows * cols
    to = lax.broadcasted_iota(jnp.int32, (size, size), 0)
    come = lax.broadcasted_iota(jnp.int32, (size, size), 1)
    return (come == (to % rows) * cols + to // rows).astype(F32).astype(BF)


def pieces(v):
    high = v.astype(BF)
    rest = v - high.astype(F32)
    mid = rest.astype(BF)
    return high, mid, (rest - mid.astype(F32)).astype(BF)


def whole(shape):
    return pl.BlockSpec(shape, lambda i: (0,) * len(shape))


def bias_body(block_tab, grid_tab, block_out, grid_out, turned):
    lane = lax.broadcasted_iota(jnp.int32, (256, 128), 1) % 64
    spot = lax.broadcasted_iota(jnp.int32, (256, 128), 0)
    for tab, out, column_major in ((block_tab, block_out, True), (grid_tab, grid_out, False)):
        slow, fast = lane // 8, lane % 8
        row, col = (fast, slow) if column_major else (slow, fast)
        pick = (spot == (row + 7) * 15 + col + 7).astype(F32).astype(BF)
        slow_step, fast_step = (1, 15) if column_major else (15, 1)
        for head in range(16):
            base = jnp.broadcast_to(tab[head:head + 1, :], (8, 256))
            for q in range(8):
                turned[64 * head + 8 * q:64 * head + 8 * q + 8, :] = pltpu.roll(
                    base, slow_step * q, 1, stride=fast_step, stride_axis=0)
        high, mid, low = pieces(turned[...])
        out[...] = (dot(high, pick) + dot(mid, pick) + dot(low, pick)).reshape(16, 64, 128)


def bias_call(block_table, grid_table):
    pad = lambda t: jnp.pad(t, ((0, 0), (0, 256 - t.shape[1])))
    shape = jax.ShapeDtypeStruct((16, 64, 128), F32)
    return pl.pallas_call(
        bias_body,
        grid=(1,),
        in_specs=[whole((16, 256))] * 2,
        out_specs=[whole((16, 64, 128))] * 2,
        out_shape=[shape, shape],
        scratch_shapes=[pltpu.VMEM((1024, 256), F32)],
        compiler_params=pltpu.CompilerParams(vmem_limit_bytes=16 * 2**20),
    )(pad(block_table), pad(grid_table))


def conv_body(flags, latent, above, below, left, right, scale, shift, weight, taps,
              ordered, depthwise, sums, conv_in, field):
    lanes = weight.shape[1]
    blocks = lanes // 128

    @pl.when(pl.program_id(0) == 0)
    def _():
        turn = swapped(8, 32)
        for i in range(4):
            part = dot(turn, latent[8 * i:8 * i + 8].reshape(256, 512))
            ordered[256 * i:256 * i + 256, :] = part.astype(BF)
            conv_in[256 * i:256 * i + 256, :] = (part * scale[...] + shift[...]).astype(BF)
        start = CELLS
        for edge in (above, below, left, right):
            size = edge.shape[0]
            conv_in[start:start + size, :] = (edge[...].astype(F32) * scale[...] + shift[...]).astype(BF)
            start += size

    halo = gelu(dot(conv_in[CELLS:CELLS + HALO, :], weight[...])).astype(BF).astype(F32)
    place = lax.broadcasted_iota(jnp.int32, (48, 1), 0)
    corner = jnp.where(place == 32, flags[0], jnp.where(place == 33, flags[1], 1.0))
    top, bottom = halo[0:32] * flags[0], halo[32:64] * flags[1]
    west, east = halo[64:112] * (corner * flags[2]), halo[112:160] * (corner * flags[3])
    for b in range(blocks):
        cut = slice(128 * b, 128 * b + 128)
        field[b, pl.ds(48 + 7, 32, stride=48), :] = top[:, cut]
        field[b, pl.ds(48 + 40, 32, stride=48), :] = bottom[:, cut]
        for side, at in ((west, 0), (east, 33 * 48)):
            field[b, at + 8:at + 40, :] = side[0:32, cut]
            field[b, at + 7:at + 8, :] = side[32:33, cut]
            field[b, at + 40:at + 41, :] = side[33:34, cut]

    def expand(i, carry):
        rows = pl.ds(pl.multiple_of(i * 256, 256), 256)
        res = gelu(dot(conv_in[rows, :], weight[...])).astype(BF).astype(F32)
        for b in range(blocks):
            for c in range(32):
                field[b, pl.ds(pl.multiple_of(48 * (c + 1) + 8 + 8 * i, 8), 8), :] = (
                    res[8 * c:8 * c + 8, 128 * b:128 * b + 128])
        return carry

    lax.fori_loop(0, 4, expand, 0)

    for b in range(blocks):
        cut = slice(128 * b, 128 * b + 128)
        k = [jnp.broadcast_to(taps[t:t + 1, cut], (8, 128)) for t in range(9)]

        def stencil(i, total):
            def partial(c):
                at = 48 * c + 8 + 8 * i
                up = field[b, pl.ds(at - 1, 8), :]
                mid = field[b, pl.ds(pl.multiple_of(at, 8), 8), :]
                down = field[b, pl.ds(at + 1, 8), :]
                return [k[t] * up + k[3 + t] * mid + k[6 + t] * down for t in range(3)]

            before = partial(0)
            now = partial(1)
            held = None
            for c in range(32):
                after = partial(c + 2)
                value = gelu(before[0] + now[1] + after[2])
                total = total + value
                before, now = now, after
                if c % 2 == 0:
                    held = value
                else:
                    rows = pl.ds(pl.multiple_of(256 * i + 8 * (c - 1), 16), 16)
                    depthwise[rows, cut] = jnp.concatenate([held, value], axis=0).astype(BF)
            return total

        total = lax.fori_loop(0, 4, stencil, jnp.zeros((8, 128), F32))
        sums[:, cut] = jnp.broadcast_to(jnp.sum(total, axis=0, keepdims=True), (8, 128))


def conv_call(flags, latent, above, below, left, right, scale, shift, weight, taps, lanes=512):
    channels, wide = weight.shape
    one = lambda v: v.reshape(1, -1)
    edges = [whole(e.shape) for e in (above, below, left, right)]
    return pl.pallas_call(
        conv_body,
        grid=(wide // lanes,),
        in_specs=[pl.BlockSpec(memory_space=pltpu.SMEM), whole(latent.shape)] + edges + [
            whole((1, channels)), whole((1, channels)),
            pl.BlockSpec((channels, lanes), lambda i: (0, i)),
            pl.BlockSpec((9, lanes), lambda i: (0, i)),
        ],
        out_specs=[
            whole((CELLS, channels)),
            pl.BlockSpec((CELLS, lanes), lambda i: (0, i)),
            pl.BlockSpec((8, lanes), lambda i: (0, i)),
        ],
        out_shape=[
            jax.ShapeDtypeStruct((CELLS, channels), BF),
            jax.ShapeDtypeStruct((CELLS, wide), BF),
            jax.ShapeDtypeStruct((8, wide), F32),
        ],
        scratch_shapes=[
            pltpu.VMEM((CELLS + HALO, channels), BF),
            pltpu.VMEM((lanes // 128, 34 * 48, 128), F32),
        ],
        compiler_params=pltpu.CompilerParams(vmem_limit_bytes=40 * 2**20),
    )(flags, latent, above, below, left, right, one(scale), one(shift), weight, taps)


def attn_ff(x, g1, pk, pqvt, o, bias, g2, u, w, mixt, kbuf, qvt, ff_block=512):
    m = x.shape[0]
    xf = x.astype(F32)
    n = norm(xf, g1[...])
    kbuf[...] = dot(n, pk[...]).astype(BF)
    qvt[...] = dot_nt(pqvt[...], n).astype(BF)
    low = lax.broadcasted_iota(jnp.int32, (64, 128), 1) < 64
    zero = jnp.zeros((32, 128), BF)

    def pair(p, carry):
        lanes = pl.ds(pl.multiple_of(p * 128, 128), 128)
        for g in range(4):
            keys = kbuf[lanes, 128 * g:128 * g + 128]
            q = [qvt[128 * g + 32 * h:128 * g + 32 * h + 32, lanes] for h in range(4)]
            qbd = jnp.concatenate(
                [jnp.concatenate([q[h] if j == h else zero for j in range(4)], axis=0) for h in range(4)],
                axis=1)
            s4 = dot(keys, qbd)
            for h in range(4):
                head = 4 * g + h
                s = s4[:, 128 * h:128 * h + 128]
                s = jnp.where(low, s[:64], s[64:]) * (32 ** -0.5) + bias[head]
                e = jnp.exp(s - jnp.max(s, axis=0, keepdims=True))
                r = 1.0 / jnp.sum(e, axis=0, keepdims=True)
                pbd = jnp.concatenate(
                    [jnp.where(low, e, 0.0).astype(BF), jnp.where(low, 0.0, e).astype(BF)], axis=0)
                vt = qvt[512 + 32 * head:544 + 32 * head, lanes]
                mixt[32 * head:32 * head + 32, lanes] = (dot(vt, pbd) * r).astype(BF)
        return carry

    lax.fori_loop(0, m // 128, pair, 0)
    y = (xf + dot_tn(mixt[...], o[...])).astype(BF)
    yf = y.astype(F32)
    n2 = norm(yf, g2[...])
    acc = yf
    for j in range(u.shape[1] // ff_block):
        cols = slice(j * ff_block, (j + 1) * ff_block)
        hidden = gelu(dot(n2, u[:, cols])).astype(BF)
        acc = acc + dot(hidden, w[cols, :])
    return acc.astype(BF)


def section_body(x, g1, pk, pqvt, o, bias, g2, u, w, out, mixt, kbuf, qvt):
    out[...] = attn_ff(x[...], g1, pk, pqvt, o, bias, g2, u, w, mixt, kbuf, qvt)


def gated_body(copies, down, up, depthwise, ordered, project, g1, pk, pqvt, o, bias, g2, u, w,
               out, mixt, kbuf, qvt, excite):
    @pl.when(pl.program_id(0) == 0)
    def _():
        pooled = jnp.sum(copies[...], axis=0) * (1.0 / (256 * 512))
        parts = pieces(pooled)
        reduced = jnp.zeros((1, down.shape[1]), F32)
        for b in range(pooled.shape[0]):
            for part in parts:
                row = jnp.broadcast_to(part[b:b + 1, :].astype(F32), (16, 128)).astype(BF)
                reduced = reduced + dot(row, down[128 * b:128 * b + 128, :])[0:1]
        reduced = reduced / (1.0 + jnp.exp(-reduced))
        raised = jnp.zeros((1, up.shape[1]), F32)
        for part in pieces(reduced):
            row = jnp.broadcast_to(part.astype(F32), (16, 128)).astype(BF)
            raised = raised + dot(row, up[...])[0:1]
        excite[...] = 1.0 / (1.0 + jnp.exp(-raised))

    acc = ordered[...].astype(F32)
    for j in range(4):
        cols = slice(512 * j, 512 * j + 512)
        gated = (depthwise[:, cols].astype(F32) * excite[:, cols]).astype(BF)
        acc = acc + dot(gated, project[cols, :])
    out[...] = attn_ff(acc.astype(BF), g1, pk, pqvt, o, bias, g2, u, w, mixt, kbuf, qvt)


def scratch(m, feats):
    return [pltpu.VMEM((feats, m), BF), pltpu.VMEM((m, feats), BF), pltpu.VMEM((2 * feats, m), BF)]


def section_call(x, g1, pk, pqvt, o, bias, g2, u, w, m=256):
    cells, feats = x.shape
    args = (g1.reshape(1, -1), pk, pqvt, o, bias, g2.reshape(1, -1), u, w)
    return pl.pallas_call(
        section_body,
        grid=(cells // m,),
        in_specs=[pl.BlockSpec((m, feats), lambda i: (i, 0))] + [whole(a.shape) for a in args],
        out_specs=pl.BlockSpec((m, feats), lambda i: (i, 0)),
        out_shape=jax.ShapeDtypeStruct((cells, feats), BF),
        scratch_shapes=scratch(m, feats),
        compiler_params=pltpu.CompilerParams(vmem_limit_bytes=40 * 2**20),
    )(x, *args)


def gated_call(copies, down, up, depthwise, ordered, project, g1, pk, pqvt, o, bias, g2, u, w, m=256):
    cells, feats = ordered.shape
    args = (project, g1.reshape(1, -1), pk, pqvt, o, bias, g2.reshape(1, -1), u, w)
    return pl.pallas_call(
        gated_body,
        grid=(cells // m,),
        in_specs=[whole(copies.shape), whole(down.shape), whole(up.shape),
                  pl.BlockSpec((m, depthwise.shape[1]), lambda i: (i, 0)),
                  pl.BlockSpec((m, feats), lambda i: (i, 0))] + [whole(a.shape) for a in args],
        out_specs=pl.BlockSpec((m, feats), lambda i: (i, 0)),
        out_shape=jax.ShapeDtypeStruct((cells, feats), BF),
        scratch_shapes=scratch(m, feats) + [pltpu.VMEM((1, depthwise.shape[1]), F32)],
        compiler_params=pltpu.CompilerParams(vmem_limit_bytes=44 * 2**20),
    )(copies, down, up, depthwise, ordered, *args)


def step(cells, axis, count, forward):
    pairs = [(i, i + 1) if forward else (i + 1, i) for i in range(count - 1)]
    return lax.ppermute(cells, axis, pairs)


def channel_copies(sums):
    sums = sums + lax.ppermute(sums, "core", [(0, 1), (1, 0)])
    width = sums.shape[0]
    copies = jnp.broadcast_to(sums.reshape(1, width // 128, 128), (64, width // 128, 128))
    return lax.all_to_all(copies, ("row", "ch"), 0, 0, tiled=True)


def swap(windows):
    return lax.all_to_all(
        windows.reshape(16, 64, -1), ("row", "ch"), split_axis=1, concat_axis=1, tiled=True
    ).reshape(1024, -1)


def per_device(
    latent, conv_scale, conv_shift, expand_weight, depth_kernel, squeeze_down, squeeze_up, project_weight,
    block_gain, block_projection, block_output, block_table, first_gain, first_expand, first_reduce,
    grid_gain, grid_projection, grid_output, grid_table, second_gain, second_expand, second_reduce,
):
    row_count, col_count, channels = latent.shape
    cols = ("ch", "core")
    above = step(latent[-1], "row", 8, True)
    below = step(latent[0], "row", 8, False)
    fill = jnp.zeros((14, channels), BF)
    left = step(jnp.concatenate([latent[:, -1], above[-1:], below[-1:], fill]), cols, 16, True)
    right = step(jnp.concatenate([latent[:, 0], above[:1], below[:1], fill]), cols, 16, False)
    row, col = lax.axis_index("row"), lax.axis_index(cols)
    flags = jnp.stack([row > 0, row < 7, col > 0, col < 15]).astype(F32)
    ordered, depthwise, sums = conv_call(
        flags, latent, above, below, left, right, conv_scale, conv_shift, expand_weight, depth_kernel
    )
    copies = channel_copies(sums[0])

    def split(projection):
        keys = projection[:, channels : 2 * channels]
        others = jnp.concatenate([projection[:, :channels], projection[:, 2 * channels :]], axis=1).T
        return keys, others

    block_bias, grid_bias = bias_call(block_table, grid_table)
    windows = gated_call(
        copies, squeeze_down, squeeze_up, depthwise, ordered, project_weight,
        block_gain, *split(block_projection), block_output, block_bias,
        first_gain, first_expand, first_reduce,
    )
    windows = swap(windows)
    windows = section_call(
        windows, grid_gain, *split(grid_projection), grid_output, grid_bias,
        second_gain, second_expand, second_reduce,
    )
    windows = swap(windows)
    return windows.reshape(4, 32, 8, channels).transpose(0, 2, 1, 3).reshape(row_count, col_count, channels)


def solution(mesh):
    wide = Mesh(mesh.devices.reshape(8, 8, 2), ("row", "ch", "core"))
    field = P("row", ("ch", "core"), None)
    return jax.shard_map(
        per_device, mesh=wide, in_specs=(field,) + (P(),) * 21, out_specs=field, check_vma=False
    )
```

time: 201 us -> 181 us (0.900)
  other arithmetic: 27.5 us -> 2.64 us
  Pallas kernels: 44.8 us -> 65.8 us
  local copies, waits for them, and re-layouts: 45.9 us -> 30.9 us
  matrix products: 14.5 us -> 0 us
  waiting for transfers between devices: 10.8 us -> 24.7 us
    pallas_call x0 -> x3, Pallas kernels: none -> 45.7 us  [the longest x1 26.9 us: gated_call(): pl.pallas_call(gated_body, grid=(cells // m,), in_specs=[whole(copies.sha...]
    pallas_call x2 -> x1, Pallas kernels: 44.8 us -> 20.1 us  [section_call(): pl.pallas_call(section_body, grid=(cells // m,), in_specs=[pl.BlockSpec((...]
    reduce_sum x2 -> x0, other arithmetic: 15.7 us -> none  [the longest x1 14.6 us: per_device(): channel_sums = channel_total(jnp.sum(depthwise, axis=(0, 1)))]
    dot_general x4 -> x0, matrix products: 14.5 us -> none  [the longest x2 11.8 us: dot(): return jnp.dot(a, b, preferred_element_type=F32)]
    all_to_all x1, waiting for transfers between devices: 1.7 us -> 13 us  [swap(): lax.all_to_all(windows.reshape(16, 64, -1), ('row', 'ch'), split_axis=1,...]
    another operation x7 -> x0, local copies, waits for them, and re-layouts: 10.5 us -> none  [the longest x4 9.32 us: bias_table(): both = jnp.stack([rows[..., 7 - q:15 - q] for q in range(8)], axis=2)]
    concatenate x3 -> x1, other arithmetic: 6.5 us -> 0.08 us  [per_device(): jnp.concatenate([latent[:, 0], above[:1], below[:1], fill])]
    ppermute x5, waiting for transfers between devices: 0.97 us -> 6.65 us  [the longest x4 5.48 us: step(): return lax.ppermute(cells, axis, pairs)]
  transfers between devices with their start and end apart: 7 -> 7, of which waited for: 3 -> 5; matrix products, arithmetic and copies ran while one was open for 19% -> 5% of each run, Pallas kernels for 0% -> 1%
where the time goes in v2:
time: 181 us; the launch traced here: 178 us
  Pallas kernels  65.8 us (36%)
  starting transfers between devices  31.6 us (17%)
  local copies, waits for them, and re-layouts  30.9 us (17%)
  waiting for transfers between devices  24.7 us (14%)
  blocking collectives  21.7 us (12%)
  other arithmetic  2.64 us (1%)
    pallas_call x1, Pallas kernels, gated_call(): pl.pallas_call(gated_body, grid=(cells // m,), in_specs=[whole(copies.sha...  26.9 us
    all_to_all x1, blocking collectives, swap(): lax.all_to_all(windows.reshape(16, 64, -1), ('row', 'ch'), split_axis=1,...  21.7 us
    unnamed x60, local copies, waits for them, and re-layouts  20.9 us
    pallas_call x1, Pallas kernels, section_call(): pl.pallas_call(section_body, grid=(cells // m,), in_specs=[pl.BlockSpec((...  20.1 us
    pallas_call x1, Pallas kernels, conv_call(): pl.pallas_call(conv_body, grid=(wide // lanes,), in_specs=[pl.BlockSpec(m...  17.6 us
    all_to_all x1, starting transfers between devices, channel_copies(): return lax.all_to_all(copies, ('row', 'ch'), 0, 0, tiled=True)  13.1 us
    all_to_all x1, waiting for transfers between devices, swap(): lax.all_to_all(windows.reshape(16, 64, -1), ('row', 'ch'), split_axis=1,...  13 us
    ppermute x4, starting transfers between devices, step(): return lax.ppermute(cells, axis, pairs)  12.8 us
  transfers between devices with their start and end apart: 7, of which 5 were waited for; matrix products, arithmetic and copies ran while one was open for 5% of the time, Pallas kernels for 1%

profile of v2, /device:TPU:1, one launch (start us, length us, event | category | flops | bytes accessed | tf_op | source)
XLA Modules:
  0.0 177.5 jit_solution(4775494377001543591)
XLA Ops:
  0.8 4.0 %collective-permute-start = (bf16[32,512]{1,0:T(8,128)(2,1)S(1)}, bf16[32,512]{1,0:T(8,128)(2,1)S(1)}, u32[]{:S(2)}, u32[]{:S(2)}) collective-permute-start(bf16[32,512]{1,0:T(8,128)(2,1)S(1)} %get-tuple-element.24), channel_id=1, source_target_pairs={{0,16},{16,32},{32,48},{48,64},{64,80},{80,96},{96,112},{1,17},{17... | collective-permute-start | bytes 98312 | tf_op jit(solution)/shard_map/ppermute | solution.py:298
  4.8 1.3 collective-permute-start.1
  6.1 1.1 fusion.2
  7.4 2.1 %collective-permute-done.1.below = bf16[32,512]{1,0:T(8,128)(2,1)S(1)} collective-permute-done((bf16[32,512]{1,0:T(8,128)(2,1)S(1)}, bf16[32,512]{1,0:T(8,128)(2,1)S(1)}, u32[]{:S(2)}, u32[]{:S(2)}) %collective-permute-start.1) | collective-permute-done | bytes 32800 | tf_op jit(solution)/shard_map/ppermute | solution.py:298
  9.6 5.5 %collective-permute-start.2 = (bf16[48,512]{1,0:T(8,128)(2,1)S(1)}, bf16[48,512]{1,0:T(8,128)(2,1)S(1)}, u32[]{:S(2)}, u32[]{:S(2)}) collective-permute-start(bf16[48,512]{1,0:T(8,128)(2,1)S(1)} %get-tuple-element.30), channel_id=1, source_target_pairs={{0,1},{1,2},{2,3},{3,4},{4,5},{5,6},{6,7},{7,8},{8,9},{9,10},{10,1... | collective-permute-start | bytes 147464 | tf_op jit(solution)/shard_map/ppermute | solution.py:298
  15.1 1.9 %collective-permute-start.3 = (bf16[48,512]{1,0:T(8,128)(2,1)S(1)}, bf16[48,512]{1,0:T(8,128)(2,1)S(1)}, u32[]{:S(2)}, u32[]{:S(2)}) collective-permute-start(bf16[48,512]{1,0:T(8,128)(2,1)S(1)} %get-tuple-element.29), channel_id=1, source_target_pairs={{1,0},{2,1},{3,2},{4,3},{5,4},{6,5},{7,6},{8,7},{9,8},{10,9},{11,1... | collective-permute-start | bytes 147464 | tf_op jit(solution)/shard_map/ppermute | solution.py:298
  17.1 3.4 %collective-permute-done.3.right = bf16[48,512]{1,0:T(8,128)(2,1)S(1)} collective-permute-done((bf16[48,512]{1,0:T(8,128)(2,1)S(1)}, bf16[48,512]{1,0:T(8,128)(2,1)S(1)}, u32[]{:S(2)}, u32[]{:S(2)}) %collective-permute-start.3) | collective-permute-done | bytes 49184 | tf_op jit(solution)/shard_map/ppermute | solution.py:298
  20.5 1.6 copy-done.2
  22.1 1.2 copy-done.6
  25.6 17.6 %shard_map.208 = (bf16[1024,512]{1,0:T(8,128)(2,1)S(1)}, bf16[1024,2048]{1,0:T(8,128)(2,1)S(1)}, f32[8,2048]{1,0:T(8,128)S(1)}) custom-call(f32[4]{0:T(128)S(1)} %add_convert_fusion.flags, bf16[32,32,512]{2,1,0:T(8,128)(2,1)S(1)} %copy-done.6, bf16[32,512]{1,0:T(8,128)(2,1)S(1)} %collective-permute-done.above, ...), custom_call_target="tpu_custom_call" | custom-call | tf_op jit(solution)/shard_map/pallas_call | solution.py:164
  43.2 1.9 %copy-done = bf16[1024,2048]{1,0:T(8,128)(2,1)} copy-done((bf16[1024,2048]{1,0:T(8,128)(2,1)}, bf16[1024,2048]{1,0:T(8,128)(2,1)S(1)}, u32[]{:S(2)}) %copy-start) | copy-done | bytes 4194328
  46.1 1.2 collective-permute-done.4
  48.1 13.1 %all-to-all-start = ((f32[64,16,128]{2,1,0:T(8,128)}), f32[64,16,128]{2,1,0:T(8,128)}, u32[]{:S(2)}, u32[]{:S(2)}) async-start(f32[64,16,128]{2,1,0:T(8,128)} %broadcast_in_dim.12), calls=%async_computation | async-start | bytes 1048576 | tf_op jit(solution)/shard_map/all_to_all | solution.py:305
  62.2 1.0 copy.62
  64.3 1.3 shard_map.209
  67.2 1.3 maximum_bitcast_fusion.pqvt
  68.4 5.0 %all-to-all-done.copies = f32[64,16,128]{2,1,0:T(8,128)} async-done(((f32[64,16,128]{2,1,0:T(8,128)}), f32[64,16,128]{2,1,0:T(8,128)}, u32[]{:S(2)}, u32[]{:S(2)}) %all-to-all-start) | async-done | bytes 524320 | tf_op jit(solution)/shard_map/all_to_all | solution.py:305
  74.5 1.2 copy-done.8
  75.7 1.0 copy-done.9
  76.7 1.0 copy-done.10
  77.8 1.0 copy-done.11
  78.8 1.0 copy-done.16
  79.9 26.9 %shard_map.210 = bf16[1024,512]{1,0:T(8,128)(2,1)S(1)} custom-call(f32[64,16,128]{2,1,0:T(8,128)} %all-to-all-done.copies, bf16[2048,128]{1,0:T(8,128)(2,1)S(1)} %copy-done.9, bf16[128,2048]{1,0:T(8,128)(2,1)S(1)} %copy-done.10, bf16[1024,2048]{1,0:T(8,128)(2,1)} %copy-done, bf16[1024,512]{1,0:T(8,128)(2,1)S(1)} %copy-done.8, ...), custom_call_target="tpu_custom_call" | custom-call | tf_op jit(solution)/shard_map/pallas_call | solution.py:283
  106.7 1.5 copy.53
  108.3 5.7 %all-to-all-start.1 = ((bf16[16,64,512]{2,0,1:T(8,128)(2,1)}), bf16[16,64,512]{2,0,1:T(8,128)(2,1)}, u32[]{:S(2)}, u32[]{:S(2)}) async-start(bf16[16,64,512]{2,0,1:T(8,128)(2,1)} %copy.53), calls=%async_computation.1 | async-start | bytes 2097152 | tf_op jit(solution)/shard_map/all_to_all | solution.py:309
  115.4 1.2 maximum_bitcast_fusion.1.pqvt
  116.6 13.0 %all-to-all-done.1 = bf16[16,64,512]{2,0,1:T(8,128)(2,1)} async-done(((bf16[16,64,512]{2,0,1:T(8,128)(2,1)}), bf16[16,64,512]{2,0,1:T(8,128)(2,1)}, u32[]{:S(2)}, u32[]{:S(2)}) %all-to-all-start.1) | async-done | bytes 1048608 | tf_op jit(solution)/shard_map/all_to_all | solution.py:309
  129.6 2.0 %copy.54 = bf16[16,64,512]{2,1,0:T(8,128)(2,1)S(1)} copy(bf16[16,64,512]{2,0,1:T(8,128)(2,1)} %all-to-all-done.1) | data formatting | bytes 2097152 | tf_op jit(solution)/shard_map/all_to_all | solution.py:309
  131.7 1.6 copy-done.5
  133.2 20.1 %shard_map.211 = bf16[1024,512]{1,0:T(8,128)(2,1)S(1)} custom-call(bf16[1024,512]{1,0:T(8,128)(2,1)S(1)} %bitcast.33, f32[1,512]{1,0:T(1,128)S(1)} %bitcast.39, bf16[512,512]{1,0:T(8,128)(2,1)S(1)} %get-tuple-element.16.pk, bf16[1024,512]{1,0:T(8,128)(2,1)S(1)} %maximum_bitcast_fusion.1.pqvt, bf16[512,512]{1,0:T(8,128)(2,1)S(1)} %copy-done.12, ...), custom_call_target="tpu_custom_call" | custom-call | tf_op jit(solution)/shard_map/pallas_call | solution.py:269
  154.0 21.7 %all_to_all.15 = bf16[16,64,512]{2,0,1:T(8,128)(2,1)S(1)} all-to-all(bf16[16,64,512]{2,0,1:T(8,128)(2,1)S(1)} %copy.57), channel_id=1, replica_groups=mesh['row'=8,'ch'=8,'core'=2] {'row','ch'}, dimensions={1} | all-to-all | bytes 2097152 | tf_op jit(solution)/shard_map/all_to_all | solution.py:309
  176.2 1.3 copy.59
  (70 shorter events, 12.3 us)
Async XLA Ops:
  0.8 6.6 %collective-permute-start = (bf16[32,512]{1,0:T(8,128)(2,1)S(1)}, bf16[32,512]{1,0:T(8,128)(2,1)S(1)}, u32[]{:S(2)}, u32[]{:S(2)}) collective-permute-start(bf16[32,512]{1,0:T(8,128)(2,1)S(1)} %get-tuple-element.24), channel_id=1, source_target_pairs={{0,16},{16,32},{32,48},{48,64},{64,80},{80,96},{96,112},{1,17},{17... | collective-permute-start | bytes 98312 | tf_op jit(solution)/shard_map/ppermute | solution.py:298
  4.8 4.7 %collective-permute-start.1 = (bf16[32,512]{1,0:T(8,128)(2,1)S(1)}, bf16[32,512]{1,0:T(8,128)(2,1)S(1)}, u32[]{:S(2)}, u32[]{:S(2)}) collective-permute-start(bf16[32,512]{1,0:T(8,128)(2,1)S(1)} %get-tuple-element.23), channel_id=1, source_target_pairs={{16,0},{32,16},{48,32},{64,48},{80,64},{96,80},{112,96},{17,1},{33... | collective-permute-start | bytes 98312 | tf_op jit(solution)/shard_map/ppermute | solution.py:298
  9.6 7.6 %collective-permute-start.2 = (bf16[48,512]{1,0:T(8,128)(2,1)S(1)}, bf16[48,512]{1,0:T(8,128)(2,1)S(1)}, u32[]{:S(2)}, u32[]{:S(2)}) collective-permute-start(bf16[48,512]{1,0:T(8,128)(2,1)S(1)} %get-tuple-element.30), channel_id=1, source_target_pairs={{0,1},{1,2},{2,3},{3,4},{4,5},{5,6},{6,7},{7,8},{8,9},{9,10},{10,1... | collective-permute-start | bytes 147464 | tf_op jit(solution)/shard_map/ppermute | solution.py:298
  15.1 5.4 %collective-permute-start.3 = (bf16[48,512]{1,0:T(8,128)(2,1)S(1)}, bf16[48,512]{1,0:T(8,128)(2,1)S(1)}, u32[]{:S(2)}, u32[]{:S(2)}) collective-permute-start(bf16[48,512]{1,0:T(8,128)(2,1)S(1)} %get-tuple-element.29), channel_id=1, source_target_pairs={{1,0},{2,1},{3,2},{4,3},{5,4},{6,5},{7,6},{8,7},{9,8},{10,9},{11,1... | collective-permute-start | bytes 147464 | tf_op jit(solution)/shard_map/ppermute | solution.py:298
  20.5 1.6 copy-start.2
  22.1 1.2 copy-start.6
  23.3 0.9 copy-start.17
  25.6 35.6 %copy-start.24 = (bf16[512,1536]{1,0:T(8,128)(2,1)S(1)}, bf16[512,1536]{1,0:T(8,128)(2,1)}, u32[]{:S(2)}) copy-start(bf16[512,1536]{1,0:T(8,128)(2,1)} %param.31) | copy-start | bytes 4718596
  43.2 2.0 %copy-start = (bf16[1024,2048]{1,0:T(8,128)(2,1)}, bf16[1024,2048]{1,0:T(8,128)(2,1)S(1)}, u32[]{:S(2)}) copy-start(bf16[1024,2048]{1,0:T(8,128)(2,1)S(1)} %get-tuple-element.11.depthwise) | copy-start | bytes 12582916
  45.1 1.0 copy-start.7
  46.1 1.2 collective-permute-start.4
  48.1 25.3 %all-to-all-start = ((f32[64,16,128]{2,1,0:T(8,128)}), f32[64,16,128]{2,1,0:T(8,128)}, u32[]{:S(2)}, u32[]{:S(2)}) async-start(f32[64,16,128]{2,1,0:T(8,128)} %broadcast_in_dim.12), calls=%async_computation | async-start | bytes 1048576 | tf_op jit(solution)/shard_map/all_to_all | solution.py:305
  61.3 3.0 %copy-start.26 = (f32[16,225]{1,0:T(8,128)S(1)}, f32[16,225]{1,0:T(8,128)}, u32[]{:S(2)}) copy-start(f32[16,225]{1,0:T(8,128)} %param.33) | copy-start | bytes 43204
  61.3 3.0 %copy-start.27 = (f32[16,225]{1,0:T(8,128)S(1)}, f32[16,225]{1,0:T(8,128)}, u32[]{:S(2)}) copy-start(f32[16,225]{1,0:T(8,128)} %param.40) | copy-start | bytes 43204
  62.2 11.2 %copy-start.1 = (bf16[2048,512]{1,0:T(8,128)(2,1)S(1)}, bf16[2048,512]{1,0:T(8,128)(2,1)}, u32[]{:S(2)}) copy-start(bf16[2048,512]{1,0:T(8,128)(2,1)} %project.1) | copy-start | bytes 6291460
  62.2 11.2 %copy-start.18 = (f32[512]{0:T(512)S(1)}, f32[512]{0:T(512)}, u32[]{:S(2)}) copy-start(f32[512]{0:T(512)} %param.30) | copy-start | bytes 6148
  62.2 11.2 %copy-start.19 = (f32[512]{0:T(512)S(1)}, f32[512]{0:T(512)}, u32[]{:S(2)}) copy-start(f32[512]{0:T(512)} %param.34) | copy-start | bytes 6148
  65.6 0.8 copy-start.13
  73.4 1.0 copy-start.3
  74.5 1.2 copy-start.8
  75.7 1.0 copy-start.9
  76.7 1.0 copy-start.10
  77.8 1.0 copy-start.11
  78.8 1.0 copy-start.16
  106.7 7.3 %copy-start.25 = (bf16[512,1536]{1,0:T(8,128)(2,1)S(1)}, bf16[512,1536]{1,0:T(8,128)(2,1)}, u32[]{:S(2)}) copy-start(bf16[512,1536]{1,0:T(8,128)(2,1)} %param.38) | copy-start | bytes 4718596
  108.3 21.3 %all-to-all-start.1 = ((bf16[16,64,512]{2,0,1:T(8,128)(2,1)}), bf16[16,64,512]{2,0,1:T(8,128)(2,1)}, u32[]{:S(2)}, u32[]{:S(2)}) async-start(bf16[16,64,512]{2,0,1:T(8,128)(2,1)} %copy.53), calls=%async_computation.1 | async-start | bytes 2097152 | tf_op jit(solution)/shard_map/all_to_all | solution.py:309
  115.4 16.2 %copy-start.12 = (bf16[512,512]{1,0:T(8,128)(2,1)S(1)}, bf16[512,512]{1,0:T(8,128)(2,1)}, u32[]{:S(2)}) copy-start(bf16[512,512]{1,0:T(8,128)(2,1)} %o.3) | copy-start | bytes 1572868
  115.4 16.2 %copy-start.14 = (f32[16,64,128]{2,1,0:T(8,128)S(1)}, f32[16,64,128]{2,1,0:T(8,128)}, u32[]{:S(2)}) copy-start(f32[16,64,128]{2,1,0:T(8,128)} %copy-done.13) | copy-start | bytes 1572868
  115.4 16.2 %copy-start.22 = (f32[512]{0:T(512)S(1)}, f32[512]{0:T(512)}, u32[]{:S(2)}) copy-start(f32[512]{0:T(512)} %param.37) | copy-start | bytes 6148
  115.4 16.2 %copy-start.23 = (f32[512]{0:T(512)S(1)}, f32[512]{0:T(512)}, u32[]{:S(2)}) copy-start(f32[512]{0:T(512)} %param.41) | copy-start | bytes 6148
  129.6 2.0 %copy-start.4 = (bf16[512,2048]{1,0:T(8,128)(2,1)S(1)}, bf16[512,2048]{1,0:T(8,128)(2,1)}, u32[]{:S(2)}) copy-start(bf16[512,2048]{1,0:T(8,128)(2,1)} %u.3) | copy-start | bytes 6291460
  131.7 1.6 copy-start.5
  (3 other events, 2.2 us)

commit v3 on v2

--- a/solution.py
+++ b/solution.py
@@ -84,7 +84,7 @@
 
 
 def conv_body(flags, latent, above, below, left, right, scale, shift, weight, taps,
-              ordered, depthwise, sums, conv_in, field):
+              ordered, depthwise, sums, conv_in, field, totals):
     lanes = weight.shape[1]
     blocks = lanes // 128
 
@@ -154,7 +154,11 @@
             return total
 
         total = lax.fori_loop(0, 4, stencil, jnp.zeros((8, 128), F32))
-        sums[:, cut] = jnp.broadcast_to(jnp.sum(total, axis=0, keepdims=True), (8, 128))
+        totals[pl.ds(blocks * pl.program_id(0) + b, 1), :] = jnp.sum(total, axis=0, keepdims=True)
+
+    @pl.when(pl.program_id(0) == pl.num_programs(0) - 1)
+    def _():
+        sums[...] = jnp.broadcast_to(totals[...].astype(BF)[None], sums.shape)
 
 
 def conv_call(flags, latent, above, below, left, right, scale, shift, weight, taps, lanes=512):
@@ -172,32 +176,48 @@
         out_specs=[
             whole((CELLS, channels)),
             pl.BlockSpec((CELLS, lanes), lambda i: (0, i)),
-            pl.BlockSpec((8, lanes), lambda i: (0, i)),
+            whole((128, wide // 128, 128)),
         ],
         out_shape=[
             jax.ShapeDtypeStruct((CELLS, channels), BF),
             jax.ShapeDtypeStruct((CELLS, wide), BF),
-            jax.ShapeDtypeStruct((8, wide), F32),
+            jax.ShapeDtypeStruct((128, wide // 128, 128), BF),
         ],
         scratch_shapes=[
             pltpu.VMEM((CELLS + HALO, channels), BF),
             pltpu.VMEM((lanes // 128, 34 * 48, 128), F32),
+            pltpu.VMEM((wide // 128, 128), F32),
         ],
-        compiler_params=pltpu.CompilerParams(vmem_limit_bytes=40 * 2**20),
+        compiler_params=pltpu.CompilerParams(vmem_limit_bytes=60 * 2**20),
     )(flags, latent, above, below, left, right, one(scale), one(shift), weight, taps)
 
 
-def attn_ff(x, g1, pk, pqvt, o, bias, g2, u, w, mixt, kbuf, qvt, ff_block=512):
-    m = x.shape[0]
+class Fetch:
+    def __init__(self, sources, places, sems):
+        self.copies = [pltpu.make_async_copy(s, p, sems.at[k]) for k, (s, p) in enumerate(zip(sources, places))]
+
+    def start(self):
+        for copy in self.copies:
+            copy.start()
+
+    def wait(self, *which):
+        for k in which:
+            self.copies[k].wait()
+
+
+def attn_ff(x, wait, g1, p, pqvt, o, bias, g2, u, w, mixt, kbuf, qvt, ff_block=512):
+    m, feats = x.shape
     xf = x.astype(F32)
     n = norm(xf, g1[...])
-    kbuf[...] = dot(n, pk[...]).astype(BF)
+    wait(0, 1)
+    kbuf[...] = dot(n, p[:, feats:2 * feats]).astype(BF)
     qvt[...] = dot_nt(pqvt[...], n).astype(BF)
     low = lax.broadcasted_iota(jnp.int32, (64, 128), 1) < 64
     zero = jnp.zeros((32, 128), BF)
-
-    def pair(p, carry):
-        lanes = pl.ds(pl.multiple_of(p * 128, 128), 128)
+    wait(2, 3)
+
+    def pair(t, carry):
+        lanes = pl.ds(pl.multiple_of(t * 128, 128), 128)
         for g in range(4):
             keys = kbuf[lanes, 128 * g:128 * g + 128]
             q = [qvt[128 * g + 32 * h:128 * g + 32 * h + 32, lanes] for h in range(4)]
@@ -217,11 +237,12 @@
                 mixt[32 * head:32 * head + 32, lanes] = (dot(vt, pbd) * r).astype(BF)
         return carry
 
-    lax.fori_loop(0, m // 128, pair, 0)
+    lax.fori_loop(0, m // 128, pair, 0, unroll=4)
     y = (xf + dot_tn(mixt[...], o[...])).astype(BF)
     yf = y.astype(F32)
     n2 = norm(yf, g2[...])
     acc = yf
+    wait(4, 5)
     for j in range(u.shape[1] // ff_block):
         cols = slice(j * ff_block, (j + 1) * ff_block)
         hidden = gelu(dot(n2, u[:, cols])).astype(BF)
@@ -229,86 +250,132 @@
     return acc.astype(BF)
 
 
-def section_body(x, g1, pk, pqvt, o, bias, g2, u, w, out, mixt, kbuf, qvt):
-    out[...] = attn_ff(x[...], g1, pk, pqvt, o, bias, g2, u, w, mixt, kbuf, qvt)
-
-
-def gated_body(copies, down, up, depthwise, ordered, project, g1, pk, pqvt, o, bias, g2, u, w,
-               out, mixt, kbuf, qvt, excite):
-    @pl.when(pl.program_id(0) == 0)
-    def _():
-        pooled = jnp.sum(copies[...], axis=0) * (1.0 / (256 * 512))
-        parts = pieces(pooled)
-        reduced = jnp.zeros((1, down.shape[1]), F32)
-        for b in range(pooled.shape[0]):
-            for part in parts:
-                row = jnp.broadcast_to(part[b:b + 1, :].astype(F32), (16, 128)).astype(BF)
-                reduced = reduced + dot(row, down[128 * b:128 * b + 128, :])[0:1]
-        reduced = reduced / (1.0 + jnp.exp(-reduced))
-        raised = jnp.zeros((1, up.shape[1]), F32)
-        for part in pieces(reduced):
-            row = jnp.broadcast_to(part.astype(F32), (16, 128)).astype(BF)
-            raised = raised + dot(row, up[...])[0:1]
-        excite[...] = 1.0 / (1.0 + jnp.exp(-raised))
-
-    acc = ordered[...].astype(F32)
-    for j in range(4):
-        cols = slice(512 * j, 512 * j + 512)
-        gated = (depthwise[:, cols].astype(F32) * excite[:, cols]).astype(BF)
-        acc = acc + dot(gated, project[cols, :])
-    out[...] = attn_ff(acc.astype(BF), g1, pk, pqvt, o, bias, g2, u, w, mixt, kbuf, qvt)
-
-
-def scratch(m, feats):
-    return [pltpu.VMEM((feats, m), BF), pltpu.VMEM((m, feats), BF), pltpu.VMEM((2 * feats, m), BF)]
-
-
-def section_call(x, g1, pk, pqvt, o, bias, g2, u, w, m=256):
-    cells, feats = x.shape
-    args = (g1.reshape(1, -1), pk, pqvt, o, bias, g2.reshape(1, -1), u, w)
+def turn_out(sec, out):
+    def one(q, carry):
+        for b in range(4):
+            out[q, :, 128 * b:128 * b + 128] = sec[b, pl.ds(q, 16, stride=64), :].astype(BF)
+        return carry
+
+    lax.fori_loop(0, 64, one, 0, unroll=4)
+
+
+def turn_in(x, sec):
+    def one(q, carry):
+        for b in range(4):
+            sec[b, pl.ds(q, 16, stride=64), :] = x[q, :, 128 * b:128 * b + 128].astype(F32)
+        return carry
+
+    lax.fori_loop(0, 64, one, 0, unroll=4)
+
+
+def section_body(x, g1, g2, p_h, pqvt_h, o_h, bias_h, u_h, w_h, out,
+                 p, pqvt, o, bias, u, w, mixt, kbuf, qvt, sec, sems):
+    fetch = Fetch((p_h, pqvt_h, o_h, bias_h, u_h, w_h), (p, pqvt, o, bias, u, w), sems)
+    fetch.start()
+    turn_in(x, sec)
+    m = kbuf.shape[0]
+
+    def chunk(i, carry):
+        def wait(*which):
+            @pl.when(i == 0)
+            def _():
+                fetch.wait(*which)
+
+        rows = pl.ds(pl.multiple_of(i * m, m), m)
+        cells = jnp.concatenate([sec[b, rows, :] for b in range(4)], axis=1).astype(BF)
+        res = attn_ff(cells, wait, g1, p, pqvt, o, bias, g2, u, w, mixt, kbuf, qvt).astype(F32)
+        for b in range(4):
+            sec[b, rows, :] = res[:, 128 * b:128 * b + 128]
+        return carry
+
+    lax.fori_loop(0, CELLS // m, chunk, 0)
+    turn_out(sec, out)
+
+
+def gated_body(copies, g1, g2, down_h, up_h, project_h, ordered_h, depthwise_h,
+               p_h, pqvt_h, o_h, bias_h, u_h, w_h, out,
+               down, up, project, ordered, depthwise, p, pqvt, o, bias, u, w,
+               mixt, kbuf, qvt, sec, excite, sems):
+    fetch = Fetch(
+        (down_h, up_h, project_h, ordered_h, depthwise_h, p_h, pqvt_h, o_h, bias_h, u_h, w_h),
+        (down, up, project, ordered, depthwise, p, pqvt, o, bias, u, w), sems)
+    fetch.start()
+    pooled = jnp.sum(copies[...].astype(F32), axis=0) * (1.0 / (256 * 512))
+    parts = pieces(pooled)
+    reduced = jnp.zeros((1, down.shape[1]), F32)
+    fetch.wait(0, 1)
+    for b in range(pooled.shape[0]):
+        row = jnp.concatenate([part[b:b + 1, :].astype(F32) for part in parts] + [jnp.zeros((13, 128), F32)], axis=0)
+        reduced = reduced + jnp.sum(dot(row.astype(BF), down[128 * b:128 * b + 128, :]), axis=0, keepdims=True)
+    reduced = reduced / (1.0 + jnp.exp(-reduced))
+    row = jnp.concatenate([part.astype(F32) for part in pieces(reduced)] + [jnp.zeros((13, 128), F32)], axis=0)
+    raised = jnp.sum(dot(row.astype(BF), up[...]), axis=0, keepdims=True)
+    excite[...] = 1.0 / (1.0 + jnp.exp(-raised))
+    m = kbuf.shape[0]
+    fetch.wait(2, 3, 4)
+
+    def chunk(i, carry):
+        def wait(*which):
+            @pl.when(i == 0)
+            def _():
+                fetch.wait(*[5 + k for k in which])
+
+        rows = pl.ds(pl.multiple_of(i * m, m), m)
+        acc = ordered[rows, :].astype(F32)
+        for j in range(4):
+            cols = slice(512 * j, 512 * j + 512)
+            gated = (depthwise[rows, cols].astype(F32) * excite[:, cols]).astype(BF)
+            acc = acc + dot(gated, project[cols, :])
+        res = attn_ff(acc.astype(BF), wait, g1, p, pqvt, o, bias, g2, u, w, mixt, kbuf, qvt).astype(F32)
+        for b in range(4):
+            sec[b, rows, :] = res[:, 128 * b:128 * b + 128]
+        return carry
+
+    lax.fori_loop(0, CELLS // m, chunk, 0)
+    turn_out(sec, out)
+
+
+HELD = pl.BlockSpec(memory_space=pltpu.HBM)
+
+
+def common_scratch(feats, m):
+    return [pltpu.VMEM((feats, m), BF), pltpu.VMEM((m, feats), BF), pltpu.VMEM((2 * feats, m), BF),
+            pltpu.VMEM((4, CELLS, 128), F32)]
+
+
+def section_call(x, g1, g2, p, pqvt, o, bias, u, w, m=512):
+    feats = x.shape[-1]
+    held = (p, pqvt, o, bias, u, w)
     return pl.pallas_call(
         section_body,
-        grid=(cells // m,),
-        in_specs=[pl.BlockSpec((m, feats), lambda i: (i, 0))] + [whole(a.shape) for a in args],
-        out_specs=pl.BlockSpec((m, feats), lambda i: (i, 0)),
-        out_shape=jax.ShapeDtypeStruct((cells, feats), BF),
-        scratch_shapes=scratch(m, feats),
-        compiler_params=pltpu.CompilerParams(vmem_limit_bytes=40 * 2**20),
-    )(x, *args)
-
-
-def gated_call(copies, down, up, depthwise, ordered, project, g1, pk, pqvt, o, bias, g2, u, w, m=256):
-    cells, feats = ordered.shape
-    args = (project, g1.reshape(1, -1), pk, pqvt, o, bias, g2.reshape(1, -1), u, w)
+        grid=(1,),
+        in_specs=[whole(x.shape)] + [whole((1, feats))] * 2 + [HELD] * len(held),
+        out_specs=whole((64, 16, feats)),
+        out_shape=jax.ShapeDtypeStruct((64, 16, feats), BF),
+        scratch_shapes=[pltpu.VMEM(a.shape, a.dtype) for a in held] + common_scratch(feats, m)
+        + [pltpu.SemaphoreType.DMA((len(held),))],
+        compiler_params=pltpu.CompilerParams(vmem_limit_bytes=60 * 2**20),
+    )(x, g1.reshape(1, -1), g2.reshape(1, -1), *held)
+
+
+def gated_call(copies, g1, g2, down, up, project, ordered, depthwise, p, pqvt, o, bias, u, w, m=512):
+    feats = ordered.shape[-1]
+    held = (down, up, project, ordered, depthwise, p, pqvt, o, bias, u, w)
     return pl.pallas_call(
         gated_body,
-        grid=(cells // m,),
-        in_specs=[whole(copies.shape), whole(down.shape), whole(up.shape),
-                  pl.BlockSpec((m, depthwise.shape[1]), lambda i: (i, 0)),
-                  pl.BlockSpec((m, feats), lambda i: (i, 0))] + [whole(a.shape) for a in args],
-        out_specs=pl.BlockSpec((m, feats), lambda i: (i, 0)),
-        out_shape=jax.ShapeDtypeStruct((cells, feats), BF),
-        scratch_shapes=scratch(m, feats) + [pltpu.VMEM((1, depthwise.shape[1]), F32)],
-        compiler_params=pltpu.CompilerParams(vmem_limit_bytes=44 * 2**20),
-    )(copies, down, up, depthwise, ordered, *args)
+        grid=(1,),
+        in_specs=[whole(copies.shape)] + [whole((1, feats))] * 2 + [HELD] * len(held),
+        out_specs=whole((64, 16, feats)),
+        out_shape=jax.ShapeDtypeStruct((64, 16, feats), BF),
+        scratch_shapes=[pltpu.VMEM(a.shape, a.dtype) for a in held] + common_scratch(feats, m)
+        + [pltpu.VMEM((1, depthwise.shape[1]), F32), pltpu.SemaphoreType.DMA((len(held),))],
+        compiler_params=pltpu.CompilerParams(vmem_limit_bytes=60 * 2**20),
+    )(copies, g1.reshape(1, -1), g2.reshape(1, -1), *held)
 
 
 def step(cells, axis, count, forward):
     pairs = [(i, i + 1) if forward else (i + 1, i) for i in range(count - 1)]
     return lax.ppermute(cells, axis, pairs)
-
-
-def channel_copies(sums):
-    sums = sums + lax.ppermute(sums, "core", [(0, 1), (1, 0)])
-    width = sums.shape[0]
-    copies = jnp.broadcast_to(sums.reshape(1, width // 128, 128), (64, width // 128, 128))
-    return lax.all_to_all(copies, ("row", "ch"), 0, 0, tiled=True)
-
-
-def swap(windows):
-    return lax.all_to_all(
-        windows.reshape(16, 64, -1), ("row", "ch"), split_axis=1, concat_axis=1, tiled=True
-    ).reshape(1024, -1)
 
 
 def per_device(
@@ -325,29 +392,28 @@
     right = step(jnp.concatenate([latent[:, 0], above[:1], below[:1], fill]), cols, 16, False)
     row, col = lax.axis_index("row"), lax.axis_index(cols)
     flags = jnp.stack([row > 0, row < 7, col > 0, col < 15]).astype(F32)
-    ordered, depthwise, sums = conv_call(
+    ordered, depthwise, copies = conv_call(
         flags, latent, above, below, left, right, conv_scale, conv_shift, expand_weight, depth_kernel
     )
-    copies = channel_copies(sums[0])
-
-    def split(projection):
-        keys = projection[:, channels : 2 * channels]
-        others = jnp.concatenate([projection[:, :channels], projection[:, 2 * channels :]], axis=1).T
-        return keys, others
+    copies = lax.all_to_all(copies, ("row", "ch", "core"), 0, 0, tiled=True)
+
+    def outer(projection):
+        return jnp.concatenate([projection[:, :channels], projection[:, 2 * channels :]], axis=1).T
+
+    def swap(windows):
+        return lax.all_to_all(windows, ("row", "ch"), 0, 0, tiled=True)
 
     block_bias, grid_bias = bias_call(block_table, grid_table)
     windows = gated_call(
-        copies, squeeze_down, squeeze_up, depthwise, ordered, project_weight,
-        block_gain, *split(block_projection), block_output, block_bias,
-        first_gain, first_expand, first_reduce,
+        copies, block_gain, first_gain, squeeze_down, squeeze_up, project_weight, ordered, depthwise,
+        block_projection, outer(block_projection), block_output, block_bias, first_expand, first_reduce,
     )
-    windows = swap(windows)
     windows = section_call(
-        windows, grid_gain, *split(grid_projection), grid_output, grid_bias,
-        second_gain, second_expand, second_reduce,
+        swap(windows), grid_gain, second_gain,
+        grid_projection, outer(grid_projection), grid_output, grid_bias, second_expand, second_reduce,
     )
-    windows = swap(windows)
-    return windows.reshape(4, 32, 8, channels).transpose(0, 2, 1, 3).reshape(row_count, col_count, channels)
+    windows = swap(windows).reshape(8, 8, 4, 4, channels)
+    return windows.transpose(2, 1, 3, 0, 4).reshape(row_count, col_count, channels)
 
 
 def solution(mesh):

time: 181 us -> 165 us (0.912)
  local copies, waits for them, and re-layouts: 30.9 us -> 11.2 us
  Pallas kernels: 65.8 us -> 69.5 us
  waiting for transfers between devices: 24.7 us -> 27.6 us
    unnamed x60 -> x28, local copies, waits for them, and re-layouts: 20.9 us -> 6.1 us
    all_to_all x2, waiting for transfers between devices: 18 us -> 22.7 us  [the longest x1 13.7 us: swap(): return lax.all_to_all(windows, ('row', 'ch'), 0, 0, tiled=True)]
    all_to_all x2 -> x0, local copies, waits for them, and re-layouts: 2.53 us -> none  [swap(): lax.all_to_all(windows.reshape(16, 64, -1), ('row', 'ch'), split_axis=1,...]
    pallas_call x1, Pallas kernels: 17.6 us -> 19.8 us  [conv_call(): pl.pallas_call(conv_body, grid=(wide // lanes,), in_specs=[pl.BlockSpec(m...]
    reshape x2 -> x1, local copies, waits for them, and re-layouts: 2.13 us -> 0.27 us  [per_device(): windows = swap(windows).reshape(8, 8, 4, 4, channels)]
  transfers between devices with their start and end apart: 7 -> 6, of which waited for: 5 -> 4; matrix products, arithmetic and copies ran while one was open for 5% -> 4% of each run, Pallas kernels for 1% -> 1%
where the time goes in v3:
time: 165 us; the launch traced here: 162 us
  Pallas kernels  69.5 us (42%)
  starting transfers between devices  29.8 us (18%)
  waiting for transfers between devices  27.6 us (17%)
  blocking collectives  21 us (13%)
  local copies, waits for them, and re-layouts  11.2 us (7%)
  other arithmetic  2.88 us (2%)
    pallas_call x1, Pallas kernels, gated_call(): pl.pallas_call(gated_body, grid=(1,), in_specs=[whole(copies.shape)] + [w...  26.1 us
    pallas_call x1, Pallas kernels, section_call(): pl.pallas_call(section_body, grid=(1,), in_specs=[whole(x.shape)] + [whol...  22.4 us
    all_to_all x1, blocking collectives, swap(): return lax.all_to_all(windows, ('row', 'ch'), 0, 0, tiled=True)  21 us
    pallas_call x1, Pallas kernels, conv_call(): pl.pallas_call(conv_body, grid=(wide // lanes,), in_specs=[pl.BlockSpec(m...  19.8 us
    all_to_all x1, waiting for transfers between devices, swap(): return lax.all_to_all(windows, ('row', 'ch'), 0, 0, tiled=True)  13.7 us
    ppermute x4, starting transfers between devices, step(): return lax.ppermute(cells, axis, pairs)  12.8 us
    all_to_all x1, starting transfers between devices, per_device(): copies = lax.all_to_all(copies, ('row', 'ch', 'core'), 0, 0, tiled=True)  11.8 us
    all_to_all x1, waiting for transfers between devices, per_device(): copies = lax.all_to_all(copies, ('row', 'ch', 'core'), 0, 0, tiled=True)  9.04 us
  transfers between devices with their start and end apart: 6, of which 4 were waited for; matrix products, arithmetic and copies ran while one was open for 4% of the time, Pallas kernels for 1%

profile of v3, /device:TPU:1, one launch (start us, length us, event | category | flops | bytes accessed | tf_op | source)
XLA Modules:
  0.0 162.2 jit_solution(9194971591350084699)
XLA Ops:
  0.0 0.8 slice_bitcast_fusion
  0.8 4.0 %collective-permute-start = (bf16[32,512]{1,0:T(8,128)(2,1)S(1)}, bf16[32,512]{1,0:T(8,128)(2,1)S(1)}, u32[]{:S(2)}, u32[]{:S(2)}) collective-permute-start(bf16[32,512]{1,0:T(8,128)(2,1)S(1)} %get-tuple-element.22), channel_id=1, source_target_pairs={{0,16},{16,32},{32,48},{48,64},{64,80},{80,96},{96,112},{1,17},{17... | collective-permute-start | bytes 98312 | tf_op jit(solution)/shard_map/ppermute | solution.py:378
  4.8 1.3 collective-permute-start.1
  6.1 1.1 fusion.2
  7.4 2.1 %collective-permute-done.1.below = bf16[32,512]{1,0:T(8,128)(2,1)S(1)} collective-permute-done((bf16[32,512]{1,0:T(8,128)(2,1)S(1)}, bf16[32,512]{1,0:T(8,128)(2,1)S(1)}, u32[]{:S(2)}, u32[]{:S(2)}) %collective-permute-start.1) | collective-permute-done | bytes 32800 | tf_op jit(solution)/shard_map/ppermute | solution.py:378
  9.6 5.5 %collective-permute-start.2 = (bf16[48,512]{1,0:T(8,128)(2,1)S(1)}, bf16[48,512]{1,0:T(8,128)(2,1)S(1)}, u32[]{:S(2)}, u32[]{:S(2)}) collective-permute-start(bf16[48,512]{1,0:T(8,128)(2,1)S(1)} %get-tuple-element.28), channel_id=1, source_target_pairs={{0,1},{1,2},{2,3},{3,4},{4,5},{5,6},{6,7},{7,8},{8,9},{9,10},{10,1... | collective-permute-start | bytes 147464 | tf_op jit(solution)/shard_map/ppermute | solution.py:378
  15.1 1.9 %collective-permute-start.3 = (bf16[48,512]{1,0:T(8,128)(2,1)S(1)}, bf16[48,512]{1,0:T(8,128)(2,1)S(1)}, u32[]{:S(2)}, u32[]{:S(2)}) collective-permute-start(bf16[48,512]{1,0:T(8,128)(2,1)S(1)} %get-tuple-element.27), channel_id=1, source_target_pairs={{1,0},{2,1},{3,2},{4,3},{5,4},{6,5},{7,6},{8,7},{9,8},{10,9},{11,1... | collective-permute-start | bytes 147464 | tf_op jit(solution)/shard_map/ppermute | solution.py:378
  17.0 0.7 add_convert_fusion.flags
  17.7 2.8 %collective-permute-done.3.right = bf16[48,512]{1,0:T(8,128)(2,1)S(1)} collective-permute-done((bf16[48,512]{1,0:T(8,128)(2,1)S(1)}, bf16[48,512]{1,0:T(8,128)(2,1)S(1)}, u32[]{:S(2)}, u32[]{:S(2)}) %collective-permute-start.3) | collective-permute-done | bytes 49184 | tf_op jit(solution)/shard_map/ppermute | solution.py:378
  20.5 0.6 copy-done.7
  21.1 19.8 %shard_map.208 = (bf16[1024,512]{1,0:T(8,128)(2,1)}, bf16[1024,2048]{1,0:T(8,128)(2,1)}, bf16[128,16,128]{2,1,0:T(8,128)(2,1)}) custom-call(f32[4]{0:T(128)} %add_convert_fusion.flags, bf16[32,32,512]{2,1,0:T(8,128)(2,1)} %latent.1, bf16[32,512]{1,0:T(8,128)(2,1)} %copy-done.8, bf16[32,512]{1,0:T(8,128)(2,1)} %copy-done.9, bf16[48,512]{1,0:T(8,128)(2,1)} %copy-done.6, ...), custom_call_target="tpu_custom_call" | custom-call | tf_op jit(solution)/shard_map/pallas_call | solution.py:168
  40.9 11.8 %all-to-all-start = ((bf16[128,16,128]{2,1,0:T(8,128)(2,1)}), bf16[128,16,128]{2,1,0:T(8,128)(2,1)S(1)}, u32[]{:S(2)}, u32[]{:S(2)}) async-start(bf16[128,16,128]{2,1,0:T(8,128)(2,1)} %get-tuple-element.10), calls=%async_computation | async-start | bytes 1048576 | tf_op jit(solution)/shard_map/all_to_all | solution.py:398
  52.9 0.2 copy.32
  53.1 0.2 copy.33
  53.5 1.3 shard_map.209
  54.8 0.8 copy-done
  55.6 0.8 copy-done.1
  56.4 1.1 maximum_bitcast_fusion.pqvt_h
  57.5 9.0 %all-to-all-done.copies = bf16[128,16,128]{2,1,0:T(8,128)(2,1)S(1)} async-done(((bf16[128,16,128]{2,1,0:T(8,128)(2,1)}), bf16[128,16,128]{2,1,0:T(8,128)(2,1)S(1)}, u32[]{:S(2)}, u32[]{:S(2)}) %all-to-all-start) | async-done | bytes 524320 | tf_op jit(solution)/shard_map/all_to_all | solution.py:398
  66.5 0.8 copy-done.5
  67.3 26.1 %shard_map.210 = bf16[64,16,512]{2,1,0:T(8,128)(2,1)} custom-call(bf16[128,16,128]{2,1,0:T(8,128)(2,1)} %copy-done.5, f32[1,512]{1,0:T(1,128)} %bitcast.25, f32[1,512]{1,0:T(1,128)} %bitcast.26, bf16[2048,128]{1,0:T(8,128)(2,1)} %down_h.1, bf16[128,2048]{1,0:T(8,128)(2,1)} %up_h.1, bf16[2048,512]{1,0:T(8,128)(2,1)} %project_h.1, ...), custom_call_target="tpu_custom_call" | custom-call | tf_op jit(solution)/shard_map/pallas_call | solution.py:364
  93.4 5.3 %all-to-all-start.1 = ((bf16[64,16,512]{2,1,0:T(8,128)(2,1)}), bf16[64,16,512]{2,1,0:T(8,128)(2,1)S(1)}, u32[]{:S(2)}, u32[]{:S(2)}) async-start(bf16[64,16,512]{2,1,0:T(8,128)(2,1)} %shard_map.210), calls=%async_computation.1 | async-start | bytes 2097152 | tf_op jit(solution)/shard_map/all_to_all | solution.py:404
  98.7 0.9 fusion
  99.6 1.3 copy.34
  100.8 0.2 copy.35
  101.0 1.1 maximum_bitcast_fusion.1.pqvt_h
  102.1 13.7 %all-to-all-done.1.x = bf16[64,16,512]{2,1,0:T(8,128)(2,1)S(1)} async-done(((bf16[64,16,512]{2,1,0:T(8,128)(2,1)}), bf16[64,16,512]{2,1,0:T(8,128)(2,1)S(1)}, u32[]{:S(2)}, u32[]{:S(2)}) %all-to-all-start.1) | async-done | bytes 1048608 | tf_op jit(solution)/shard_map/all_to_all | solution.py:404
  115.8 1.0 copy-done.4
  116.8 22.4 %shard_map.211 = bf16[64,16,512]{2,1,0:T(8,128)(2,1)} custom-call(bf16[64,16,512]{2,1,0:T(8,128)(2,1)} %copy-done.4, f32[1,512]{1,0:T(1,128)} %bitcast.27, f32[1,512]{1,0:T(1,128)} %bitcast.28, bf16[512,1536]{1,0:T(8,128)(2,1)} %p_h.3, bf16[1024,512]{1,0:T(8,128)(2,1)} %maximum_bitcast_fusion.1.pqvt_h, bf16[512,512]{1,0:T(8,128)(2,1)} %o_h.3, ...), custom_call_target="tpu_custom_call" | custom-call | tf_op jit(solution)/shard_map/pallas_call | solution.py:349
  139.1 21.0 %all_to_all.15 = bf16[64,16,512]{2,1,0:T(8,128)(2,1)S(1)} all-to-all(bf16[64,16,512]{2,1,0:T(8,128)(2,1)} %shard_map.211), channel_id=1, replica_groups=mesh['row'=8,'ch'=8,'core'=2] {'row','ch'}, dimensions={0} | all-to-all | bytes 2097152 | tf_op jit(solution)/shard_map/all_to_all | solution.py:404
  160.1 0.3 reshape.30
  160.4 1.8 %copy.29 = bf16[4,8,4,8,512]{4,3,2,1,0:T(8,128)(2,1)} copy(bf16[4,8,4,8,512]{4,2,0,1,3:T(4,128)(2,1)S(1)} %bitcast.24) | data formatting | bytes 2097152 | tf_op jit(solution)/shard_map/transpose | solution.py:416
  (30 shorter events, 0.5 us)
Async XLA Ops:
  0.8 6.6 %collective-permute-start = (bf16[32,512]{1,0:T(8,128)(2,1)S(1)}, bf16[32,512]{1,0:T(8,128)(2,1)S(1)}, u32[]{:S(2)}, u32[]{:S(2)}) collective-permute-start(bf16[32,512]{1,0:T(8,128)(2,1)S(1)} %get-tuple-element.22), channel_id=1, source_target_pairs={{0,16},{16,32},{32,48},{48,64},{64,80},{80,96},{96,112},{1,17},{17... | collective-permute-start | bytes 98312 | tf_op jit(solution)/shard_map/ppermute | solution.py:378
  4.8 4.7 %collective-permute-start.1 = (bf16[32,512]{1,0:T(8,128)(2,1)S(1)}, bf16[32,512]{1,0:T(8,128)(2,1)S(1)}, u32[]{:S(2)}, u32[]{:S(2)}) collective-permute-start(bf16[32,512]{1,0:T(8,128)(2,1)S(1)} %get-tuple-element.21), channel_id=1, source_target_pairs={{16,0},{32,16},{48,32},{64,48},{80,64},{96,80},{112,96},{17,1},{33... | collective-permute-start | bytes 98312 | tf_op jit(solution)/shard_map/ppermute | solution.py:378
  7.4 13.1 %copy-start.8 = (bf16[32,512]{1,0:T(8,128)(2,1)}, bf16[32,512]{1,0:T(8,128)(2,1)S(1)}, u32[]{:S(2)}) copy-start(bf16[32,512]{1,0:T(8,128)(2,1)S(1)} %collective-permute-done.above) | copy-start | bytes 98308
  9.5 11.1 %copy-start.9 = (bf16[32,512]{1,0:T(8,128)(2,1)}, bf16[32,512]{1,0:T(8,128)(2,1)S(1)}, u32[]{:S(2)}) copy-start(bf16[32,512]{1,0:T(8,128)(2,1)S(1)} %collective-permute-done.1.below) | copy-start | bytes 98308
  9.6 8.1 %collective-permute-start.2 = (bf16[48,512]{1,0:T(8,128)(2,1)S(1)}, bf16[48,512]{1,0:T(8,128)(2,1)S(1)}, u32[]{:S(2)}, u32[]{:S(2)}) collective-permute-start(bf16[48,512]{1,0:T(8,128)(2,1)S(1)} %get-tuple-element.28), channel_id=1, source_target_pairs={{0,1},{1,2},{2,3},{3,4},{4,5},{5,6},{6,7},{7,8},{8,9},{9,10},{10,1... | collective-permute-start | bytes 147464 | tf_op jit(solution)/shard_map/ppermute | solution.py:378
  15.1 5.4 %collective-permute-start.3 = (bf16[48,512]{1,0:T(8,128)(2,1)S(1)}, bf16[48,512]{1,0:T(8,128)(2,1)S(1)}, u32[]{:S(2)}, u32[]{:S(2)}) collective-permute-start(bf16[48,512]{1,0:T(8,128)(2,1)S(1)} %get-tuple-element.27), channel_id=1, source_target_pairs={{1,0},{2,1},{3,2},{4,3},{5,4},{6,5},{7,6},{8,7},{9,8},{10,9},{11,1... | collective-permute-start | bytes 147464 | tf_op jit(solution)/shard_map/ppermute | solution.py:378
  17.7 2.8 %copy-start.6 = (bf16[48,512]{1,0:T(8,128)(2,1)}, bf16[48,512]{1,0:T(8,128)(2,1)S(1)}, u32[]{:S(2)}) copy-start(bf16[48,512]{1,0:T(8,128)(2,1)S(1)} %collective-permute-done.2.left) | copy-start | bytes 147460
  20.5 0.6 copy-start.7
  21.1 31.6 %copy-start.2 = (bf16[512,1536]{1,0:T(8,128)(2,1)S(1)}, bf16[512,1536]{1,0:T(8,128)(2,1)}, u32[]{:S(2)}) copy-start(bf16[512,1536]{1,0:T(8,128)(2,1)} %p_h.2) | copy-start | bytes 4718596
  40.9 25.6 %all-to-all-start = ((bf16[128,16,128]{2,1,0:T(8,128)(2,1)}), bf16[128,16,128]{2,1,0:T(8,128)(2,1)S(1)}, u32[]{:S(2)}, u32[]{:S(2)}) async-start(bf16[128,16,128]{2,1,0:T(8,128)(2,1)} %get-tuple-element.10), calls=%async_computation | async-start | bytes 1048576 | tf_op jit(solution)/shard_map/all_to_all | solution.py:398
  52.8 0.7 copy-start.10
  52.8 0.7 copy-start.11
  54.8 0.8 copy-start
  55.6 0.8 copy-start.1
  66.5 0.8 copy-start.5
  93.4 5.3 %copy-start.3 = (bf16[512,1536]{1,0:T(8,128)(2,1)S(1)}, bf16[512,1536]{1,0:T(8,128)(2,1)}, u32[]{:S(2)}) copy-start(bf16[512,1536]{1,0:T(8,128)(2,1)} %p_h.3) | copy-start | bytes 4718596
  93.4 22.4 %all-to-all-start.1 = ((bf16[64,16,512]{2,1,0:T(8,128)(2,1)}), bf16[64,16,512]{2,1,0:T(8,128)(2,1)S(1)}, u32[]{:S(2)}, u32[]{:S(2)}) async-start(bf16[64,16,512]{2,1,0:T(8,128)(2,1)} %shard_map.210), calls=%async_computation.1 | async-start | bytes 2097152 | tf_op jit(solution)/shard_map/all_to_all | solution.py:404
  115.8 1.0 copy-start.4

commit v4 on v3

--- a/solution.py
+++ b/solution.py
@@ -18,8 +18,9 @@
 
 
 def gelu(v):
-    half = 0.5 * v
-    return half + half * jnp.tanh(v * (0.7978845608028654 + 0.035677408136300125 * (v * v)))
+    v = v.astype(BF)
+    half = v * 0.5
+    return half + half * jnp.tanh(v * (v * v * 0.035677408136300125 + 0.7978845608028654))
 
 
 def dot(a, b):
@@ -101,7 +102,7 @@
             conv_in[start:start + size, :] = (edge[...].astype(F32) * scale[...] + shift[...]).astype(BF)
             start += size
 
-    halo = gelu(dot(conv_in[CELLS:CELLS + HALO, :], weight[...])).astype(BF).astype(F32)
+    halo = gelu(dot(conv_in[CELLS:CELLS + HALO, :], weight[...])).astype(F32)
     place = lax.broadcasted_iota(jnp.int32, (48, 1), 0)
     corner = jnp.where(place == 32, flags[0], jnp.where(place == 33, flags[1], 1.0))
     top, bottom = halo[0:32] * flags[0], halo[32:64] * flags[1]
@@ -116,15 +117,17 @@
             field[b, at + 40:at + 41, :] = side[33:34, cut]
 
     def expand(i, carry):
-        rows = pl.ds(pl.multiple_of(i * 256, 256), 256)
-        res = gelu(dot(conv_in[rows, :], weight[...])).astype(BF).astype(F32)
+        rows = pl.ds(pl.multiple_of(i * 512, 512), 512)
+        res = gelu(dot(conv_in[rows, :], weight[...])).astype(F32)
         for b in range(blocks):
-            for c in range(32):
-                field[b, pl.ds(pl.multiple_of(48 * (c + 1) + 8 + 8 * i, 8), 8), :] = (
-                    res[8 * c:8 * c + 8, 128 * b:128 * b + 128])
+            for t in range(2):
+                for c in range(32):
+                    at = 48 * (c + 1) + 8 + 16 * i + 8 * t
+                    field[b, pl.ds(pl.multiple_of(at, 8), 8), :] = (
+                        res[256 * t + 8 * c:256 * t + 8 * c + 8, 128 * b:128 * b + 128])
         return carry
 
-    lax.fori_loop(0, 4, expand, 0)
+    lax.fori_loop(0, 2, expand, 0)
 
     for b in range(blocks):
         cut = slice(128 * b, 128 * b + 128)
@@ -143,14 +146,16 @@
             held = None
             for c in range(32):
                 after = partial(c + 2)
-                value = gelu(before[0] + now[1] + after[2])
-                total = total + value
+                value = before[0] + now[1] + after[2]
                 before, now = now, after
                 if c % 2 == 0:
                     held = value
                 else:
                     rows = pl.ds(pl.multiple_of(256 * i + 8 * (c - 1), 16), 16)
-                    depthwise[rows, cut] = jnp.concatenate([held, value], axis=0).astype(BF)
+                    value = gelu(jnp.concatenate([held, value], axis=0))
+                    depthwise[rows, cut] = value
+                    wide = value.astype(F32)
+                    total = total + (wide[:8] + wide[8:])
             return total
 
         total = lax.fori_loop(0, 4, stencil, jnp.zeros((8, 128), F32))
@@ -245,7 +250,7 @@
     wait(4, 5)
     for j in range(u.shape[1] // ff_block):
         cols = slice(j * ff_block, (j + 1) * ff_block)
-        hidden = gelu(dot(n2, u[:, cols])).astype(BF)
+        hidden = gelu(dot(n2, u[:, cols]))
         acc = acc + dot(hidden, w[cols, :])
     return acc.astype(BF)
 
@@ -260,12 +265,12 @@
 
 
 def turn_in(x, sec):
-    def one(q, carry):
-        for b in range(4):
-            sec[b, pl.ds(q, 16, stride=64), :] = x[q, :, 128 * b:128 * b + 128].astype(F32)
-        return carry
-
-    lax.fori_loop(0, 64, one, 0, unroll=4)
+    to = lax.broadcasted_iota(jnp.int32, (CELLS, CELLS), 0)
+    come = lax.broadcasted_iota(jnp.int32, (CELLS, CELLS), 1)
+    pick = (come == to % 64 * 16 + to // 64).astype(F32).astype(BF)
+    res = dot(pick, x[...].reshape(CELLS, -1))
+    for b in range(4):
+        sec[b] = res[:, 128 * b:128 * b + 128]
 
 
 def section_body(x, g1, g2, p_h, pqvt_h, o_h, bias_h, u_h, w_h, out,
@@ -296,9 +301,12 @@
                p_h, pqvt_h, o_h, bias_h, u_h, w_h, out,
                down, up, project, ordered, depthwise, p, pqvt, o, bias, u, w,
                mixt, kbuf, qvt, sec, excite, sems):
+    m = kbuf.shape[0]
+    one, two = pl.ds(0, m), pl.ds(m, m)
     fetch = Fetch(
-        (down_h, up_h, project_h, ordered_h, depthwise_h, p_h, pqvt_h, o_h, bias_h, u_h, w_h),
-        (down, up, project, ordered, depthwise, p, pqvt, o, bias, u, w), sems)
+        (down_h, up_h, project_h, ordered_h, depthwise_h.at[one], p_h, pqvt_h, o_h, bias_h, u_h, w_h,
+         depthwise_h.at[two]),
+        (down, up, project, ordered, depthwise.at[one], p, pqvt, o, bias, u, w, depthwise.at[two]), sems)
     fetch.start()
     pooled = jnp.sum(copies[...].astype(F32), axis=0) * (1.0 / (256 * 512))
     parts = pieces(pooled)
@@ -311,7 +319,6 @@
     row = jnp.concatenate([part.astype(F32) for part in pieces(reduced)] + [jnp.zeros((13, 128), F32)], axis=0)
     raised = jnp.sum(dot(row.astype(BF), up[...]), axis=0, keepdims=True)
     excite[...] = 1.0 / (1.0 + jnp.exp(-raised))
-    m = kbuf.shape[0]
     fetch.wait(2, 3, 4)
 
     def chunk(i, carry):
@@ -319,6 +326,10 @@
             @pl.when(i == 0)
             def _():
                 fetch.wait(*[5 + k for k in which])
+
+        @pl.when(i == 1)
+        def _():
+            fetch.wait(11)
 
         rows = pl.ds(pl.multiple_of(i * m, m), m)
         acc = ordered[rows, :].astype(F32)
@@ -368,7 +379,7 @@
         out_specs=whole((64, 16, feats)),
         out_shape=jax.ShapeDtypeStruct((64, 16, feats), BF),
         scratch_shapes=[pltpu.VMEM(a.shape, a.dtype) for a in held] + common_scratch(feats, m)
-        + [pltpu.VMEM((1, depthwise.shape[1]), F32), pltpu.SemaphoreType.DMA((len(held),))],
+        + [pltpu.VMEM((1, depthwise.shape[1]), F32), pltpu.SemaphoreType.DMA((len(held) + 1,))],
         compiler_params=pltpu.CompilerParams(vmem_limit_bytes=60 * 2**20),
     )(copies, g1.reshape(1, -1), g2.reshape(1, -1), *held)
 

time: 165 us -> 159 us (0.964)
  Pallas kernels: 69.5 us -> 63.3 us
    pallas_call x1, Pallas kernels: 19.8 us -> 16.7 us  [conv_call(): pl.pallas_call(conv_body, grid=(wide // lanes,), in_specs=[pl.BlockSpec(m...]
where the time goes in v4:
time: 159 us; the launch traced here: 156 us
  Pallas kernels  63.3 us (40%)
  starting transfers between devices  29.7 us (19%)
  waiting for transfers between devices  27.6 us (17%)
  blocking collectives  21 us (13%)
  local copies, waits for them, and re-layouts  11.2 us (7%)
  other arithmetic  2.88 us (2%)
    pallas_call x1, Pallas kernels, gated_call(): pl.pallas_call(gated_body, grid=(1,), in_specs=[whole(copies.shape)] + [w...  24.5 us
    all_to_all x1, blocking collectives, swap(): return lax.all_to_all(windows, ('row', 'ch'), 0, 0, tiled=True)  21 us
    pallas_call x1, Pallas kernels, section_call(): pl.pallas_call(section_body, grid=(1,), in_specs=[whole(x.shape)] + [whol...  20.8 us
    pallas_call x1, Pallas kernels, conv_call(): pl.pallas_call(conv_body, grid=(wide // lanes,), in_specs=[pl.BlockSpec(m...  16.7 us
    all_to_all x1, waiting for transfers between devices, swap(): return lax.all_to_all(windows, ('row', 'ch'), 0, 0, tiled=True)  13.7 us
    ppermute x4, starting transfers between devices, step(): return lax.ppermute(cells, axis, pairs)  12.8 us
    all_to_all x1, starting transfers between devices, per_device(): copies = lax.all_to_all(copies, ('row', 'ch', 'core'), 0, 0, tiled=True)  11.8 us
    all_to_all x1, waiting for transfers between devices, per_device(): copies = lax.all_to_all(copies, ('row', 'ch', 'core'), 0, 0, tiled=True)  9.05 us
  transfers between devices with their start and end apart: 6, of which 4 were waited for; matrix products, arithmetic and copies ran while one was open for 4% of the time, Pallas kernels for 1%

profile of v4, /device:TPU:1, one launch (start us, length us, event | category | flops | bytes accessed | tf_op | source)
XLA Modules:
  0.0 155.9 jit_solution(6865170272424196688)
XLA Ops:
  0.0 0.8 slice_bitcast_fusion
  0.8 4.0 %collective-permute-start = (bf16[32,512]{1,0:T(8,128)(2,1)S(1)}, bf16[32,512]{1,0:T(8,128)(2,1)S(1)}, u32[]{:S(2)}, u32[]{:S(2)}) collective-permute-start(bf16[32,512]{1,0:T(8,128)(2,1)S(1)} %get-tuple-element.22), channel_id=1, source_target_pairs={{0,16},{16,32},{32,48},{48,64},{64,80},{80,96},{96,112},{1,17},{17... | collective-permute-start | bytes 98312 | tf_op jit(solution)/shard_map/ppermute | solution.py:389
  4.8 1.3 collective-permute-start.1
  6.1 1.1 fusion.2
  7.4 2.1 %collective-permute-done.1.below = bf16[32,512]{1,0:T(8,128)(2,1)S(1)} collective-permute-done((bf16[32,512]{1,0:T(8,128)(2,1)S(1)}, bf16[32,512]{1,0:T(8,128)(2,1)S(1)}, u32[]{:S(2)}, u32[]{:S(2)}) %collective-permute-start.1) | collective-permute-done | bytes 32800 | tf_op jit(solution)/shard_map/ppermute | solution.py:389
  9.6 5.5 %collective-permute-start.2 = (bf16[48,512]{1,0:T(8,128)(2,1)S(1)}, bf16[48,512]{1,0:T(8,128)(2,1)S(1)}, u32[]{:S(2)}, u32[]{:S(2)}) collective-permute-start(bf16[48,512]{1,0:T(8,128)(2,1)S(1)} %get-tuple-element.28), channel_id=1, source_target_pairs={{0,1},{1,2},{2,3},{3,4},{4,5},{5,6},{6,7},{7,8},{8,9},{9,10},{10,1... | collective-permute-start | bytes 147464 | tf_op jit(solution)/shard_map/ppermute | solution.py:389
  15.1 1.9 %collective-permute-start.3 = (bf16[48,512]{1,0:T(8,128)(2,1)S(1)}, bf16[48,512]{1,0:T(8,128)(2,1)S(1)}, u32[]{:S(2)}, u32[]{:S(2)}) collective-permute-start(bf16[48,512]{1,0:T(8,128)(2,1)S(1)} %get-tuple-element.27), channel_id=1, source_target_pairs={{1,0},{2,1},{3,2},{4,3},{5,4},{6,5},{7,6},{8,7},{9,8},{10,9},{11,1... | collective-permute-start | bytes 147464 | tf_op jit(solution)/shard_map/ppermute | solution.py:389
  17.0 0.7 add_convert_fusion.flags
  17.7 2.8 %collective-permute-done.3.right = bf16[48,512]{1,0:T(8,128)(2,1)S(1)} collective-permute-done((bf16[48,512]{1,0:T(8,128)(2,1)S(1)}, bf16[48,512]{1,0:T(8,128)(2,1)S(1)}, u32[]{:S(2)}, u32[]{:S(2)}) %collective-permute-start.3) | collective-permute-done | bytes 49184 | tf_op jit(solution)/shard_map/ppermute | solution.py:389
  20.5 0.6 copy-done.7
  21.1 16.7 %shard_map.208 = (bf16[1024,512]{1,0:T(8,128)(2,1)}, bf16[1024,2048]{1,0:T(8,128)(2,1)}, bf16[128,16,128]{2,1,0:T(8,128)(2,1)}) custom-call(f32[4]{0:T(128)} %add_convert_fusion.flags, bf16[32,32,512]{2,1,0:T(8,128)(2,1)} %latent.1, bf16[32,512]{1,0:T(8,128)(2,1)} %copy-done.8, bf16[32,512]{1,0:T(8,128)(2,1)} %copy-done.9, bf16[48,512]{1,0:T(8,128)(2,1)} %copy-done.6, ...), custom_call_target="tpu_custom_call" | custom-call | tf_op jit(solution)/shard_map/pallas_call | solution.py:173
  37.8 11.8 %all-to-all-start = ((bf16[128,16,128]{2,1,0:T(8,128)(2,1)}), bf16[128,16,128]{2,1,0:T(8,128)(2,1)S(1)}, u32[]{:S(2)}, u32[]{:S(2)}) async-start(bf16[128,16,128]{2,1,0:T(8,128)(2,1)} %get-tuple-element.10), calls=%async_computation | async-start | bytes 1048576 | tf_op jit(solution)/shard_map/all_to_all | solution.py:409
  49.8 0.2 copy.32
  50.0 0.2 copy.33
  50.4 1.3 shard_map.209
  51.7 0.8 copy-done
  52.5 0.8 copy-done.1
  53.3 1.1 maximum_bitcast_fusion.pqvt_h
  54.4 9.0 %all-to-all-done.copies = bf16[128,16,128]{2,1,0:T(8,128)(2,1)S(1)} async-done(((bf16[128,16,128]{2,1,0:T(8,128)(2,1)}), bf16[128,16,128]{2,1,0:T(8,128)(2,1)S(1)}, u32[]{:S(2)}, u32[]{:S(2)}) %all-to-all-start) | async-done | bytes 524320 | tf_op jit(solution)/shard_map/all_to_all | solution.py:409
  63.4 0.8 copy-done.5
  64.2 24.5 %shard_map.210 = bf16[64,16,512]{2,1,0:T(8,128)(2,1)} custom-call(bf16[128,16,128]{2,1,0:T(8,128)(2,1)} %copy-done.5, f32[1,512]{1,0:T(1,128)} %bitcast.25, f32[1,512]{1,0:T(1,128)} %bitcast.26, bf16[2048,128]{1,0:T(8,128)(2,1)} %down_h.1, bf16[128,2048]{1,0:T(8,128)(2,1)} %up_h.1, bf16[2048,512]{1,0:T(8,128)(2,1)} %project_h.1, ...), custom_call_target="tpu_custom_call" | custom-call | tf_op jit(solution)/shard_map/pallas_call | solution.py:375
  88.8 5.1 %all-to-all-start.1 = ((bf16[64,16,512]{2,1,0:T(8,128)(2,1)}), bf16[64,16,512]{2,1,0:T(8,128)(2,1)S(1)}, u32[]{:S(2)}, u32[]{:S(2)}) async-start(bf16[64,16,512]{2,1,0:T(8,128)(2,1)} %shard_map.210), calls=%async_computation.1 | async-start | bytes 2097152 | tf_op jit(solution)/shard_map/all_to_all | solution.py:415
  93.9 0.9 fusion
  94.8 1.3 copy.34
  96.0 0.2 copy.35
  96.2 1.1 maximum_bitcast_fusion.1.pqvt_h
  97.3 13.7 %all-to-all-done.1.x = bf16[64,16,512]{2,1,0:T(8,128)(2,1)S(1)} async-done(((bf16[64,16,512]{2,1,0:T(8,128)(2,1)}), bf16[64,16,512]{2,1,0:T(8,128)(2,1)S(1)}, u32[]{:S(2)}, u32[]{:S(2)}) %all-to-all-start.1) | async-done | bytes 1048608 | tf_op jit(solution)/shard_map/all_to_all | solution.py:415
  111.0 1.0 copy-done.4
  112.0 20.8 %shard_map.211 = bf16[64,16,512]{2,1,0:T(8,128)(2,1)} custom-call(bf16[64,16,512]{2,1,0:T(8,128)(2,1)} %copy-done.4, f32[1,512]{1,0:T(1,128)} %bitcast.27, f32[1,512]{1,0:T(1,128)} %bitcast.28, bf16[512,1536]{1,0:T(8,128)(2,1)} %p_h.3, bf16[1024,512]{1,0:T(8,128)(2,1)} %maximum_bitcast_fusion.1.pqvt_h, bf16[512,512]{1,0:T(8,128)(2,1)} %o_h.3, ...), custom_call_target="tpu_custom_call" | custom-call | tf_op jit(solution)/shard_map/pallas_call | solution.py:360
  132.8 21.0 %all_to_all.15 = bf16[64,16,512]{2,1,0:T(8,128)(2,1)S(1)} all-to-all(bf16[64,16,512]{2,1,0:T(8,128)(2,1)} %shard_map.211), channel_id=1, replica_groups=mesh['row'=8,'ch'=8,'core'=2] {'row','ch'}, dimensions={0} | all-to-all | bytes 2097152 | tf_op jit(solution)/shard_map/all_to_all | solution.py:415
  153.7 0.3 reshape.30
  154.0 1.8 %copy.29 = bf16[4,8,4,8,512]{4,3,2,1,0:T(8,128)(2,1)} copy(bf16[4,8,4,8,512]{4,2,0,1,3:T(4,128)(2,1)S(1)} %bitcast.24) | data formatting | bytes 2097152 | tf_op jit(solution)/shard_map/transpose | solution.py:427
  (30 shorter events, 0.5 us)
Async XLA Ops:
  0.8 6.6 %collective-permute-start = (bf16[32,512]{1,0:T(8,128)(2,1)S(1)}, bf16[32,512]{1,0:T(8,128)(2,1)S(1)}, u32[]{:S(2)}, u32[]{:S(2)}) collective-permute-start(bf16[32,512]{1,0:T(8,128)(2,1)S(1)} %get-tuple-element.22), channel_id=1, source_target_pairs={{0,16},{16,32},{32,48},{48,64},{64,80},{80,96},{96,112},{1,17},{17... | collective-permute-start | bytes 98312 | tf_op jit(solution)/shard_map/ppermute | solution.py:389
  4.8 4.7 %collective-permute-start.1 = (bf16[32,512]{1,0:T(8,128)(2,1)S(1)}, bf16[32,512]{1,0:T(8,128)(2,1)S(1)}, u32[]{:S(2)}, u32[]{:S(2)}) collective-permute-start(bf16[32,512]{1,0:T(8,128)(2,1)S(1)} %get-tuple-element.21), channel_id=1, source_target_pairs={{16,0},{32,16},{48,32},{64,48},{80,64},{96,80},{112,96},{17,1},{33... | collective-permute-start | bytes 98312 | tf_op jit(solution)/shard_map/ppermute | solution.py:389
  7.4 13.1 %copy-start.8 = (bf16[32,512]{1,0:T(8,128)(2,1)}, bf16[32,512]{1,0:T(8,128)(2,1)S(1)}, u32[]{:S(2)}) copy-start(bf16[32,512]{1,0:T(8,128)(2,1)S(1)} %collective-permute-done.above) | copy-start | bytes 98308
  9.5 11.1 %copy-start.9 = (bf16[32,512]{1,0:T(8,128)(2,1)}, bf16[32,512]{1,0:T(8,128)(2,1)S(1)}, u32[]{:S(2)}) copy-start(bf16[32,512]{1,0:T(8,128)(2,1)S(1)} %collective-permute-done.1.below) | copy-start | bytes 98308
  9.6 8.1 %collective-permute-start.2 = (bf16[48,512]{1,0:T(8,128)(2,1)S(1)}, bf16[48,512]{1,0:T(8,128)(2,1)S(1)}, u32[]{:S(2)}, u32[]{:S(2)}) collective-permute-start(bf16[48,512]{1,0:T(8,128)(2,1)S(1)} %get-tuple-element.28), channel_id=1, source_target_pairs={{0,1},{1,2},{2,3},{3,4},{4,5},{5,6},{6,7},{7,8},{8,9},{9,10},{10,1... | collective-permute-start | bytes 147464 | tf_op jit(solution)/shard_map/ppermute | solution.py:389
  15.1 5.4 %collective-permute-start.3 = (bf16[48,512]{1,0:T(8,128)(2,1)S(1)}, bf16[48,512]{1,0:T(8,128)(2,1)S(1)}, u32[]{:S(2)}, u32[]{:S(2)}) collective-permute-start(bf16[48,512]{1,0:T(8,128)(2,1)S(1)} %get-tuple-element.27), channel_id=1, source_target_pairs={{1,0},{2,1},{3,2},{4,3},{5,4},{6,5},{7,6},{8,7},{9,8},{10,9},{11,1... | collective-permute-start | bytes 147464 | tf_op jit(solution)/shard_map/ppermute | solution.py:389
  17.7 2.8 %copy-start.6 = (bf16[48,512]{1,0:T(8,128)(2,1)}, bf16[48,512]{1,0:T(8,128)(2,1)S(1)}, u32[]{:S(2)}) copy-start(bf16[48,512]{1,0:T(8,128)(2,1)S(1)} %collective-permute-done.2.left) | copy-start | bytes 147460
  20.5 0.6 copy-start.7
  21.1 28.5 %copy-start.2 = (bf16[512,1536]{1,0:T(8,128)(2,1)S(1)}, bf16[512,1536]{1,0:T(8,128)(2,1)}, u32[]{:S(2)}) copy-start(bf16[512,1536]{1,0:T(8,128)(2,1)} %p_h.2) | copy-start | bytes 4718596
  37.8 25.6 %all-to-all-start = ((bf16[128,16,128]{2,1,0:T(8,128)(2,1)}), bf16[128,16,128]{2,1,0:T(8,128)(2,1)S(1)}, u32[]{:S(2)}, u32[]{:S(2)}) async-start(bf16[128,16,128]{2,1,0:T(8,128)(2,1)} %get-tuple-element.10), calls=%async_computation | async-start | bytes 1048576 | tf_op jit(solution)/shard_map/all_to_all | solution.py:409
  49.7 0.7 copy-start.10
  49.7 0.7 copy-start.11
  51.7 0.8 copy-start
  52.5 0.8 copy-start.1
  63.4 0.8 copy-start.5
  88.8 5.1 %copy-start.3 = (bf16[512,1536]{1,0:T(8,128)(2,1)S(1)}, bf16[512,1536]{1,0:T(8,128)(2,1)}, u32[]{:S(2)}) copy-start(bf16[512,1536]{1,0:T(8,128)(2,1)} %p_h.3) | copy-start | bytes 4718596
  88.8 22.2 %all-to-all-start.1 = ((bf16[64,16,512]{2,1,0:T(8,128)(2,1)}), bf16[64,16,512]{2,1,0:T(8,128)(2,1)S(1)}, u32[]{:S(2)}, u32[]{:S(2)}) async-start(bf16[64,16,512]{2,1,0:T(8,128)(2,1)} %shard_map.210), calls=%async_computation.1 | async-start | bytes 2097152 | tf_op jit(solution)/shard_map/all_to_all | solution.py:415
  111.0 1.0 copy-start.4

commit v5 on v4

--- a/solution.py
+++ b/solution.py
@@ -201,9 +201,9 @@
     def __init__(self, sources, places, sems):
         self.copies = [pltpu.make_async_copy(s, p, sems.at[k]) for k, (s, p) in enumerate(zip(sources, places))]
 
-    def start(self):
-        for copy in self.copies:
-            copy.start()
+    def start(self, *which):
+        for k in which:
+            self.copies[k].start()
 
     def wait(self, *which):
         for k in which:
@@ -255,29 +255,39 @@
     return acc.astype(BF)
 
 
+PITCH = 72
+
+
+def put(sec, first, res):
+    for b in range(4):
+        for t in range(res.shape[0] // 64):
+            rows = pl.ds(pl.multiple_of((first + t) * PITCH, 8), 64)
+            sec[b, rows, :] = res[64 * t:64 * t + 64, 128 * b:128 * b + 128]
+
+
 def turn_out(sec, out):
     def one(q, carry):
         for b in range(4):
-            out[q, :, 128 * b:128 * b + 128] = sec[b, pl.ds(q, 16, stride=64), :].astype(BF)
+            out[q, :, 128 * b:128 * b + 128] = sec[b, pl.ds(q, 16, stride=PITCH), :].astype(BF)
         return carry
 
     lax.fori_loop(0, 64, one, 0, unroll=4)
 
 
-def turn_in(x, sec):
+def turn_in(x, sec, wait):
     to = lax.broadcasted_iota(jnp.int32, (CELLS, CELLS), 0)
     come = lax.broadcasted_iota(jnp.int32, (CELLS, CELLS), 1)
     pick = (come == to % 64 * 16 + to // 64).astype(F32).astype(BF)
+    wait(6)
     res = dot(pick, x[...].reshape(CELLS, -1))
-    for b in range(4):
-        sec[b] = res[:, 128 * b:128 * b + 128]
-
-
-def section_body(x, g1, g2, p_h, pqvt_h, o_h, bias_h, u_h, w_h, out,
-                 p, pqvt, o, bias, u, w, mixt, kbuf, qvt, sec, sems):
-    fetch = Fetch((p_h, pqvt_h, o_h, bias_h, u_h, w_h), (p, pqvt, o, bias, u, w), sems)
-    fetch.start()
-    turn_in(x, sec)
+    put(sec, 0, res)
+
+
+def section_body(x_h, g1, g2, p_h, pqvt_h, o_h, bias_h, u_h, w_h, out,
+                 x, p, pqvt, o, bias, u, w, mixt, kbuf, qvt, sec, sems):
+    fetch = Fetch((p_h, pqvt_h, o_h, bias_h, u_h, w_h, x_h), (p, pqvt, o, bias, u, w, x), sems)
+    fetch.start(6, 0, 1)
+    turn_in(x, sec, fetch.wait)
     m = kbuf.shape[0]
 
     def chunk(i, carry):
@@ -285,33 +295,37 @@
             @pl.when(i == 0)
             def _():
                 fetch.wait(*which)
-
-        rows = pl.ds(pl.multiple_of(i * m, m), m)
-        cells = jnp.concatenate([sec[b, rows, :] for b in range(4)], axis=1).astype(BF)
+                if 1 in which:
+                    fetch.start(2, 3, 4, 5)
+
+        cells = jnp.concatenate(
+            [jnp.concatenate(
+                [sec[b, pl.ds(pl.multiple_of((i * (m // 64) + t) * PITCH, 8), 64), :] for t in range(m // 64)], axis=0)
+             for b in range(4)], axis=1).astype(BF)
         res = attn_ff(cells, wait, g1, p, pqvt, o, bias, g2, u, w, mixt, kbuf, qvt).astype(F32)
-        for b in range(4):
-            sec[b, rows, :] = res[:, 128 * b:128 * b + 128]
+        put(sec, i * (m // 64), res)
         return carry
 
     lax.fori_loop(0, CELLS // m, chunk, 0)
     turn_out(sec, out)
 
 
-def gated_body(copies, g1, g2, down_h, up_h, project_h, ordered_h, depthwise_h,
+def gated_body(copies_h, g1, g2, down_h, up_h, project_h, ordered_h, depthwise_h,
                p_h, pqvt_h, o_h, bias_h, u_h, w_h, out,
-               down, up, project, ordered, depthwise, p, pqvt, o, bias, u, w,
+               copies, down, up, project, ordered, depthwise, p, pqvt, o, bias, u, w,
                mixt, kbuf, qvt, sec, excite, sems):
     m = kbuf.shape[0]
     one, two = pl.ds(0, m), pl.ds(m, m)
     fetch = Fetch(
-        (down_h, up_h, project_h, ordered_h, depthwise_h.at[one], p_h, pqvt_h, o_h, bias_h, u_h, w_h,
+        (copies_h, down_h, up_h, project_h, ordered_h, depthwise_h.at[one], p_h, pqvt_h, o_h, bias_h, u_h, w_h,
          depthwise_h.at[two]),
-        (down, up, project, ordered, depthwise.at[one], p, pqvt, o, bias, u, w, depthwise.at[two]), sems)
-    fetch.start()
+        (copies, down, up, project, ordered, depthwise.at[one], p, pqvt, o, bias, u, w, depthwise.at[two]), sems)
+    fetch.start(0, 1, 2, 3, 4, 5)
+    fetch.wait(0)
     pooled = jnp.sum(copies[...].astype(F32), axis=0) * (1.0 / (256 * 512))
     parts = pieces(pooled)
     reduced = jnp.zeros((1, down.shape[1]), F32)
-    fetch.wait(0, 1)
+    fetch.wait(1, 2)
     for b in range(pooled.shape[0]):
         row = jnp.concatenate([part[b:b + 1, :].astype(F32) for part in parts] + [jnp.zeros((13, 128), F32)], axis=0)
         reduced = reduced + jnp.sum(dot(row.astype(BF), down[128 * b:128 * b + 128, :]), axis=0, keepdims=True)
@@ -319,17 +333,20 @@
     row = jnp.concatenate([part.astype(F32) for part in pieces(reduced)] + [jnp.zeros((13, 128), F32)], axis=0)
     raised = jnp.sum(dot(row.astype(BF), up[...]), axis=0, keepdims=True)
     excite[...] = 1.0 / (1.0 + jnp.exp(-raised))
-    fetch.wait(2, 3, 4)
+    fetch.wait(3, 4, 5)
+    fetch.start(6, 7)
 
     def chunk(i, carry):
         def wait(*which):
             @pl.when(i == 0)
             def _():
-                fetch.wait(*[5 + k for k in which])
+                fetch.wait(*[6 + k for k in which])
+                if 1 in which:
+                    fetch.start(8, 9, 10, 11, 12)
 
         @pl.when(i == 1)
         def _():
-            fetch.wait(11)
+            fetch.wait(12)
 
         rows = pl.ds(pl.multiple_of(i * m, m), m)
         acc = ordered[rows, :].astype(F32)
@@ -338,8 +355,7 @@
             gated = (depthwise[rows, cols].astype(F32) * excite[:, cols]).astype(BF)
             acc = acc + dot(gated, project[cols, :])
         res = attn_ff(acc.astype(BF), wait, g1, p, pqvt, o, bias, g2, u, w, mixt, kbuf, qvt).astype(F32)
-        for b in range(4):
-            sec[b, rows, :] = res[:, 128 * b:128 * b + 128]
+        put(sec, i * (m // 64), res)
         return carry
 
     lax.fori_loop(0, CELLS // m, chunk, 0)
@@ -351,7 +367,7 @@
 
 def common_scratch(feats, m):
     return [pltpu.VMEM((feats, m), BF), pltpu.VMEM((m, feats), BF), pltpu.VMEM((2 * feats, m), BF),
-            pltpu.VMEM((4, CELLS, 128), F32)]
+            pltpu.VMEM((4, 16 * PITCH, 128), F32)]
 
 
 def section_call(x, g1, g2, p, pqvt, o, bias, u, w, m=512):
@@ -360,11 +376,11 @@
     return pl.pallas_call(
         section_body,
         grid=(1,),
-        in_specs=[whole(x.shape)] + [whole((1, feats))] * 2 + [HELD] * len(held),
+        in_specs=[HELD] + [whole((1, feats))] * 2 + [HELD] * len(held),
         out_specs=whole((64, 16, feats)),
         out_shape=jax.ShapeDtypeStruct((64, 16, feats), BF),
-        scratch_shapes=[pltpu.VMEM(a.shape, a.dtype) for a in held] + common_scratch(feats, m)
-        + [pltpu.SemaphoreType.DMA((len(held),))],
+        scratch_shapes=[pltpu.VMEM(a.shape, a.dtype) for a in (x,) + held] + common_scratch(feats, m)
+        + [pltpu.SemaphoreType.DMA((len(held) + 1,))],
         compiler_params=pltpu.CompilerParams(vmem_limit_bytes=60 * 2**20),
     )(x, g1.reshape(1, -1), g2.reshape(1, -1), *held)
 
@@ -375,11 +391,11 @@
     return pl.pallas_call(
         gated_body,
         grid=(1,),
-        in_specs=[whole(copies.shape)] + [whole((1, feats))] * 2 + [HELD] * len(held),
+        in_specs=[HELD] + [whole((1, feats))] * 2 + [HELD] * len(held),
         out_specs=whole((64, 16, feats)),
         out_shape=jax.ShapeDtypeStruct((64, 16, feats), BF),
-        scratch_shapes=[pltpu.VMEM(a.shape, a.dtype) for a in held] + common_scratch(feats, m)
-        + [pltpu.VMEM((1, depthwise.shape[1]), F32), pltpu.SemaphoreType.DMA((len(held) + 1,))],
+        scratch_shapes=[pltpu.VMEM(a.shape, a.dtype) for a in (copies,) + held] + common_scratch(feats, m)
+        + [pltpu.VMEM((1, depthwise.shape[1]), F32), pltpu.SemaphoreType.DMA((len(held) + 2,))],
         compiler_params=pltpu.CompilerParams(vmem_limit_bytes=60 * 2**20),
     )(copies, g1.reshape(1, -1), g2.reshape(1, -1), *held)
 
@@ -421,7 +437,7 @@
     )
     windows = section_call(
         swap(windows), grid_gain, second_gain,
-        grid_projection, outer(grid_projection), grid_output, grid_bias, second_expand, second_reduce,
+        grid_projection, outer(grid_projection), grid_output, grid_bias, second_expand, second_reduce, m=1024,
     )
     windows = swap(windows).reshape(8, 8, 4, 4, channels)
     return windows.transpose(2, 1, 3, 0, 4).reshape(row_count, col_count, channels)

time: 159 us -> 157 us (0.987)
  Pallas kernels: 63.3 us -> 61.5 us
    pallas_call x2, Pallas kernels: 45.3 us -> 43.6 us  [the longest x1 23.7 us: gated_call(): pl.pallas_call(gated_body, grid=(1,), in_specs=[HELD] + [whole((1, feats)...]
where the time goes in v5:
time: 157 us; the launch traced here: 154 us
  Pallas kernels  61.5 us (39%)
  starting transfers between devices  29.7 us (19%)
  waiting for transfers between devices  27.7 us (18%)
  blocking collectives  21 us (13%)
  local copies, waits for them, and re-layouts  11.2 us (7%)
  other arithmetic  2.88 us (2%)
    pallas_call x1, Pallas kernels, gated_call(): pl.pallas_call(gated_body, grid=(1,), in_specs=[HELD] + [whole((1, feats)...  23.7 us
    all_to_all x1, blocking collectives, swap(): return lax.all_to_all(windows, ('row', 'ch'), 0, 0, tiled=True)  21 us
    pallas_call x1, Pallas kernels, section_call(): pl.pallas_call(section_body, grid=(1,), in_specs=[HELD] + [whole((1, feat...  19.9 us
    pallas_call x1, Pallas kernels, conv_call(): pl.pallas_call(conv_body, grid=(wide // lanes,), in_specs=[pl.BlockSpec(m...  16.7 us
    all_to_all x1, waiting for transfers between devices, swap(): return lax.all_to_all(windows, ('row', 'ch'), 0, 0, tiled=True)  13.7 us
    ppermute x4, starting transfers between devices, step(): return lax.ppermute(cells, axis, pairs)  12.8 us
    all_to_all x1, starting transfers between devices, per_device(): copies = lax.all_to_all(copies, ('row', 'ch', 'core'), 0, 0, tiled=True)  11.8 us
    all_to_all x1, waiting for transfers between devices, per_device(): copies = lax.all_to_all(copies, ('row', 'ch', 'core'), 0, 0, tiled=True)  9.05 us
  transfers between devices with their start and end apart: 6, of which 4 were waited for; matrix products, arithmetic and copies ran while one was open for 4% of the time, Pallas kernels for 1%

profile of v5, /device:TPU:1, one launch (start us, length us, event | category | flops | bytes accessed | tf_op | source)
XLA Modules:
  0.0 154.1 jit_solution(4208156663505155194)
XLA Ops:
  0.0 0.8 slice_bitcast_fusion
  0.8 4.0 %collective-permute-start = (bf16[32,512]{1,0:T(8,128)(2,1)S(1)}, bf16[32,512]{1,0:T(8,128)(2,1)S(1)}, u32[]{:S(2)}, u32[]{:S(2)}) collective-permute-start(bf16[32,512]{1,0:T(8,128)(2,1)S(1)} %get-tuple-element.22), channel_id=1, source_target_pairs={{0,16},{16,32},{32,48},{48,64},{64,80},{80,96},{96,112},{1,17},{17... | collective-permute-start | bytes 98312 | tf_op jit(solution)/shard_map/ppermute | solution.py:405
  4.8 1.3 collective-permute-start.1
  6.1 1.1 fusion.2
  7.4 2.1 %collective-permute-done.1.below = bf16[32,512]{1,0:T(8,128)(2,1)S(1)} collective-permute-done((bf16[32,512]{1,0:T(8,128)(2,1)S(1)}, bf16[32,512]{1,0:T(8,128)(2,1)S(1)}, u32[]{:S(2)}, u32[]{:S(2)}) %collective-permute-start.1) | collective-permute-done | bytes 32800 | tf_op jit(solution)/shard_map/ppermute | solution.py:405
  9.6 5.5 %collective-permute-start.2 = (bf16[48,512]{1,0:T(8,128)(2,1)S(1)}, bf16[48,512]{1,0:T(8,128)(2,1)S(1)}, u32[]{:S(2)}, u32[]{:S(2)}) collective-permute-start(bf16[48,512]{1,0:T(8,128)(2,1)S(1)} %get-tuple-element.28), channel_id=1, source_target_pairs={{0,1},{1,2},{2,3},{3,4},{4,5},{5,6},{6,7},{7,8},{8,9},{9,10},{10,1... | collective-permute-start | bytes 147464 | tf_op jit(solution)/shard_map/ppermute | solution.py:405
  15.1 1.9 %collective-permute-start.3 = (bf16[48,512]{1,0:T(8,128)(2,1)S(1)}, bf16[48,512]{1,0:T(8,128)(2,1)S(1)}, u32[]{:S(2)}, u32[]{:S(2)}) collective-permute-start(bf16[48,512]{1,0:T(8,128)(2,1)S(1)} %get-tuple-element.27), channel_id=1, source_target_pairs={{1,0},{2,1},{3,2},{4,3},{5,4},{6,5},{7,6},{8,7},{9,8},{10,9},{11,1... | collective-permute-start | bytes 147464 | tf_op jit(solution)/shard_map/ppermute | solution.py:405
  17.0 0.7 add_convert_fusion.flags
  17.7 2.8 %collective-permute-done.3.right = bf16[48,512]{1,0:T(8,128)(2,1)S(1)} collective-permute-done((bf16[48,512]{1,0:T(8,128)(2,1)S(1)}, bf16[48,512]{1,0:T(8,128)(2,1)S(1)}, u32[]{:S(2)}, u32[]{:S(2)}) %collective-permute-start.3) | collective-permute-done | bytes 49184 | tf_op jit(solution)/shard_map/ppermute | solution.py:405
  20.5 0.6 copy-done.7
  21.1 16.7 %shard_map.208 = (bf16[1024,512]{1,0:T(8,128)(2,1)}, bf16[1024,2048]{1,0:T(8,128)(2,1)}, bf16[128,16,128]{2,1,0:T(8,128)(2,1)}) custom-call(f32[4]{0:T(128)} %add_convert_fusion.flags, bf16[32,32,512]{2,1,0:T(8,128)(2,1)} %latent.1, bf16[32,512]{1,0:T(8,128)(2,1)} %copy-done.8, bf16[32,512]{1,0:T(8,128)(2,1)} %copy-done.9, bf16[48,512]{1,0:T(8,128)(2,1)} %copy-done.6, ...), custom_call_target="tpu_custom_call" | custom-call | tf_op jit(solution)/shard_map/pallas_call | solution.py:173
  37.8 11.8 %all-to-all-start = ((bf16[128,16,128]{2,1,0:T(8,128)(2,1)}), bf16[128,16,128]{2,1,0:T(8,128)(2,1)S(1)}, u32[]{:S(2)}, u32[]{:S(2)}) async-start(bf16[128,16,128]{2,1,0:T(8,128)(2,1)} %get-tuple-element.10), calls=%async_computation | async-start | bytes 1048576 | tf_op jit(solution)/shard_map/all_to_all | solution.py:425
  49.8 0.2 copy.32
  50.0 0.2 copy.33
  50.4 1.3 shard_map.209
  51.7 0.8 copy-done
  52.5 0.8 copy-done.1
  53.3 1.1 maximum_bitcast_fusion.pqvt_h
  54.4 9.0 %all-to-all-done.copies_h = bf16[128,16,128]{2,1,0:T(8,128)(2,1)S(1)} async-done(((bf16[128,16,128]{2,1,0:T(8,128)(2,1)}), bf16[128,16,128]{2,1,0:T(8,128)(2,1)S(1)}, u32[]{:S(2)}, u32[]{:S(2)}) %all-to-all-start) | async-done | bytes 524320 | tf_op jit(solution)/shard_map/all_to_all | solution.py:425
  63.4 0.8 copy-done.5
  64.2 23.7 %shard_map.210 = bf16[64,16,512]{2,1,0:T(8,128)(2,1)} custom-call(bf16[128,16,128]{2,1,0:T(8,128)(2,1)} %copy-done.5, f32[1,512]{1,0:T(1,128)} %bitcast.25, f32[1,512]{1,0:T(1,128)} %bitcast.26, bf16[2048,128]{1,0:T(8,128)(2,1)} %down_h.1, bf16[128,2048]{1,0:T(8,128)(2,1)} %up_h.1, bf16[2048,512]{1,0:T(8,128)(2,1)} %project_h.1, ...), custom_call_target="tpu_custom_call" | custom-call | tf_op jit(solution)/shard_map/pallas_call | solution.py:391
  88.0 5.1 %all-to-all-start.1 = ((bf16[64,16,512]{2,1,0:T(8,128)(2,1)}), bf16[64,16,512]{2,1,0:T(8,128)(2,1)S(1)}, u32[]{:S(2)}, u32[]{:S(2)}) async-start(bf16[64,16,512]{2,1,0:T(8,128)(2,1)} %shard_map.210), calls=%async_computation.1 | async-start | bytes 2097152 | tf_op jit(solution)/shard_map/all_to_all | solution.py:431
  93.1 0.9 fusion
  93.9 1.3 copy.34
  95.2 0.2 copy.35
  95.4 1.1 maximum_bitcast_fusion.1.pqvt_h
  96.4 13.7 %all-to-all-done.1.x_h = bf16[64,16,512]{2,1,0:T(8,128)(2,1)S(1)} async-done(((bf16[64,16,512]{2,1,0:T(8,128)(2,1)}), bf16[64,16,512]{2,1,0:T(8,128)(2,1)S(1)}, u32[]{:S(2)}, u32[]{:S(2)}) %all-to-all-start.1) | async-done | bytes 1048608 | tf_op jit(solution)/shard_map/all_to_all | solution.py:431
  110.2 1.0 copy-done.4
  111.1 19.9 %shard_map.211 = bf16[64,16,512]{2,1,0:T(8,128)(2,1)} custom-call(bf16[64,16,512]{2,1,0:T(8,128)(2,1)} %copy-done.4, f32[1,512]{1,0:T(1,128)} %bitcast.27, f32[1,512]{1,0:T(1,128)} %bitcast.28, bf16[512,1536]{1,0:T(8,128)(2,1)} %p_h.3, bf16[1024,512]{1,0:T(8,128)(2,1)} %maximum_bitcast_fusion.1.pqvt_h, bf16[512,512]{1,0:T(8,128)(2,1)} %o_h.3, ...), custom_call_target="tpu_custom_call" | custom-call | tf_op jit(solution)/shard_map/pallas_call | solution.py:376
  131.0 21.0 %all_to_all.15 = bf16[64,16,512]{2,1,0:T(8,128)(2,1)S(1)} all-to-all(bf16[64,16,512]{2,1,0:T(8,128)(2,1)} %shard_map.211), channel_id=1, replica_groups=mesh['row'=8,'ch'=8,'core'=2] {'row','ch'}, dimensions={0} | all-to-all | bytes 2097152 | tf_op jit(solution)/shard_map/all_to_all | solution.py:431
  152.0 0.3 reshape.30
  152.3 1.8 %copy.29 = bf16[4,8,4,8,512]{4,3,2,1,0:T(8,128)(2,1)} copy(bf16[4,8,4,8,512]{4,2,0,1,3:T(4,128)(2,1)S(1)} %bitcast.24) | data formatting | bytes 2097152 | tf_op jit(solution)/shard_map/transpose | solution.py:443
  (30 shorter events, 0.5 us)
Async XLA Ops:
  0.8 6.6 %collective-permute-start = (bf16[32,512]{1,0:T(8,128)(2,1)S(1)}, bf16[32,512]{1,0:T(8,128)(2,1)S(1)}, u32[]{:S(2)}, u32[]{:S(2)}) collective-permute-start(bf16[32,512]{1,0:T(8,128)(2,1)S(1)} %get-tuple-element.22), channel_id=1, source_target_pairs={{0,16},{16,32},{32,48},{48,64},{64,80},{80,96},{96,112},{1,17},{17... | collective-permute-start | bytes 98312 | tf_op jit(solution)/shard_map/ppermute | solution.py:405
  4.8 4.7 %collective-permute-start.1 = (bf16[32,512]{1,0:T(8,128)(2,1)S(1)}, bf16[32,512]{1,0:T(8,128)(2,1)S(1)}, u32[]{:S(2)}, u32[]{:S(2)}) collective-permute-start(bf16[32,512]{1,0:T(8,128)(2,1)S(1)} %get-tuple-element.21), channel_id=1, source_target_pairs={{16,0},{32,16},{48,32},{64,48},{80,64},{96,80},{112,96},{17,1},{33... | collective-permute-start | bytes 98312 | tf_op jit(solution)/shard_map/ppermute | solution.py:405
  7.4 13.1 %copy-start.8 = (bf16[32,512]{1,0:T(8,128)(2,1)}, bf16[32,512]{1,0:T(8,128)(2,1)S(1)}, u32[]{:S(2)}) copy-start(bf16[32,512]{1,0:T(8,128)(2,1)S(1)} %collective-permute-done.above) | copy-start | bytes 98308
  9.5 11.1 %copy-start.9 = (bf16[32,512]{1,0:T(8,128)(2,1)}, bf16[32,512]{1,0:T(8,128)(2,1)S(1)}, u32[]{:S(2)}) copy-start(bf16[32,512]{1,0:T(8,128)(2,1)S(1)} %collective-permute-done.1.below) | copy-start | bytes 98308
  9.6 8.1 %collective-permute-start.2 = (bf16[48,512]{1,0:T(8,128)(2,1)S(1)}, bf16[48,512]{1,0:T(8,128)(2,1)S(1)}, u32[]{:S(2)}, u32[]{:S(2)}) collective-permute-start(bf16[48,512]{1,0:T(8,128)(2,1)S(1)} %get-tuple-element.28), channel_id=1, source_target_pairs={{0,1},{1,2},{2,3},{3,4},{4,5},{5,6},{6,7},{7,8},{8,9},{9,10},{10,1... | collective-permute-start | bytes 147464 | tf_op jit(solution)/shard_map/ppermute | solution.py:405
  15.1 5.4 %collective-permute-start.3 = (bf16[48,512]{1,0:T(8,128)(2,1)S(1)}, bf16[48,512]{1,0:T(8,128)(2,1)S(1)}, u32[]{:S(2)}, u32[]{:S(2)}) collective-permute-start(bf16[48,512]{1,0:T(8,128)(2,1)S(1)} %get-tuple-element.27), channel_id=1, source_target_pairs={{1,0},{2,1},{3,2},{4,3},{5,4},{6,5},{7,6},{8,7},{9,8},{10,9},{11,1... | collective-permute-start | bytes 147464 | tf_op jit(solution)/shard_map/ppermute | solution.py:405
  17.7 2.8 %copy-start.6 = (bf16[48,512]{1,0:T(8,128)(2,1)}, bf16[48,512]{1,0:T(8,128)(2,1)S(1)}, u32[]{:S(2)}) copy-start(bf16[48,512]{1,0:T(8,128)(2,1)S(1)} %collective-permute-done.2.left) | copy-start | bytes 147460
  20.5 0.6 copy-start.7
  21.1 28.5 %copy-start.2 = (bf16[512,1536]{1,0:T(8,128)(2,1)S(1)}, bf16[512,1536]{1,0:T(8,128)(2,1)}, u32[]{:S(2)}) copy-start(bf16[512,1536]{1,0:T(8,128)(2,1)} %p_h.2) | copy-start | bytes 4718596
  37.8 25.6 %all-to-all-start = ((bf16[128,16,128]{2,1,0:T(8,128)(2,1)}), bf16[128,16,128]{2,1,0:T(8,128)(2,1)S(1)}, u32[]{:S(2)}, u32[]{:S(2)}) async-start(bf16[128,16,128]{2,1,0:T(8,128)(2,1)} %get-tuple-element.10), calls=%async_computation | async-start | bytes 1048576 | tf_op jit(solution)/shard_map/all_to_all | solution.py:425
  49.7 0.7 copy-start.10
  49.7 0.7 copy-start.11
  51.7 0.8 copy-start
  52.5 0.8 copy-start.1
  63.4 0.8 copy-start.5
  87.9 5.1 %copy-start.3 = (bf16[512,1536]{1,0:T(8,128)(2,1)S(1)}, bf16[512,1536]{1,0:T(8,128)(2,1)}, u32[]{:S(2)}) copy-start(bf16[512,1536]{1,0:T(8,128)(2,1)} %p_h.3) | copy-start | bytes 4718596
  88.0 22.2 %all-to-all-start.1 = ((bf16[64,16,512]{2,1,0:T(8,128)(2,1)}), bf16[64,16,512]{2,1,0:T(8,128)(2,1)S(1)}, u32[]{:S(2)}, u32[]{:S(2)}) async-start(bf16[64,16,512]{2,1,0:T(8,128)(2,1)} %shard_map.210), calls=%async_computation.1 | async-start | bytes 2097152 | tf_op jit(solution)/shard_map/all_to_all | solution.py:431
  110.2 1.0 copy-start.4

commit v6 on v5

--- a/solution.py
+++ b/solution.py
@@ -352,7 +352,7 @@
         acc = ordered[rows, :].astype(F32)
         for j in range(4):
             cols = slice(512 * j, 512 * j + 512)
-            gated = (depthwise[rows, cols].astype(F32) * excite[:, cols]).astype(BF)
+            gated = depthwise[rows, cols] * excite[:, cols].astype(BF)
             acc = acc + dot(gated, project[cols, :])
         res = attn_ff(acc.astype(BF), wait, g1, p, pqvt, o, bias, g2, u, w, mixt, kbuf, qvt).astype(F32)
         put(sec, i * (m // 64), res)

time: 157 us -> 157 us (level)
  no operation moved by 1% of the time
where the time goes in v6:
time: 157 us; the launch traced here: 154 us
  Pallas kernels  61.5 us (39%)
  starting transfers between devices  29.7 us (19%)
  waiting for transfers between devices  27.7 us (18%)
  blocking collectives  21 us (13%)
  local copies, waits for them, and re-layouts  11.2 us (7%)
  other arithmetic  2.88 us (2%)
    pallas_call x1, Pallas kernels, gated_call(): pl.pallas_call(gated_body, grid=(1,), in_specs=[HELD] + [whole((1, feats)...  23.7 us
    all_to_all x1, blocking collectives, swap(): return lax.all_to_all(windows, ('row', 'ch'), 0, 0, tiled=True)  21 us
    pallas_call x1, Pallas kernels, section_call(): pl.pallas_call(section_body, grid=(1,), in_specs=[HELD] + [whole((1, feat...  19.9 us
    pallas_call x1, Pallas kernels, conv_call(): pl.pallas_call(conv_body, grid=(wide // lanes,), in_specs=[pl.BlockSpec(m...  16.7 us
    all_to_all x1, waiting for transfers between devices, swap(): return lax.all_to_all(windows, ('row', 'ch'), 0, 0, tiled=True)  13.7 us
    ppermute x4, starting transfers between devices, step(): return lax.ppermute(cells, axis, pairs)  12.8 us
    all_to_all x1, starting transfers between devices, per_device(): copies = lax.all_to_all(copies, ('row', 'ch', 'core'), 0, 0, tiled=True)  11.8 us
    all_to_all x1, waiting for transfers between devices, per_device(): copies = lax.all_to_all(copies, ('row', 'ch', 'core'), 0, 0, tiled=True)  9.05 us
  transfers between devices with their start and end apart: 6, of which 4 were waited for; matrix products, arithmetic and copies ran while one was open for 4% of the time, Pallas kernels for 1%

profile of v6, /device:TPU:1, one launch (start us, length us, event | category | flops | bytes accessed | tf_op | source)
XLA Modules:
  0.0 154.1 jit_solution(10169920877102438653)
XLA Ops:
  0.0 0.8 slice_bitcast_fusion
  0.8 4.0 %collective-permute-start = (bf16[32,512]{1,0:T(8,128)(2,1)S(1)}, bf16[32,512]{1,0:T(8,128)(2,1)S(1)}, u32[]{:S(2)}, u32[]{:S(2)}) collective-permute-start(bf16[32,512]{1,0:T(8,128)(2,1)S(1)} %get-tuple-element.22), channel_id=1, source_target_pairs={{0,16},{16,32},{32,48},{48,64},{64,80},{80,96},{96,112},{1,17},{17... | collective-permute-start | bytes 98312 | tf_op jit(solution)/shard_map/ppermute | solution.py:405
  4.8 1.3 collective-permute-start.1
  6.1 1.1 fusion.2
  7.4 2.1 %collective-permute-done.1.below = bf16[32,512]{1,0:T(8,128)(2,1)S(1)} collective-permute-done((bf16[32,512]{1,0:T(8,128)(2,1)S(1)}, bf16[32,512]{1,0:T(8,128)(2,1)S(1)}, u32[]{:S(2)}, u32[]{:S(2)}) %collective-permute-start.1) | collective-permute-done | bytes 32800 | tf_op jit(solution)/shard_map/ppermute | solution.py:405
  9.6 5.5 %collective-permute-start.2 = (bf16[48,512]{1,0:T(8,128)(2,1)S(1)}, bf16[48,512]{1,0:T(8,128)(2,1)S(1)}, u32[]{:S(2)}, u32[]{:S(2)}) collective-permute-start(bf16[48,512]{1,0:T(8,128)(2,1)S(1)} %get-tuple-element.28), channel_id=1, source_target_pairs={{0,1},{1,2},{2,3},{3,4},{4,5},{5,6},{6,7},{7,8},{8,9},{9,10},{10,1... | collective-permute-start | bytes 147464 | tf_op jit(solution)/shard_map/ppermute | solution.py:405
  15.1 1.9 %collective-permute-start.3 = (bf16[48,512]{1,0:T(8,128)(2,1)S(1)}, bf16[48,512]{1,0:T(8,128)(2,1)S(1)}, u32[]{:S(2)}, u32[]{:S(2)}) collective-permute-start(bf16[48,512]{1,0:T(8,128)(2,1)S(1)} %get-tuple-element.27), channel_id=1, source_target_pairs={{1,0},{2,1},{3,2},{4,3},{5,4},{6,5},{7,6},{8,7},{9,8},{10,9},{11,1... | collective-permute-start | bytes 147464 | tf_op jit(solution)/shard_map/ppermute | solution.py:405
  17.0 0.7 add_convert_fusion.flags
  17.7 2.8 %collective-permute-done.3.right = bf16[48,512]{1,0:T(8,128)(2,1)S(1)} collective-permute-done((bf16[48,512]{1,0:T(8,128)(2,1)S(1)}, bf16[48,512]{1,0:T(8,128)(2,1)S(1)}, u32[]{:S(2)}, u32[]{:S(2)}) %collective-permute-start.3) | collective-permute-done | bytes 49184 | tf_op jit(solution)/shard_map/ppermute | solution.py:405
  20.5 0.6 copy-done.7
  21.1 16.7 %shard_map.208 = (bf16[1024,512]{1,0:T(8,128)(2,1)}, bf16[1024,2048]{1,0:T(8,128)(2,1)}, bf16[128,16,128]{2,1,0:T(8,128)(2,1)}) custom-call(f32[4]{0:T(128)} %add_convert_fusion.flags, bf16[32,32,512]{2,1,0:T(8,128)(2,1)} %latent.1, bf16[32,512]{1,0:T(8,128)(2,1)} %copy-done.8, bf16[32,512]{1,0:T(8,128)(2,1)} %copy-done.9, bf16[48,512]{1,0:T(8,128)(2,1)} %copy-done.6, ...), custom_call_target="tpu_custom_call" | custom-call | tf_op jit(solution)/shard_map/pallas_call | solution.py:173
  37.8 11.8 %all-to-all-start = ((bf16[128,16,128]{2,1,0:T(8,128)(2,1)}), bf16[128,16,128]{2,1,0:T(8,128)(2,1)S(1)}, u32[]{:S(2)}, u32[]{:S(2)}) async-start(bf16[128,16,128]{2,1,0:T(8,128)(2,1)} %get-tuple-element.10), calls=%async_computation | async-start | bytes 1048576 | tf_op jit(solution)/shard_map/all_to_all | solution.py:425
  49.8 0.2 copy.32
  50.0 0.2 copy.33
  50.4 1.3 shard_map.209
  51.7 0.8 copy-done
  52.5 0.8 copy-done.1
  53.3 1.1 maximum_bitcast_fusion.pqvt_h
  54.4 9.0 %all-to-all-done.copies_h = bf16[128,16,128]{2,1,0:T(8,128)(2,1)S(1)} async-done(((bf16[128,16,128]{2,1,0:T(8,128)(2,1)}), bf16[128,16,128]{2,1,0:T(8,128)(2,1)S(1)}, u32[]{:S(2)}, u32[]{:S(2)}) %all-to-all-start) | async-done | bytes 524320 | tf_op jit(solution)/shard_map/all_to_all | solution.py:425
  63.4 0.8 copy-done.5
  64.2 23.7 %shard_map.210 = bf16[64,16,512]{2,1,0:T(8,128)(2,1)} custom-call(bf16[128,16,128]{2,1,0:T(8,128)(2,1)} %copy-done.5, f32[1,512]{1,0:T(1,128)} %bitcast.25, f32[1,512]{1,0:T(1,128)} %bitcast.26, bf16[2048,128]{1,0:T(8,128)(2,1)} %down_h.1, bf16[128,2048]{1,0:T(8,128)(2,1)} %up_h.1, bf16[2048,512]{1,0:T(8,128)(2,1)} %project_h.1, ...), custom_call_target="tpu_custom_call" | custom-call | tf_op jit(solution)/shard_map/pallas_call | solution.py:391
  87.9 5.1 %all-to-all-start.1 = ((bf16[64,16,512]{2,1,0:T(8,128)(2,1)}), bf16[64,16,512]{2,1,0:T(8,128)(2,1)S(1)}, u32[]{:S(2)}, u32[]{:S(2)}) async-start(bf16[64,16,512]{2,1,0:T(8,128)(2,1)} %shard_map.210), calls=%async_computation.1 | async-start | bytes 2097152 | tf_op jit(solution)/shard_map/all_to_all | solution.py:431
  93.0 0.9 fusion
  93.9 1.3 copy.34
  95.2 0.2 copy.35
  95.4 1.1 maximum_bitcast_fusion.1.pqvt_h
  96.4 13.7 %all-to-all-done.1.x_h = bf16[64,16,512]{2,1,0:T(8,128)(2,1)S(1)} async-done(((bf16[64,16,512]{2,1,0:T(8,128)(2,1)}), bf16[64,16,512]{2,1,0:T(8,128)(2,1)S(1)}, u32[]{:S(2)}, u32[]{:S(2)}) %all-to-all-start.1) | async-done | bytes 1048608 | tf_op jit(solution)/shard_map/all_to_all | solution.py:431
  110.2 1.0 copy-done.4
  111.1 19.9 %shard_map.211 = bf16[64,16,512]{2,1,0:T(8,128)(2,1)} custom-call(bf16[64,16,512]{2,1,0:T(8,128)(2,1)} %copy-done.4, f32[1,512]{1,0:T(1,128)} %bitcast.27, f32[1,512]{1,0:T(1,128)} %bitcast.28, bf16[512,1536]{1,0:T(8,128)(2,1)} %p_h.3, bf16[1024,512]{1,0:T(8,128)(2,1)} %maximum_bitcast_fusion.1.pqvt_h, bf16[512,512]{1,0:T(8,128)(2,1)} %o_h.3, ...), custom_call_target="tpu_custom_call" | custom-call | tf_op jit(solution)/shard_map/pallas_call | solution.py:376
  131.0 21.0 %all_to_all.15 = bf16[64,16,512]{2,1,0:T(8,128)(2,1)S(1)} all-to-all(bf16[64,16,512]{2,1,0:T(8,128)(2,1)} %shard_map.211), channel_id=1, replica_groups=mesh['row'=8,'ch'=8,'core'=2] {'row','ch'}, dimensions={0} | all-to-all | bytes 2097152 | tf_op jit(solution)/shard_map/all_to_all | solution.py:431
  152.0 0.3 reshape.30
  152.3 1.8 %copy.29 = bf16[4,8,4,8,512]{4,3,2,1,0:T(8,128)(2,1)} copy(bf16[4,8,4,8,512]{4,2,0,1,3:T(4,128)(2,1)S(1)} %bitcast.24) | data formatting | bytes 2097152 | tf_op jit(solution)/shard_map/transpose | solution.py:443
  (30 shorter events, 0.5 us)
Async XLA Ops:
  0.8 6.6 %collective-permute-start = (bf16[32,512]{1,0:T(8,128)(2,1)S(1)}, bf16[32,512]{1,0:T(8,128)(2,1)S(1)}, u32[]{:S(2)}, u32[]{:S(2)}) collective-permute-start(bf16[32,512]{1,0:T(8,128)(2,1)S(1)} %get-tuple-element.22), channel_id=1, source_target_pairs={{0,16},{16,32},{32,48},{48,64},{64,80},{80,96},{96,112},{1,17},{17... | collective-permute-start | bytes 98312 | tf_op jit(solution)/shard_map/ppermute | solution.py:405
  4.8 4.7 %collective-permute-start.1 = (bf16[32,512]{1,0:T(8,128)(2,1)S(1)}, bf16[32,512]{1,0:T(8,128)(2,1)S(1)}, u32[]{:S(2)}, u32[]{:S(2)}) collective-permute-start(bf16[32,512]{1,0:T(8,128)(2,1)S(1)} %get-tuple-element.21), channel_id=1, source_target_pairs={{16,0},{32,16},{48,32},{64,48},{80,64},{96,80},{112,96},{17,1},{33... | collective-permute-start | bytes 98312 | tf_op jit(solution)/shard_map/ppermute | solution.py:405
  7.4 13.1 %copy-start.8 = (bf16[32,512]{1,0:T(8,128)(2,1)}, bf16[32,512]{1,0:T(8,128)(2,1)S(1)}, u32[]{:S(2)}) copy-start(bf16[32,512]{1,0:T(8,128)(2,1)S(1)} %collective-permute-done.above) | copy-start | bytes 98308
  9.5 11.1 %copy-start.9 = (bf16[32,512]{1,0:T(8,128)(2,1)}, bf16[32,512]{1,0:T(8,128)(2,1)S(1)}, u32[]{:S(2)}) copy-start(bf16[32,512]{1,0:T(8,128)(2,1)S(1)} %collective-permute-done.1.below) | copy-start | bytes 98308
  9.6 8.1 %collective-permute-start.2 = (bf16[48,512]{1,0:T(8,128)(2,1)S(1)}, bf16[48,512]{1,0:T(8,128)(2,1)S(1)}, u32[]{:S(2)}, u32[]{:S(2)}) collective-permute-start(bf16[48,512]{1,0:T(8,128)(2,1)S(1)} %get-tuple-element.28), channel_id=1, source_target_pairs={{0,1},{1,2},{2,3},{3,4},{4,5},{5,6},{6,7},{7,8},{8,9},{9,10},{10,1... | collective-permute-start | bytes 147464 | tf_op jit(solution)/shard_map/ppermute | solution.py:405
  15.1 5.4 %collective-permute-start.3 = (bf16[48,512]{1,0:T(8,128)(2,1)S(1)}, bf16[48,512]{1,0:T(8,128)(2,1)S(1)}, u32[]{:S(2)}, u32[]{:S(2)}) collective-permute-start(bf16[48,512]{1,0:T(8,128)(2,1)S(1)} %get-tuple-element.27), channel_id=1, source_target_pairs={{1,0},{2,1},{3,2},{4,3},{5,4},{6,5},{7,6},{8,7},{9,8},{10,9},{11,1... | collective-permute-start | bytes 147464 | tf_op jit(solution)/shard_map/ppermute | solution.py:405
  17.7 2.8 %copy-start.6 = (bf16[48,512]{1,0:T(8,128)(2,1)}, bf16[48,512]{1,0:T(8,128)(2,1)S(1)}, u32[]{:S(2)}) copy-start(bf16[48,512]{1,0:T(8,128)(2,1)S(1)} %collective-permute-done.2.left) | copy-start | bytes 147460
  20.5 0.6 copy-start.7
  21.1 28.5 %copy-start.2 = (bf16[512,1536]{1,0:T(8,128)(2,1)S(1)}, bf16[512,1536]{1,0:T(8,128)(2,1)}, u32[]{:S(2)}) copy-start(bf16[512,1536]{1,0:T(8,128)(2,1)} %p_h.2) | copy-start | bytes 4718596
  37.8 25.6 %all-to-all-start = ((bf16[128,16,128]{2,1,0:T(8,128)(2,1)}), bf16[128,16,128]{2,1,0:T(8,128)(2,1)S(1)}, u32[]{:S(2)}, u32[]{:S(2)}) async-start(bf16[128,16,128]{2,1,0:T(8,128)(2,1)} %get-tuple-element.10), calls=%async_computation | async-start | bytes 1048576 | tf_op jit(solution)/shard_map/all_to_all | solution.py:425
  49.7 0.7 copy-start.10
  49.7 0.7 copy-start.11
  51.7 0.8 copy-start
  52.5 0.8 copy-start.1
  63.4 0.8 copy-start.5
  87.9 5.1 %copy-start.3 = (bf16[512,1536]{1,0:T(8,128)(2,1)S(1)}, bf16[512,1536]{1,0:T(8,128)(2,1)}, u32[]{:S(2)}) copy-start(bf16[512,1536]{1,0:T(8,128)(2,1)} %p_h.3) | copy-start | bytes 4718596
  87.9 22.2 %all-to-all-start.1 = ((bf16[64,16,512]{2,1,0:T(8,128)(2,1)}), bf16[64,16,512]{2,1,0:T(8,128)(2,1)S(1)}, u32[]{:S(2)}, u32[]{:S(2)}) async-start(bf16[64,16,512]{2,1,0:T(8,128)(2,1)} %shard_map.210), calls=%async_computation.1 | async-start | bytes 2097152 | tf_op jit(solution)/shard_map/all_to_all | solution.py:431
  110.1 1.0 copy-start.4
